TPU v7x, 32 devices: a whole 2x2x4 slice. The times are simulated.
32 devices in a mesh: dp: 4 (over x, core), expert: 8 (over z, y).
Axes of the slice: x: 2, y: 2, z: 4, core: 2. Of those that a mesh axis runs over, the one named last changes fastest.
Arguments:
- tokens: bfloat16 [32768, 768], P(('dp', 'expert')), may hold values from -6 to 6
- segment_ids: int32 [32, 1024], P(('dp', 'expert')), may hold values from 0 to 3, never falling along the last dimension, each value on 1 to 512 neighbouring positions
- routes: int32 [32768, 1], P(('dp', 'expert')), may hold values from 0 to 7; in each aligned block of 1024 rows (0 to 1023, 1024 to 2047, ...) at most 256 rows name the same one
- norm1_gain: float32 [768], replicated, may hold values from 0.5 to 1.5
- norm1_bias: float32 [768], replicated, may hold values from -1 to 1
- query_weight: bfloat16 [768, 768], replicated, may hold values from -0.21875 to 0.21875
- w_key: bfloat16 [768, 768], replicated, may hold values from -0.21875 to 0.21875
- w_value: bfloat16 [768, 768], replicated, may hold values from -0.21875 to 0.21875
- w_output: bfloat16 [768, 768], replicated, may hold values from -1.75 to 1.75
- norm2_gain: float32 [768], replicated, may hold values from 0.5 to 1.5
- norm2_bias: float32 [768], replicated, may hold values from -1 to 1
- router_proj: float32 [768, 16], replicated, may hold values from -0.0546875 to 0.0546875
- expert_embed: float32 [8, 16], replicated, may hold values from -1.5 to 1.5
- expert_in: bfloat16 [8, 768, 3072], P('expert'), may hold values from -0.21875 to 0.21875
- expert_out: bfloat16 [8, 3072, 768], P('expert'), may hold values from -1.25 to 1.25
- cotangent: bfloat16 [32768, 768], P(('dp', 'expert')), may hold values from -6 to 6
Outputs:
- output: bfloat16 [32768, 768], P(('dp', 'expert'))
- grad_input: float32 [32768, 768], P(('dp', 'expert'))
- grad_norm1_gain: float32 [768], replicated
- grad_norm1_bias: float32 [768], replicated
- grad_w_query: float32 [768, 768], replicated
- grad_w_key: float32 [768, 768], replicated
- grad_w_value: float32 [768, 768], replicated
- grad_w_output: float32 [768, 768], replicated
- grad_norm2_gain: float32 [768], replicated
- grad_norm2_bias: float32 [768], replicated
- grad_router_proj: float32 [768, 16], replicated
- grad_expert_embed: float32 [8, 16], replicated
- grad_expert_in: float32 [8, 768, 3072], P('expert', None, 'dp')
- grad_expert_out: float32 [8, 3072, 768], P('expert', 'dp')
Inputs may be any that keep to these rules, and one draw needn't show every extreme that they name: `routes`: among the 1024 tokens of one device no expert is named more than 256 times, and in every draw some expert is named exactly 256 times by one device's tokens. `segment_ids`: within each sequence the ids never fall; each document has 1 to 512 tokens, and one has exactly 512.
All inputs are finite; a program needn't handle non-finite values.
Results may differ from a plain program's by a relative error of at most 0.02.
The roundings to bfloat16 on the way count: a program that leaves them out, or rounds other values in their place, can miss the bound.
Values may be sent and summed in bfloat16 or wider, within the bound.
A program may use at most 256 MiB of HBM per device.

v0:
```python
import jax
import jax.numpy as jnp
from jax import lax
from jax.sharding import PartitionSpec as P

HEAD_DIM = 64


normalizer_sharpness = 0.25
exact_arithmetic_mode = lax.Precision.HIGHEST


def layer_norm(values, gain, shift):
    average = jnp.mean(values, -1, keepdims=True)
    centred = values - average
    spread = jnp.mean(centred * centred, -1, keepdims=True)
    return centred * lax.rsqrt(spread + 1e-05) * gain + shift


def router_gate(normed, router_proj, expert_embed, chosen):
    narrowed_feature_count = jnp.dot(normed, router_proj, precision=exact_arithmetic_mode)
    narrowed_feature_count = narrowed_feature_count * lax.rsqrt(
        jnp.maximum(
            jnp.sum(narrowed_feature_count * narrowed_feature_count, -1, keepdims=True), 1.0
        )
    )
    index_mapping_array = expert_embed * lax.rsqrt(
        jnp.maximum(jnp.sum(expert_embed * expert_embed, -1, keepdims=True), 1.0)
    )
    gating_raw_scores = (
        jnp.dot(narrowed_feature_count, index_mapping_array.T, precision=exact_arithmetic_mode)
        / normalizer_sharpness
    )
    router_probs = jax.nn.softmax(gating_raw_scores, axis=-1)
    return jnp.sum(router_probs * chosen, -1)


def gelu_slope(pre):
    return (
        0.5 * (1.0 + lax.erf(pre * 0.7071067811865476))
        + pre * jnp.exp(-0.5 * pre * pre) * 0.3989422804014327
    )


def contract_rows(left, right):
    return lax.dot_general(
        left, right, (((0,), (0,)), ((), ())), preferred_element_type=jnp.float32
    )


def contract_cols(left, right):
    return lax.dot_general(
        left, right, (((1,), (1,)), ((), ())), preferred_element_type=jnp.float32
    )


def on_device(
    tokens,
    segment_ids,
    routes,
    norm1_gain,
    norm1_bias,
    query_weight,
    w_key,
    w_value,
    w_output,
    norm2_gain,
    norm2_bias,
    router_proj,
    expert_embed,
    expert_in,
    expert_out,
    cotangent,
):
    tok_count, width = tokens.shape
    seq_len = segment_ids.shape[1]
    heads = width // HEAD_DIM
    experts = lax.axis_size("expert")
    capacity = 2 * tok_count // experts
    query_rows = min(512, seq_len)
    blocks = tok_count // query_rows
    per_sequence = seq_len // query_rows
    score_scale = HEAD_DIM ** (-0.5)
    document_labels_flattened = segment_ids.reshape(-1)
    route = routes[:, 0]
    expert_ids = jnp.arange(experts, dtype=jnp.int32)
    hits = (route[:, None] == expert_ids[None, :]).astype(jnp.int32)
    slot_rank = jnp.sum((jnp.cumsum(hits, 0) - hits) * hits, 1)
    chosen = hits.astype(jnp.float32)
    slot_token = (
        jnp.full((experts, capacity), -1, jnp.int32)
        .at[route, slot_rank]
        .set(jnp.arange(tok_count, dtype=jnp.int32))
    )
    filled = slot_token >= 0
    safe_ids = jnp.maximum(slot_token, 0)
    zero_low = jnp.zeros((), jnp.bfloat16)
    xf = tokens.astype(jnp.float32)
    normed1, norm1_pull = jax.vjp(layer_norm, xf, norm1_gain, norm1_bias)
    normed1_low = normed1.astype(jnp.bfloat16)
    query_heads = (
        jnp.dot(normed1_low, query_weight, preferred_element_type=jnp.float32)
        .astype(jnp.bfloat16)
        .reshape(tok_count, heads, HEAD_DIM)
    )
    key_heads = (
        jnp.dot(normed1_low, w_key, preferred_element_type=jnp.float32)
        .astype(jnp.bfloat16)
        .reshape(tok_count, heads, HEAD_DIM)
    )
    value_heads = (
        jnp.dot(normed1_low, w_value, preferred_element_type=jnp.float32)
        .astype(jnp.bfloat16)
        .reshape(tok_count, heads, HEAD_DIM)
    )

    def block_scores(block_index):
        seq_start = block_index // per_sequence * seq_len
        query_block = lax.dynamic_slice_in_dim(query_heads, block_index * query_rows, query_rows, 0)
        seg_query = lax.dynamic_slice_in_dim(
            document_labels_flattened, block_index * query_rows, query_rows, 0
        )
        scores = (
            jnp.einsum("qhd,khd->hqk", query_block, key_heads, preferred_element_type=jnp.float32)
            * score_scale
        )
        same_doc = seg_query[:, None] == document_labels_flattened[None, :]
        scores = jnp.where(same_doc[None], scores, -1e30)
        return (scores, query_block, key_heads, value_heads, seq_start)

    def forward_block(block_index):
        scores, query_block, key_tile, value_block, seq_start = block_scores(block_index)
        largest = jnp.max(scores, -1, keepdims=True)
        weights = jnp.exp(scores - largest)
        total = jnp.sum(weights, -1, keepdims=True)
        probs_low = (weights / total).astype(jnp.bfloat16)
        attended = jnp.einsum(
            "hqk,khd->qhd", probs_low, value_block, preferred_element_type=jnp.float32
        )
        return (attended.astype(jnp.bfloat16), (largest + jnp.log(total))[:, :, 0])

    attended_all, log_totals = lax.map(forward_block, jnp.arange(blocks, dtype=jnp.int32))
    mixed = attended_all.reshape(tok_count, width)
    hidden = xf + jnp.dot(mixed, w_output, preferred_element_type=jnp.float32)

    def second_branch(hidden_in, gain, shift, proj, embed):
        normed = layer_norm(hidden_in, gain, shift)
        return (normed, router_gate(normed, proj, embed, chosen))

    (normed2, gate), branch_pull = jax.vjp(
        second_branch, hidden, norm2_gain, norm2_bias, router_proj, expert_embed
    )
    normed2_low = normed2.astype(jnp.bfloat16)
    dispatched = jnp.where(filled[:, :, None], normed2_low[safe_ids], zero_low)
    incoming = lax.all_to_all(dispatched, "expert", split_axis=0, concat_axis=0, tiled=True)
    sources = incoming.shape[0]
    count = incoming.shape[1]
    flat_rows = incoming.reshape(sources * count, width)
    pre = jnp.dot(flat_rows, expert_in[0], preferred_element_type=jnp.float32)
    active_mask = jax.nn.gelu(pre, approximate=False).astype(jnp.bfloat16)
    produced_rows = jnp.dot(active_mask, expert_out[0], preferred_element_type=jnp.float32).astype(
        jnp.bfloat16
    )
    produced = produced_rows.reshape(sources, count, width)
    pre_kept = pre.reshape(sources, count, pre.shape[-1])
    returned = lax.all_to_all(produced, "expert", split_axis=0, concat_axis=0, tiled=True)
    expert_result = returned[route, slot_rank].astype(jnp.float32)
    result = (hidden + gate[:, None] * expert_result).astype(jnp.bfloat16)
    upstream = cotangent.astype(jnp.float32)
    gate_grad = jnp.sum(upstream * expert_result, 1)
    scaled = (gate[:, None] * upstream).astype(jnp.bfloat16)
    scaled_slots = jnp.where(filled[:, :, None], scaled[safe_ids], zero_low)
    arriving = lax.all_to_all(scaled_slots, "expert", split_axis=0, concat_axis=0, tiled=True)
    grad_rows = arriving.reshape(-1, width)
    pre_rows = pre_kept.reshape(-1, pre_kept.shape[-1])
    active_rows = jax.nn.gelu(pre_rows, approximate=False).astype(jnp.bfloat16)
    grad_out_weight = contract_rows(active_rows, grad_rows)
    grad_active = contract_cols(grad_rows, expert_out[0])
    grad_pre = (grad_active * gelu_slope(pre_rows)).astype(jnp.bfloat16)
    grad_in_weight = contract_rows(incoming.reshape(-1, width), grad_pre)
    grad_normed_rows = contract_cols(grad_pre, expert_in[0]).astype(jnp.bfloat16)
    leaving = lax.all_to_all(
        grad_normed_rows.reshape(experts, capacity, width),
        "expert",
        split_axis=0,
        concat_axis=0,
        tiled=True,
    )
    grad_normed2 = leaving[route, slot_rank].astype(jnp.float32)
    grad_expert_in, grad_expert_out = (
        lax.psum_scatter(
            grad_in_weight[None].astype(jnp.bfloat16), "dp", scatter_dimension=2, tiled=True
        ).astype(jnp.float32),
        lax.psum_scatter(
            grad_out_weight[None].astype(jnp.bfloat16), "dp", scatter_dimension=1, tiled=True
        ).astype(jnp.float32),
    )
    hidden_term, grad_gain2, grad_shift2, grad_proj, grad_embed = branch_pull(
        (grad_normed2, gate_grad)
    )
    grad_hidden = upstream + hidden_term
    grad_hidden_low = grad_hidden.astype(jnp.bfloat16)
    grad_wout = contract_rows(mixed, grad_hidden_low)
    grad_mixed = (
        contract_cols(grad_hidden_low, w_output)
        .astype(jnp.bfloat16)
        .reshape(tok_count, heads, HEAD_DIM)
    )

    def backward_block(running, block_index):
        grad_keys_acc, grad_values_acc = running
        scores, query_block, key_tile, value_block, seq_start = block_scores(block_index)
        probs = jnp.exp(scores - log_totals[block_index][:, :, None])
        grad_block = lax.dynamic_slice_in_dim(grad_mixed, block_index * query_rows, query_rows, 0)
        grad_probs = jnp.einsum(
            "qhd,khd->hqk", grad_block, value_block, preferred_element_type=jnp.float32
        )
        grad_scores = (
            probs * (grad_probs - jnp.sum(probs * grad_probs, -1, keepdims=True))
        ).astype(jnp.bfloat16)
        grad_query_block = (
            jnp.einsum("hqk,khd->qhd", grad_scores, key_tile, preferred_element_type=jnp.float32)
            * score_scale
        )
        grad_key_block = (
            jnp.einsum("hqk,qhd->khd", grad_scores, query_block, preferred_element_type=jnp.float32)
            * score_scale
        )
        grad_value_block = jnp.einsum(
            "hqk,qhd->khd",
            probs.astype(jnp.bfloat16),
            grad_block,
            preferred_element_type=jnp.float32,
        )
        grad_keys_acc = grad_keys_acc + grad_key_block
        grad_values_acc = grad_values_acc + grad_value_block
        return ((grad_keys_acc, grad_values_acc), grad_query_block)

    empty_heads = jnp.zeros((tok_count, heads, HEAD_DIM), jnp.float32)
    (grad_keys_all, grad_values_all), grad_queries_all = lax.scan(
        backward_block, (empty_heads, empty_heads), jnp.arange(blocks, dtype=jnp.int32)
    )
    grad_queries_low = grad_queries_all.reshape(tok_count, width).astype(jnp.bfloat16)
    cotangent_lookups_narrow = grad_keys_all.reshape(tok_count, width).astype(jnp.bfloat16)
    grad_values_low = grad_values_all.reshape(tok_count, width).astype(jnp.bfloat16)
    grad_wq = contract_rows(normed1_low, grad_queries_low)
    grad_wk = contract_rows(normed1_low, cotangent_lookups_narrow)
    grad_wv = contract_rows(normed1_low, grad_values_low)
    grad_normed1 = (
        contract_cols(grad_queries_low, query_weight)
        + contract_cols(cotangent_lookups_narrow, w_key)
        + contract_cols(grad_values_low, w_value)
    )
    input_term, grad_gain1, grad_shift1 = norm1_pull(grad_normed1)
    grad_input = grad_hidden + input_term
    dense_terms = (
        grad_gain1,
        grad_shift1,
        grad_wq,
        grad_wk,
        grad_wv,
        grad_wout,
        grad_gain2,
        grad_shift2,
        grad_proj,
        grad_embed,
    )
    summed = lax.psum(
        (
            dense_terms[0],
            dense_terms[1],
            dense_terms[2],
            dense_terms[3],
            dense_terms[4],
            dense_terms[5],
            dense_terms[6],
            dense_terms[7],
            dense_terms[8],
            dense_terms[9],
        ),
        ("dp", "expert"),
    )
    return (
        result,
        grad_input,
        summed[0],
        summed[1],
        summed[2],
        summed[3],
        summed[4],
        summed[5],
        summed[6],
        summed[7],
        summed[8],
        summed[9],
        grad_expert_in,
        grad_expert_out,
    )


def solution(mesh):
    in_specs = (
        P(("dp", "expert"), None),
        P(("dp", "expert"), None),
        P(("dp", "expert"), None),
        P(),
        P(),
        P(),
        P(),
        P(),
        P(),
        P(),
        P(),
        P(),
        P(),
        P("expert", None, None),
        P("expert", None, None),
        P(("dp", "expert"), None),
    )
    out_specs = (
        P(("dp", "expert"), None),
        P(("dp", "expert"), None),
        P(),
        P(),
        P(),
        P(),
        P(),
        P(),
        P(),
        P(),
        P(),
        P(),
        P("expert", None, "dp"),
        P("expert", "dp", None),
    )
    return jax.shard_map(
        on_device, mesh=mesh, in_specs=in_specs, out_specs=out_specs, check_vma=False
    )
```

profile of v0, /device:TPU:0, one launch (start us, length us, event | category | flops | bytes accessed | tf_op | source)
XLA Modules:
  0.0 1028.9 jit_solution(7914575914639304814)
XLA Ops:
  15.1 4.3 scatter_custom_fusion
  26.3 3.2 convolution_convert_fusion.4
  32.3 75.8 %while.27 = (s32[]{:T(128)}, bf16[2,512,12,64]{1,3,2,0:T(8,128)(2,1)}, f32[2,12,512]{2,1,0:T(8,128)S(1)}, s32[2]{0:T(128)S(1)}, s32[1024]{0:T(1024)S(1)}, /*inde...) while((s32[]{:T(128)}, ...), condition=%wide.region_5.6_spmd, body=%wide.region_2.0_spmd.sunk | while | flops 1687021568 | bytes 189499632 | solution.py:142
  34.0 12.1 %fusion.187 = (f32[12,512]{1,0:T(8,128)S(1)}, f32[12,512,1024]{2,1,0:T(8,128)}) fusion(pred[512,1024]{1,0:T(8,128)(4,1)S(1)} %broadcast_compare_fusion.5, bf16[1024,12,64]{0,2,1:T(8,128)(2,1)S(1)} %get-tuple-element.452, bf16[1024,12,64]{0,2,1:T(8,128)(2,1)} %get-tuple-element.451, s32[]{:T(128)S(6)} %select_n.135), kind=kOutput, calls=%fused_computation.8.clone.1 | convolution fusion | flops 824174592 | bytes 28073988 | tf_op jit(solution)/shard_map/while/body/eval_jaxpr/qhd,khd->hqk/dot_general | solution.py:124
  46.2 12.3 %fusion.188 = f32[12,512]{1,0:T(8,128)S(1)} fusion(f32[12,512,1024]{2,1,0:T(8,128)} %get-tuple-element.403, f32[12,512]{1,0:T(8,128)S(1)} %get-tuple-element.404, pred[512,1024]{1,0:T(8,128)(4,1)S(1)} %broadcast_compare_fusion.5), kind=kLoop, calls=%fused_computation.9.clone.1 | loop fusion | flops 25159680 | bytes 25739264 | tf_op jit(solution)/shard_map/while/body/eval_jaxpr/reduce_sum | solution.py:135
  61.6 8.5 fusion.189
  71.8 12.1 %fusion.187 = (f32[12,512]{1,0:T(8,128)S(1)}, f32[12,512,1024]{2,1,0:T(8,128)}) fusion(pred[512,1024]{1,0:T(8,128)(4,1)S(1)} %broadcast_compare_fusion.5, bf16[1024,12,64]{0,2,1:T(8,128)(2,1)S(1)} %get-tuple-element.452, bf16[1024,12,64]{0,2,1:T(8,128)(2,1)} %get-tuple-element.451, s32[]{:T(128)S(6)} %select_n.135), kind=kOutput, calls=%fused_computation.8.clone.1 | convolution fusion | flops 824174592 | bytes 28073988 | tf_op jit(solution)/shard_map/while/body/eval_jaxpr/qhd,khd->hqk/dot_general | solution.py:124
  83.9 12.3 %fusion.188 = f32[12,512]{1,0:T(8,128)S(1)} fusion(f32[12,512,1024]{2,1,0:T(8,128)} %get-tuple-element.403, f32[12,512]{1,0:T(8,128)S(1)} %get-tuple-element.404, pred[512,1024]{1,0:T(8,128)(4,1)S(1)} %broadcast_compare_fusion.5), kind=kLoop, calls=%fused_computation.9.clone.1 | loop fusion | flops 25159680 | bytes 25739264 | tf_op jit(solution)/shard_map/while/body/eval_jaxpr/reduce_sum | solution.py:135
  99.3 8.5 fusion.189
  108.2 3.6 copy.43
  119.6 9.4 gather_fusion
  131.1 77.8 %all_to_all.20 = bf16[8,256,768]{2,1,0:T(8,128)(2,1)S(1)} all-to-all(bf16[8,256,768]{2,1,0:T(8,128)(2,1)S(1)} %broadcast_select_fusion.1), channel_id=1, replica_groups=mesh['dp'=4,'expert'=8] {'expert'}, dimensions={0} | all-to-all | bytes 6291456 | tf_op jit(solution)/shard_map/all_to_all | solution.py:155
  208.9 63.0 %fusion.31 = (bf16[2048,3072]{1,0:T(8,128)(2,1)S(1)}, f32[2048,3072]{1,0:T(8,128)}) fusion(bf16[2048,768]{1,0:T(8,128)(2,1)S(1)} %bitcast.162, bf16[1,768,3072]{2,1,0:T(8,128)(2,1)} %param.33), kind=kOutput, calls=%fused_computation.48 | convolution fusion | flops 10072621056 | bytes 45613056 | tf_op jit(solution)/shard_map/dot_general | solution.py:159
  271.9 11.3 %fusion.63 = bf16[2048,768]{1,0:T(8,128)(2,1)} fusion(bf16[2048,3072]{1,0:T(8,128)(2,1)S(1)} %get-tuple-element.275, bf16[1,3072,768]{2,1,0:T(8,128)(2,1)S(1)} %copy-done.95), kind=kOutput, calls=%fused_computation.97 | convolution fusion | flops 9665249280 | bytes 20447232 | tf_op jit(solution)/shard_map/dot_general | solution.py:161
  283.1 4.4 all-to-all-start.1
  289.6 4.4 multiply_reduce_fusion.5
  294.5 63.0 %all-to-all-done.1 = bf16[8,256,768]{2,1,0:T(8,128)(2,1)} async-done(((bf16[8,256,768]{2,1,0:T(8,128)(2,1)}), bf16[8,256,768]{2,1,0:T(8,128)(2,1)}, u32[]{:S(2)}, u32[]{:S(2)}) %all-to-all-start.1) | async-done | bytes 3145760 | tf_op jit(solution)/shard_map/all_to_all | solution.py:166
  357.4 19.7 %gather_fusion.1 = bf16[1024,768]{1,0:T(8,128)(2,1)} fusion(bf16[8,256,768]{2,1,0:T(8,128)(2,1)} %all-to-all-done.1, s32[1024]{0:T(1024)S(1)} %bitcast.151), kind=kCustom, calls=%fused_computation.1 | custom fusion | bytes 3153920 | tf_op jit(solution)/shard_map/gather | solution.py:167
  385.2 9.4 gather_fusion.2
  396.7 74.5 %all_to_all.21 = bf16[8,256,768]{2,1,0:T(8,128)(2,1)S(1)} all-to-all(bf16[8,256,768]{2,1,0:T(8,128)(2,1)S(1)} %broadcast_select_fusion), channel_id=1, replica_groups=mesh['dp'=4,'expert'=8] {'expert'}, dimensions={0} | all-to-all | bytes 6291456 | tf_op jit(solution)/shard_map/all_to_all | solution.py:173
  472.8 14.5 %fusion.57 = bf16[1,3072,768]{2,1,0:T(8,128)(2,1)} fusion(bf16[2048,3072]{1,0:T(8,128)(2,1)} %copy-done.104, bf16[2048,768]{1,0:T(8,128)(2,1)S(1)} %bitcast.166), kind=kOutput, calls=%fused_computation.92 | convolution fusion | flops 9666035712 | bytes 20447232 | tf_op jit(solution)/shard_map/dot_general | solution.py:46
  487.4 22.4 %fusion.37 = bf16[2048,3072]{1,0:T(8,128)(2,1)S(1)} fusion(f32[2048,3072]{1,0:T(8,128)} %get-tuple-element.276, bf16[2048,768]{1,0:T(8,128)(2,1)} %bitcast.167, bf16[1,3072,768]{2,1,0:T(8,128)(2,1)} %param.34), kind=kOutput, calls=%fused_computation.54 | convolution fusion | flops 9726590976 | bytes 45613056 | tf_op jit(solution)/shard_map/dot_general | solution.py:52
  509.9 11.4 %fusion.60 = bf16[2048,768]{1,0:T(8,128)(2,1)} fusion(bf16[2048,3072]{1,0:T(8,128)(2,1)S(1)} %fusion.37, bf16[1,768,3072]{2,1,0:T(8,128)(2,1)S(1)} %bitcast.190), kind=kOutput, calls=%fused_computation.96 | convolution fusion | flops 9665249280 | bytes 20447232 | tf_op jit(solution)/shard_map/dot_general | solution.py:52
  521.3 4.4 all-to-all-start.3
  526.9 15.6 %fusion.56 = bf16[1,768,3072]{2,1,0:T(8,128)(2,1)} fusion(bf16[2048,768]{1,0:T(8,128)(2,1)} %bitcast.163, bf16[2048,3072]{1,0:T(8,128)(2,1)} %copy-done.103), kind=kOutput, calls=%fused_computation.91 | convolution fusion | flops 9666035712 | bytes 20447232 | tf_op jit(solution)/shard_map/dot_general | solution.py:46
  542.5 52.8 %all-to-all-done.3 = bf16[8,256,768]{2,1,0:T(8,128)(2,1)} async-done(((bf16[8,256,768]{2,1,0:T(8,128)(2,1)}), bf16[8,256,768]{2,1,0:T(8,128)(2,1)}, u32[]{:S(2)}, u32[]{:S(2)}) %all-to-all-start.3) | async-done | bytes 3145760 | tf_op jit(solution)/shard_map/all_to_all | solution.py:182
  595.3 14.6 %gather_fusion.3 = bf16[1024,768]{1,0:T(8,128)(2,1)S(1)} fusion(bf16[8,256,768]{2,1,0:T(8,128)(2,1)} %all-to-all-done.3, s32[1024]{0:T(1024)S(1)} %bitcast.152), kind=kCustom, calls=%fused_computation.3 | custom fusion | bytes 3153920 | tf_op jit(solution)/shard_map/gather | solution.py:189
  611.6 6.5 multiply_reduce_fusion.1
  625.1 174.3 %while.28 = (s32[]{:T(128)}, f32[1024,12,64]{0,2,1:T(8,128)}, f32[1024,12,64]{0,2,1:T(8,128)}, bf16[2,512,12,64]{1,3,2,0:T(8,128)(2,1)}, s32[2]{0:T(128)S(1)}, /...) while((s32[]{:T(128)}, f32[1024,12,64]{0,2,1:T(8,128)}, ...), condition=%wide.region_24.25_spmd.clone, body=%wide.region_22.24_spmd.clone.sunk | while | flops 4125747200 | bytes 219343152 | solution.py:240
  628.9 11.5 %fusion.199 = f32[12,512,1024]{2,1,0:T(8,128)} fusion(bf16[1024,12,64]{0,2,1:T(8,128)(2,1)S(1)} %get-tuple-element.500, bf16[1024,12,64]{0,2,1:T(8,128)(2,1)} %get-tuple-element.497, s32[]{:T(128)S(6)} %select_n.139), kind=kOutput, calls=%fused_computation.35.clone.1 | convolution fusion | flops 805306368 | bytes 27525124 | tf_op jit(solution)/shard_map/while/body/eval_jaxpr/qhd,khd->hqk/dot_general | solution.py:124
  640.4 13.4 %bitcast_add_fusion.5 = f32[1024,12,64]{0,2,1:T(8,128)} fusion(f32[1024,12,64]{0,2,1:T(8,128)} %get-tuple-element.477, f32[12,512,1024]{2,1,0:T(8,128)} %fusion.199, f32[12,512]{1,0:T(8,128)S(1)} %dynamic-slice_bitcast_fusion.2, pred[512,1024]{1,0:T(8,128)(4,1)S(1)} %broadcast_compare_fusion.6, pred[]{:T(512)S(6)} %compare.7, ...), kind=kOutput, calls=%fused_computation.27.clone.1 | convolution fusion | flops 832045056 | bytes 32800772 | tf_op jit(solution)/shard_map/while/body/eval_jaxpr/hqk,qhd->khd/dot_general | solution.py:229
  653.8 18.1 %multiply_reduce_fusion.10 = (f32[12,512]{1,0:T(8,128)S(1)}, f32[12,512,1024]{2,1,0:T(8,128)}) fusion(f32[12,512,1024]{2,1,0:T(8,128)} %fusion.199, f32[12,512]{1,0:T(8,128)S(1)} %dynamic-slice_bitcast_fusion.2, pred[512,1024]{1,0:T(8,128)(4,1)S(1)} %broadcast_compare_fusion.6, bf16[1024,12,64]{0,2,1:T(8,128)(2,1)} %get-tuple-element.503, ...), kind=kOutput, calls=%fused_computation.22.clone.1 | convolution fusion | flops 836757504 | bytes 53264388 | tf_op jit(solution)/shard_map/while/body/eval_jaxpr/qhd,khd->hqk/dot_general | solution.py:215
  672.0 21.2 %multiply_convert_fusion.2 = bf16[12,512,1024]{2,1,0:T(8,128)(2,1)} fusion(f32[12,512,1024]{2,1,0:T(8,128)} %get-tuple-element.417, f32[12,512,1024]{2,1,0:T(8,128)} %fusion.199, f32[12,512]{1,0:T(8,128)S(1)} %get-tuple-element.418, f32[12,512]{1,0:T(8,128)S(1)} %dynamic-slice_bitcast_fusion.2, pred[512,1024]{1,0:T(8,128)(4,1)S(1)} %broadcast_compare_fusion.6), kind=kLoop, calls=%fused_computation.21.clone.1 | loop fusion | flops 37748736 | bytes 63488000 | tf_op jit(solution)/shard_map/while/body/eval_jaxpr/convert_element_type | solution.py:220
  693.2 9.4 bitcast_dynamic-update-slice_fusion.5
  702.5 8.8 bitcast_add_fusion.4
  715.0 11.5 %fusion.199 = f32[12,512,1024]{2,1,0:T(8,128)} fusion(bf16[1024,12,64]{0,2,1:T(8,128)(2,1)S(1)} %get-tuple-element.500, bf16[1024,12,64]{0,2,1:T(8,128)(2,1)} %get-tuple-element.497, s32[]{:T(128)S(6)} %select_n.139), kind=kOutput, calls=%fused_computation.35.clone.1 | convolution fusion | flops 805306368 | bytes 27525124 | tf_op jit(solution)/shard_map/while/body/eval_jaxpr/qhd,khd->hqk/dot_general | solution.py:124
  726.4 14.4 %bitcast_add_fusion.5 = f32[1024,12,64]{0,2,1:T(8,128)} fusion(f32[1024,12,64]{0,2,1:T(8,128)} %get-tuple-element.477, f32[12,512,1024]{2,1,0:T(8,128)} %fusion.199, f32[12,512]{1,0:T(8,128)S(1)} %dynamic-slice_bitcast_fusion.2, pred[512,1024]{1,0:T(8,128)(4,1)S(1)} %broadcast_compare_fusion.6, pred[]{:T(512)S(6)} %compare.7, ...), kind=kOutput, calls=%fused_computation.27.clone.1 | convolution fusion | flops 832045056 | bytes 32800772 | tf_op jit(solution)/shard_map/while/body/eval_jaxpr/hqk,qhd->khd/dot_general | solution.py:229
  740.8 18.1 %multiply_reduce_fusion.10 = (f32[12,512]{1,0:T(8,128)S(1)}, f32[12,512,1024]{2,1,0:T(8,128)}) fusion(f32[12,512,1024]{2,1,0:T(8,128)} %fusion.199, f32[12,512]{1,0:T(8,128)S(1)} %dynamic-slice_bitcast_fusion.2, pred[512,1024]{1,0:T(8,128)(4,1)S(1)} %broadcast_compare_fusion.6, bf16[1024,12,64]{0,2,1:T(8,128)(2,1)} %get-tuple-element.503, ...), kind=kOutput, calls=%fused_computation.22.clone.1 | convolution fusion | flops 836757504 | bytes 53264388 | tf_op jit(solution)/shard_map/while/body/eval_jaxpr/qhd,khd->hqk/dot_general | solution.py:215
  758.9 21.2 %multiply_convert_fusion.2 = bf16[12,512,1024]{2,1,0:T(8,128)(2,1)} fusion(f32[12,512,1024]{2,1,0:T(8,128)} %get-tuple-element.417, f32[12,512,1024]{2,1,0:T(8,128)} %fusion.199, f32[12,512]{1,0:T(8,128)S(1)} %get-tuple-element.418, f32[12,512]{1,0:T(8,128)S(1)} %dynamic-slice_bitcast_fusion.2, pred[512,1024]{1,0:T(8,128)(4,1)S(1)} %broadcast_compare_fusion.6), kind=kLoop, calls=%fused_computation.21.clone.1 | loop fusion | flops 37748736 | bytes 63488000 | tf_op jit(solution)/shard_map/while/body/eval_jaxpr/convert_element_type | solution.py:220
  780.1 9.4 bitcast_dynamic-update-slice_fusion.5
  789.5 9.7 bitcast_add_fusion.4
  799.4 3.2 copy.50
  820.3 5.0 fusion.76
  828.2 3.3 fusion.134
  840.6 3.6 copy.55
  844.1 41.1 %all-reduce = (f32[768]{0:T(1024)}, f32[768]{0:T(1024)}, f32[768]{0:T(1024)}, f32[768]{0:T(1024)}, f32[768,16]{0,1:T(8,128)}, /*index=5*/f32[8,16]{1,0:T(8,128)}) all-reduce(f32[768]{0:T(1024)S(1)} %get-tuple-element.200, f32[768]{0:T(1024)S(1)} %get-tuple-element.203, ...), channel_id=1, replica_groups=mesh['dp'=4,'expert'=8] {'dp','expert'}, use_global_device_ids=true, to_apply=%region_28.29 | all-reduce | flops 15488 | bytes 123904 | tf_op jit(solution)/shard_map/psum | solution.py:268
  891.0 120.3 %all-reduce.4.cloned.1.call-done = (f32[768,768]{1,0:T(8,128)}, f32[768,768]{1,0:T(8,128)}, f32[768,768]{1,0:T(8,128)}, f32[768,768]{1,0:T(8,128)}) async-done(((f32[768,768]{1,0:T(8,128)}, f32[768,768]{1,0:T(8,128)}, f32[768,768]{1,0:T(8,128)}, f32[768,768]{1,0:T(8,128)}), (f32[768,768]{1,0:T(8,128)}, f32[768,768]{1,0:T(8,128)}, f32[768,768]{1,0:T(8,128)}, ...) | async-done | bytes 9437200 | tf_op jit(solution)/shard_map/psum | solution.py:268
  1011.2 3.4 copy.92
  (325 shorter events, 101.9 us)
Async XLA Ops:
  8.0 15.5 %copy-start = (bf16[768,768]{1,0:T(8,128)(2,1)S(1)}, bf16[768,768]{1,0:T(8,128)(2,1)}, u32[]{:S(2)}) copy-start(bf16[768,768]{1,0:T(8,128)(2,1)} %param.27) | copy-start | bytes 3538948
  22.7 6.8 copy-start.54
  23.5 6.0 copy-start.69
  34.0 24.4 %copy-start.12 = (bf16[1024,12,64]{0,2,1:T(8,128)(2,1)S(1)}, bf16[1024,12,64]{0,2,1:T(8,128)(2,1)}, u32[]{:S(2)}) copy-start(bf16[1024,12,64]{0,2,1:T(8,128)(2,1)} %get-tuple-element.453) | copy-start | bytes 4718596 | tf_op jit(solution)/shard_map/while
  46.2 15.4 %copy-start.1 = (f32[12,512,1024]{2,1,0:T(8,128)S(1)}, f32[12,512,1024]{2,1,0:T(8,128)}, u32[]{:S(2)}) copy-start(f32[12,512,1024]{2,1,0:T(8,128)} %get-tuple-element.403) | copy-start | bytes 75497472 | tf_op jit(solution)/shard_map/while
  71.8 24.4 %copy-start.12 = (bf16[1024,12,64]{0,2,1:T(8,128)(2,1)S(1)}, bf16[1024,12,64]{0,2,1:T(8,128)(2,1)}, u32[]{:S(2)}) copy-start(bf16[1024,12,64]{0,2,1:T(8,128)(2,1)} %get-tuple-element.453) | copy-start | bytes 4718596 | tf_op jit(solution)/shard_map/while
  83.9 15.4 %copy-start.1 = (f32[12,512,1024]{2,1,0:T(8,128)S(1)}, f32[12,512,1024]{2,1,0:T(8,128)}, u32[]{:S(2)}) copy-start(f32[12,512,1024]{2,1,0:T(8,128)} %get-tuple-element.403) | copy-start | bytes 75497472 | tf_op jit(solution)/shard_map/while
  108.2 4.1 copy-start.2
  108.2 4.1 copy-start.38
  108.2 4.1 copy-start.10
  108.2 4.1 copy-start.96
  119.5 9.4 copy-start.83
  208.9 63.0 %copy-start.22 = (bf16[8,256,768]{2,1,0:T(8,128)(2,1)}, bf16[8,256,768]{2,1,0:T(8,128)(2,1)S(1)}, u32[]{:S(2)}) copy-start(bf16[8,256,768]{2,1,0:T(8,128)(2,1)S(1)} %all_to_all.20) | copy-start | bytes 9437188
  208.9 63.0 %copy-start.95 = (bf16[1,3072,768]{2,1,0:T(8,128)(2,1)S(1)}, bf16[1,3072,768]{2,1,0:T(8,128)(2,1)}, u32[]{:S(2)}) copy-start(bf16[1,3072,768]{2,1,0:T(8,128)(2,1)} %param.34) | copy-start | bytes 14155780
  271.8 11.3 %copy-start.104 = (bf16[2048,3072]{1,0:T(8,128)(2,1)}, bf16[2048,3072]{1,0:T(8,128)(2,1)S(1)}, u32[]{:S(2)}) copy-start(bf16[2048,3072]{1,0:T(8,128)(2,1)S(1)} %get-tuple-element.275) | copy-start | bytes 37748740
  283.1 74.3 %all-to-all-start.1 = ((bf16[8,256,768]{2,1,0:T(8,128)(2,1)}), bf16[8,256,768]{2,1,0:T(8,128)(2,1)}, u32[]{:S(2)}, u32[]{:S(2)}) async-start(bf16[8,256,768]{2,1,0:T(8,128)(2,1)} %bitcast.165), calls=%async_computation.1 | async-start | bytes 6291456 | tf_op jit(solution)/shard_map/all_to_all | solution.py:166
  287.7 69.8 %copy-start.4 = (s32[1024,1]{0,1:T(1,128)S(1)}, s32[1024,1]{0,1:T(1,128)}, u32[]{:S(2)}) copy-start(s32[1024,1]{0,1:T(1,128)} %get-tuple-element.266) | copy-start | bytes 12292
  287.7 597.6 %reduce-scatter.5.cloned.1.call-start = ((), (), s32[]{:S(2)}) async-start(), calls=%async_computation.7 | async-start | bytes 5898240 | tf_op jit(solution)/shard_map/reduce_scatter | solution.py:194
  289.4 92.4 %copy-start.13 = (bf16[1024,768]{0,1:T(8,128)(2,1)}, bf16[1024,768]{0,1:T(8,128)(2,1)S(1)}, u32[]{:S(2)}) copy-start(bf16[1024,768]{0,1:T(8,128)(2,1)S(1)} %copy.46) | copy-start | bytes 4718596
  289.6 4.6 copy-start.93
  289.6 236.6 %copy-start.91 = (f32[8]{0:T(128)}, f32[8]{0:T(128)S(1)}, u32[]{:S(2)}) copy-start(f32[8]{0:T(128)S(1)} %maximum_rsqrt_fusion.1) | copy-start | bytes 100
  294.1 317.4 %copy-start.34 = (f32[1024,16]{0,1:T(8,128)}, f32[1024,16]{0,1:T(8,128)S(1)}, u32[]{:S(2)}) copy-start(f32[1024,16]{0,1:T(8,128)S(1)} %get-tuple-element.272) | copy-start | bytes 196612
  294.1 317.4 %copy-start.58 = (f32[1024]{0:T(1024)}, f32[1024]{0:T(1024)S(1)}, u32[]{:S(2)}) copy-start(f32[1024]{0:T(1024)S(1)} %maximum_rsqrt_fusion) | copy-start | bytes 12292
  294.4 231.8 %copy-start.40 = (f32[1024,8]{0,1:T(8,128)}, f32[1024,8]{0,1:T(8,128)S(1)}, u32[]{:S(2)}) copy-start(f32[1024,8]{0,1:T(8,128)S(1)} %get-tuple-element.274) | copy-start | bytes 98308
  294.4 231.8 %copy-start.77 = (f32[1024]{0:T(1024)}, f32[1024]{0:T(1024)S(1)}, u32[]{:S(2)}) copy-start(f32[1024]{0:T(1024)S(1)} %get-tuple-element.273) | copy-start | bytes 12292
  294.4 231.8 %copy-start.79 = (f32[1024]{0:T(1024)}, f32[1024]{0:T(1024)S(1)}, u32[]{:S(2)}) copy-start(f32[1024]{0:T(1024)S(1)} %fusion.106) | copy-start | bytes 12292
  377.2 4.6 copy-start.60
  381.8 144.5 %copy-start.87 = (f32[1024]{0:T(1024)}, f32[1024]{0:T(1024)S(1)}, u32[]{:S(2)}) copy-start(f32[1024]{0:T(1024)S(1)} %fusion.74) | copy-start | bytes 12292
  385.2 9.4 copy-start.84
  487.4 22.5 %slice-start = ((s8[4718592]{0:T(1024)(128)(4,1)}), s8[524288]{0:T(1024)(128)(4,1)S(1)}, s32[]{:S(2)}) async-start(s8[4718592]{0:T(1024)(128)(4,1)} %bitcast.189), calls=%async_computation.9 | async-start | bytes 1048576
  487.4 22.4 %slice-start.1 = ((s8[4718592]{0:T(1024)(128)(4,1)}), s8[4194304]{0:T(1024)(128)(4,1)S(1)}, s32[]{:S(2)}) async-start(s8[4718592]{0:T(1024)(128)(4,1)} %bitcast.189), calls=%async_computation.10 | async-start | bytes 8388608
  509.9 11.4 %copy-start.103 = (bf16[2048,3072]{1,0:T(8,128)(2,1)}, bf16[2048,3072]{1,0:T(8,128)(2,1)S(1)}, u32[]{:S(2)}) copy-start(bf16[2048,3072]{1,0:T(8,128)(2,1)S(1)} %fusion.37) | copy-start | bytes 37748740
  521.3 74.0 %all-to-all-start.3 = ((bf16[8,256,768]{2,1,0:T(8,128)(2,1)}), bf16[8,256,768]{2,1,0:T(8,128)(2,1)}, u32[]{:S(2)}, u32[]{:S(2)}) async-start(bf16[8,256,768]{2,1,0:T(8,128)(2,1)} %bitcast.164), calls=%async_computation.3 | async-start | bytes 6291456 | tf_op jit(solution)/shard_map/all_to_all | solution.py:182
  525.7 362.4 %reduce-scatter.3.cloned.1.call-start = ((), (), s32[]{:S(2)}) async-start(), calls=%async_computation.6 | async-start | bytes 5898240 | tf_op jit(solution)/shard_map/reduce_scatter | solution.py:191
  526.9 84.7 %copy-start.42 = (f32[1024,16]{0,1:T(8,128)}, f32[1024,16]{0,1:T(8,128)S(1)}, u32[]{:S(2)}) copy-start(f32[1024,16]{0,1:T(8,128)S(1)} %get-tuple-element.278) | copy-start | bytes 196612
  526.9 84.6 %copy-start.67 = (f32[1024]{0:T(1024)}, f32[1024]{0:T(1024)S(1)}, u32[]{:S(2)}) copy-start(f32[1024]{0:T(1024)S(1)} %select_multiply_fusion) | copy-start | bytes 12292
  542.5 468.8 %all-reduce.4.cloned.1.call-start = ((), (), s32[]{:S(2)}) async-start(), calls=%async_computation.8 | async-start | bytes 18874368 | tf_op jit(solution)/shard_map/psum | solution.py:268
  611.5 6.5 copy-start.74
  611.5 6.5 copy-start.7
  611.5 6.5 copy-start.18
  628.9 11.5 %copy-start.19 = (bf16[1024,12,64]{0,2,1:T(8,128)(2,1)S(1)}, bf16[1024,12,64]{0,2,1:T(8,128)(2,1)}, u32[]{:S(2)}) copy-start(bf16[1024,12,64]{0,2,1:T(8,128)(2,1)} %get-tuple-element.502) | copy-start | bytes 4718596 | tf_op jit(solution)/shard_map/while
  714.9 11.5 %copy-start.19 = (bf16[1024,12,64]{0,2,1:T(8,128)(2,1)S(1)}, bf16[1024,12,64]{0,2,1:T(8,128)(2,1)}, u32[]{:S(2)}) copy-start(bf16[1024,12,64]{0,2,1:T(8,128)(2,1)} %get-tuple-element.502) | copy-start | bytes 4718596 | tf_op jit(solution)/shard_map/while
  799.4 3.6 copy-start.5
  803.0 12.9 %copy-start.29 = (bf16[96,8,2,512]{3,1,2,0:T(8,128)(2,1)}, bf16[96,8,2,512]{3,1,2,0:T(8,128)(2,1)S(1)}, u32[]{:S(2)}) copy-start(bf16[96,8,2,512]{3,1,2,0:T(8,128)(2,1)S(1)} %copy.62) | copy-start | bytes 4718596
  803.3 9.6 copy-start.33
  803.3 3.7 copy-start.32
  840.6 3.6 copy-start.85
  840.6 3.6 copy-start.86
  (67 other events, 134.5 us)
Sparse Core Ops, SparseCore 0:
  487.5 46.9 reduce-scatter.4
  542.6 49.1 reduce-scatter.2
Sparse Core Ops, SparseCore 1:
  819.2 191.9 all-reduce.3
where the time goes:
time: 1040 us; the launch traced here: 1030 us
  matrix products  352 us (34%)
  waiting for transfers between devices  236 us (23%)
  blocking collectives  193 us (19%)
  local copies, waits for them, and re-layouts  110 us (11%)
  other arithmetic  103 us (10%)
  between operations  17.3 us (2%)
    psum x1, waiting for transfers between devices, on_device(): lax.psum((dense_terms[0], dense_terms[1], dense_terms[2], dense_terms[3],...  120 us
    all_to_all x1, blocking collectives, on_device(): lax.all_to_all(dispatched, 'expert', split_axis=0, concat_axis=0, tiled=T...  77.8 us
    all_to_all x1, blocking collectives, on_device(): lax.all_to_all(scaled_slots, 'expert', split_axis=0, concat_axis=0, tiled...  74.5 us
    all_to_all x1, waiting for transfers between devices, on_device(): lax.all_to_all(produced, 'expert', split_axis=0, concat_axis=0, tiled=True)  63 us
    dot_general x1, matrix products, on_device(): pre = jnp.dot(flat_rows, expert_in[0], preferred_element_type=jnp.float32)  63 us
    all_to_all x1, waiting for transfers between devices, on_device(): lax.all_to_all(grad_normed_rows.reshape(experts, capacity, width), 'exper...  52.8 us
    dot_general x4, matrix products, block_scores(): jnp.einsum('qhd,khd->hqk', query_block, key_heads, preferred_element_type...  47.2 us
    dot_general x6, matrix products, contract_cols(): lax.dot_general(left, right, (((1,), (1,)), ((), ())), preferred_element_...  43 us
  transfers between devices with their start and end apart: 5, of which 3 were waited for; matrix products, arithmetic and copies ran while one was open for 29% of the time, Pallas kernels for 0%

commit v1 on v0

v1 whole, which is shorter than its diff:
```python
import functools

import jax
import jax.numpy as jnp
from jax import lax
from jax.experimental import pallas as pl
from jax.experimental.pallas import tpu as pltpu
from jax.sharding import PartitionSpec as P

HEAD_DIM = 64
PAIR = 2 * HEAD_DIM
SHARPNESS = 0.25
EXACT = lax.Precision.HIGHEST
BF16 = jnp.bfloat16
F32 = jnp.float32
FAR = -1e30
MIB = 1 << 20


def mm(left, right):
    return jnp.dot(left, right, preferred_element_type=F32)


def mm_rows(left, right, precision=None):
    return lax.dot_general(
        left, right, (((0,), (0,)), ((), ())), precision=precision, preferred_element_type=F32
    )


def mm_cols(left, right, precision=None):
    return lax.dot_general(
        left, right, (((1,), (1,)), ((), ())), precision=precision, preferred_element_type=F32
    )


def iota(shape, axis):
    return lax.broadcasted_iota(jnp.int32, shape, axis)


def one_hot(condition):
    return jnp.where(condition, 1.0, 0.0).astype(BF16)


def params(limit=56):
    return pltpu.CompilerParams(vmem_limit_bytes=limit * MIB)


def cost(flops, moved, trans=0):
    return pl.CostEstimate(flops=int(flops), bytes_accessed=int(moved), transcendentals=int(trans))


def spec_all(shape):
    zeros = (0,) * len(shape)
    return pl.BlockSpec(shape, lambda *ids: zeros)


def slot_row_of(route_row, experts, cap):
    tokens = route_row.shape[1]
    padded = max(8, experts)
    hits = one_hot(iota((padded, tokens), 0) == route_row)
    earlier = one_hot(iota((tokens, tokens), 0) < iota((tokens, tokens), 1))
    ranks = mm(hits, earlier)
    rank = jnp.sum(ranks * hits.astype(F32), 0, keepdims=True)
    return route_row * cap + rank.astype(jnp.int32)


def slot_col_of(route_col, experts, cap):
    tokens = route_col.shape[0]
    hits = one_hot(iota((tokens, 128), 1) == route_col)
    earlier = one_hot(iota((tokens, tokens), 1) < iota((tokens, tokens), 0))
    ranks = mm(earlier, hits)
    rank = jnp.sum(ranks * hits.astype(F32), 1, keepdims=True)
    return route_col * cap + rank.astype(jnp.int32)


def as_row(col):
    rows = col.shape[0]
    eye = iota((rows, rows), 0) == iota((rows, rows), 1)
    return jnp.sum(jnp.where(eye, col, 0.0), 0, keepdims=True)


def as_col(row):
    rows = row.shape[1]
    eye = iota((rows, rows), 0) == iota((rows, rows), 1)
    return jnp.sum(jnp.where(eye, row, 0.0), 1, keepdims=True)


def gather_kernel(experts, cap, route_ref, x_ref, out_ref, slot_ref):
    step = pl.program_id(0)

    @pl.when(step == 0)
    def _():
        slot = slot_row_of(route_ref[...], experts, cap)
        slot_ref[...] = jnp.broadcast_to(slot, slot_ref.shape)

    rows = out_ref.shape[0]
    tokens = x_ref.shape[0]
    pick = one_hot(iota((rows, tokens), 0) + step * rows == slot_ref[0:1, :])
    out_ref[...] = mm(pick, x_ref[...]).astype(BF16)


def gather_slots(route_row, x, experts, cap):
    tokens, width = x.shape
    slots = experts * cap
    rows = 256
    return pl.pallas_call(
        functools.partial(gather_kernel, experts, cap),
        grid=(slots // rows,),
        in_specs=[spec_all((1, tokens)), spec_all((tokens, width))],
        out_specs=pl.BlockSpec((rows, width), lambda i: (i, 0)),
        out_shape=jax.ShapeDtypeStruct((slots, width), BF16),
        scratch_shapes=[pltpu.VMEM((8, tokens), jnp.int32)],
        compiler_params=params(32),
        cost_estimate=cost(2 * slots * tokens * width, 2 * width * (tokens + slots)),
        name="gather_slots",
    )(route_row, x)


def norm_parts(values):
    average = jnp.mean(values, -1, keepdims=True)
    centred = values - average
    spread = jnp.mean(centred * centred, -1, keepdims=True)
    scale = lax.rsqrt(spread + 1e-05)
    return centred * scale, scale


def norm_back(grad, gain, unit, scale):
    grad_unit = grad * gain
    inner = jnp.mean(grad_unit * unit, -1, keepdims=True)
    return scale * (grad_unit - jnp.mean(grad_unit, -1, keepdims=True) - unit * inner)


def qkv_kernel(x_ref, gain_ref, bias_ref, wq_ref, wk_ref, wv_ref, q_ref, k_ref, v_ref):
    unit, _ = norm_parts(x_ref[...].astype(F32))
    normed = (unit * gain_ref[...] + bias_ref[...]).astype(BF16)
    for w_ref, o_ref in ((wq_ref, q_ref), (wk_ref, k_ref), (wv_ref, v_ref)):
        o_ref[...] = mm(normed, w_ref[...]).astype(BF16)


def qkv(x, gain, bias, wq, wk, wv):
    tokens, width = x.shape
    rows = 256
    block = pl.BlockSpec((rows, width), lambda i: (i, 0))
    made = jax.ShapeDtypeStruct((tokens, width), BF16)
    return pl.pallas_call(
        qkv_kernel,
        grid=(tokens // rows,),
        in_specs=[block, spec_all((1, width)), spec_all((1, width))]
        + [spec_all((width, width))] * 3,
        out_specs=[block] * 3,
        out_shape=[made] * 3,
        compiler_params=params(32),
        cost_estimate=cost(6 * tokens * width * width, 2 * (4 * tokens * width + 3 * width * width)),
        name="qkv",
    )(x, gain, bias, wq, wk, wv)


def key_window(block, rows, tokens, longest):
    first = max(0, (block * rows - longest + 1) // 128 * 128)
    last = min(tokens, -(-(block * rows + rows - 1 + longest) // 128) * 128)
    return first, last


def attention_kernel(rows, longest, q_ref, k_ref, v_ref, seg_ref, mixed_ref, prob_ref):
    tokens = q_ref.shape[0]
    lane = iota((tokens, PAIR), 1)
    own = (lane < HEAD_DIM, lane >= HEAD_DIM)
    seg = seg_ref[...]
    queries = q_ref[...] * jnp.asarray(HEAD_DIM**-0.5, BF16)
    keys = k_ref[...]
    for h in range(2):
        other = (1 - h) * HEAD_DIM
        q_tag = jnp.where(lane - other == seg, 1.0, 0.0).astype(BF16)
        k_tag = jnp.where(lane - other == seg, 0.0, FAR)
        k_tag = jnp.where((lane >= other) & (lane < other + 8), k_tag, 0.0).astype(BF16)
        q_h = jnp.where(own[h], queries, q_tag)
        k_h = jnp.where(own[h], keys, k_tag)
        for block in range(tokens // rows):
            first, last = key_window(block, rows, tokens, longest)
            mine = slice(block * rows, (block + 1) * rows)
            scores = mm_cols(k_h[first:last], q_h[mine])
            largest = jnp.max(scores, 0, keepdims=True)
            weights = jnp.exp(scores - largest)
            total = jnp.sum(weights, 0, keepdims=True)
            probs = (weights * (1.0 / total)).astype(BF16)
            prob_ref[h, first:last, mine] = probs
            out = mm_rows(probs, v_ref[first:last, :]).astype(BF16)
            if h == 0:
                mixed_ref[mine, :] = out
            else:
                mixed_ref[mine, :] = jnp.where(own[1][mine], out, mixed_ref[mine, :])


def attention(q, k, v, seg_col, longest):
    tokens, width = q.shape
    pairs = width // PAIR
    rows = 256
    block = pl.BlockSpec((tokens, PAIR), lambda p: (0, p))
    return pl.pallas_call(
        functools.partial(attention_kernel, rows, longest),
        grid=(pairs,),
        in_specs=[block, block, block, spec_all((tokens, 1))],
        out_specs=[block, pl.BlockSpec((2, tokens, tokens), lambda p: (p, 0, 0))],
        out_shape=[
            jax.ShapeDtypeStruct((tokens, width), BF16),
            jax.ShapeDtypeStruct((2 * pairs, tokens, tokens), BF16),
        ],
        compiler_params=params(),
        cost_estimate=cost(
            4 * 2 * pairs * tokens * tokens * 256, 4 * pairs * tokens * tokens, tokens * tokens
        ),
        name="attention",
    )(q, k, v, seg_col)


def attention_back_kernel(
    rows, longest, q_ref, k_ref, v_ref, do_ref, prob_ref, delta_ref,
    dq_ref, dk_ref, dv_ref, dk_sum, dv_sum,
):
    tokens = q_ref.shape[0]
    lane = iota((tokens, PAIR), 1)
    own = (lane < HEAD_DIM, lane >= HEAD_DIM)
    zero = jnp.zeros((), BF16)
    scale = HEAD_DIM**-0.5
    dk_sum[...] = jnp.zeros_like(dk_sum)
    dv_sum[...] = jnp.zeros_like(dv_sum)
    for block in range(tokens // rows):
        first, last = key_window(block, rows, tokens, longest)
        mine = slice(block * rows, (block + 1) * rows)
        values = v_ref[first:last, :]
        dq = jnp.zeros((rows, PAIR), F32)
        dk = jnp.zeros((last - first, PAIR), F32)
        dv = jnp.zeros((last - first, PAIR), F32)
        for h in range(2):
            do_h = jnp.where(own[h][mine], do_ref[mine, :], zero)
            q_h = jnp.where(own[h][mine], q_ref[mine, :], zero)
            k_h = jnp.where(own[h][first:last], k_ref[first:last, :], zero)
            probs = prob_ref[h, first:last, mine]
            grad_probs = mm_cols(values, do_h)
            grad_scores = (
                probs.astype(F32) * (grad_probs - delta_ref[0, h : h + 1, mine])
            ).astype(BF16)
            dq = dq + mm_rows(grad_scores, k_h)
            dk = dk + mm(grad_scores, q_h)
            dv = dv + mm(probs, do_h)
        dq_ref[mine, :] = (dq * scale).astype(BF16)
        dk_sum[first:last, :] += dk
        dv_sum[first:last, :] += dv
    dk_ref[...] = (dk_sum[...] * scale).astype(BF16)
    dv_ref[...] = dv_sum[...].astype(BF16)


def attention_back(q, k, v, grad_mixed, probs, delta, longest):
    tokens, width = q.shape
    pairs = width // PAIR
    rows = 256
    block = pl.BlockSpec((tokens, PAIR), lambda p: (0, p))
    made = jax.ShapeDtypeStruct((tokens, width), BF16)
    return pl.pallas_call(
        functools.partial(attention_back_kernel, rows, longest),
        grid=(pairs,),
        in_specs=[block] * 4
        + [
            pl.BlockSpec((2, tokens, tokens), lambda p: (p, 0, 0)),
            pl.BlockSpec((1, 8, tokens), lambda p: (p, 0, 0)),
        ],
        out_specs=[block] * 3,
        out_shape=[made] * 3,
        scratch_shapes=[pltpu.VMEM((tokens, PAIR), F32)] * 2,
        compiler_params=params(),
        cost_estimate=cost(8 * 2 * pairs * tokens * tokens * 256, 4 * pairs * tokens * tokens),
        name="attention_back",
    )(q, k, v, grad_mixed, probs, delta)


def router_parts(normed, proj, embed, route, experts):
    low = jnp.dot(normed, proj, precision=EXACT, preferred_element_type=F32)
    low_squares = jnp.sum(low * low, -1, keepdims=True)
    low_scale = lax.rsqrt(jnp.maximum(low_squares, 1.0))
    low_unit = low * low_scale
    squares = jnp.sum(embed * embed, -1, keepdims=True)
    table_scale = lax.rsqrt(jnp.maximum(squares, 1.0))
    table = embed * table_scale
    logits = mm_cols(low_unit, table, EXACT) / SHARPNESS
    lane = iota(logits.shape, 1)
    logits = jnp.where(lane < experts, logits, FAR)
    weights = jnp.exp(logits - jnp.max(logits, -1, keepdims=True))
    probs = weights / jnp.sum(weights, -1, keepdims=True)
    chosen = jnp.where(lane == route, 1.0, 0.0)
    gate = jnp.sum(probs * chosen, -1, keepdims=True)
    return gate, probs, chosen, low, low_squares, low_scale, low_unit, squares, table_scale, table


def clipped_back(grad_unit, raw, scale, squares):
    share = jnp.where(squares > 1.0, 1.0, jnp.where(squares == 1.0, 0.5, 0.0))
    inner = jnp.sum(grad_unit * raw, -1, keepdims=True)
    return scale * grad_unit - share * scale * scale * scale * inner * raw


def middle_kernel(
    experts, cap, mixed_ref, x_ref, wo_ref, gain_ref, bias_ref, proj_ref, embed_ref,
    route_ref, route_row_ref, hidden_ref, gate_ref, slots_ref, gates_ref, kept,
):
    tokens, width = x_ref.shape
    rows = 256

    def row_block(i, carry):
        at = pl.ds(pl.multiple_of(i * rows, rows), rows)
        hidden = x_ref[at, :].astype(F32) + mm(mixed_ref[at, :], wo_ref[...])
        hidden_ref[at, :] = hidden
        unit, _ = norm_parts(hidden)
        normed = unit * gain_ref[...] + bias_ref[...]
        gate = router_parts(normed, proj_ref[...], embed_ref[...], route_ref[at, :], experts)[0]
        gate_ref[at, :] = jnp.broadcast_to(gate, (rows, 128))
        high = gate.astype(BF16).astype(F32)
        mid = (gate - high).astype(BF16).astype(F32)
        rest = gate - high - mid
        lane = iota((rows, 128), 1)
        split = jnp.where(lane == 0, high, jnp.where(lane == 1, mid, jnp.where(lane == 2, rest, 0.0)))
        kept[at, 0:width] = normed.astype(BF16)
        kept[at, width : width + 128] = split.astype(BF16)
        return carry

    lax.fori_loop(0, tokens // rows, row_block, 0)
    slot = slot_row_of(route_row_ref[...], experts, cap)

    def slot_block(i, carry):
        at = pl.ds(pl.multiple_of(i * rows, rows), rows)
        pick = one_hot(iota((rows, tokens), 0) + i * rows == slot)
        got = mm(pick, kept[...])
        slots_ref[at, :] = got[:, 0:width].astype(BF16)
        gates_ref[pl.ds(i, 1), :, :] = jnp.broadcast_to(
            as_row(jnp.sum(got[:, width : width + 128], 1, keepdims=True)), (8, rows)
        )[None]
        return carry

    lax.fori_loop(0, experts * cap // rows, slot_block, 0)


def middle(mixed, x, wo, gain, bias, proj, embed, route, route_row, experts, cap):
    tokens, width = x.shape
    slots = experts * cap
    args = (mixed, x, wo, gain, bias, proj, embed, route, route_row)
    return pl.pallas_call(
        functools.partial(middle_kernel, experts, cap),
        out_shape=[
            jax.ShapeDtypeStruct((tokens, width), F32),
            jax.ShapeDtypeStruct((tokens, 128), F32),
            jax.ShapeDtypeStruct((slots, width), BF16),
            jax.ShapeDtypeStruct((slots // 256, 8, 256), F32),
        ],
        scratch_shapes=[pltpu.VMEM((tokens, width + 128), BF16)],
        compiler_params=params(),
        cost_estimate=cost(2 * tokens * width * (width + slots), 16 * tokens * width),
        name="middle",
    )(*args)


def gelu_parts(pre):
    size = jnp.abs(pre)
    t = pl.reciprocal(1.0 + 0.23164189298 * size, approx=False)
    bell = jnp.exp(-0.5 * pre * pre)
    tail = t * (
        0.127414796
        + t * (-0.142248368 + t * (0.7107068705 + t * (-0.7265760135 + t * 0.5307027145)))
    )
    tail = tail * bell
    phi_sum = jnp.where(pre >= 0, 1.0 - tail, tail)
    return phi_sum, pre * bell * 0.3989422804014327


def expert_kernel(
    x_ref, up_ref, gate_ref, w_in_ref, w_out_ref,
    made_ref, back_ref, gate_grad_ref, active_ref, grad_pre_ref, scaled_ref,
):
    hidden = w_in_ref.shape[1]
    step = 512
    gate = as_col(gate_ref[0, 0:1, :])
    up = up_ref[...].astype(F32)
    scaled = (up * gate).astype(BF16)
    scaled_ref[...] = scaled
    x = x_ref[...]
    for at in range(0, hidden, step):
        part = slice(at, at + step)
        pre = mm(x, w_in_ref[:, part])
        grad_active = mm_cols(scaled, w_out_ref[part, :])
        phi_sum, slope = gelu_parts(pre)
        active_ref[:, part] = (pre * phi_sum).astype(BF16)
        grad_pre_ref[:, part] = (grad_active * (phi_sum + slope)).astype(BF16)
    made = mm(active_ref[...], w_out_ref[...]).astype(BF16)
    made_ref[...] = made
    gate_grad = jnp.sum(up * made.astype(F32), 1, keepdims=True)
    gate_grad_ref[...] = jnp.broadcast_to(as_row(gate_grad), (8, x.shape[0]))[None]
    back_ref[...] = mm_cols(grad_pre_ref[...], w_in_ref[...]).astype(BF16)


def expert(x, up, gates, w_in, w_out):
    slots, width = x.shape
    hidden = w_in.shape[1]
    rows = 256
    block = pl.BlockSpec((rows, width), lambda i: (i, 0))
    wide = pl.BlockSpec((rows, hidden), lambda i: (i, 0))
    line = pl.BlockSpec((1, 8, rows), lambda i: (i, 0, 0))
    made = jax.ShapeDtypeStruct((slots, width), BF16)
    made_wide = jax.ShapeDtypeStruct((slots, hidden), BF16)
    return pl.pallas_call(
        expert_kernel,
        grid=(slots // rows,),
        in_specs=[block, block, line, spec_all((width, hidden)), spec_all((hidden, width))],
        out_specs=[block, block, line, wide, wide, block],
        out_shape=[
            made,
            made,
            jax.ShapeDtypeStruct((slots // rows, 8, rows), F32),
            made_wide,
            made_wide,
            made,
        ],
        compiler_params=params(),
        cost_estimate=cost(8 * slots * width * hidden, 4 * slots * hidden),
        name="expert",
    )(x, up, gates, w_in, w_out)


def expert_grads_kernel(x_ref, scaled_ref, active_ref, grad_pre_ref, din_ref, dout_ref):
    din_ref[...] = mm_rows(x_ref[...], grad_pre_ref[...]).astype(BF16)
    dout_ref[...] = mm_rows(active_ref[...], scaled_ref[...]).astype(BF16)


def expert_grads(x, scaled, active, grad_pre):
    slots, width = x.shape
    hidden = active.shape[1]
    step = 512
    tall = pl.BlockSpec((slots, step), lambda i: (0, i))
    return pl.pallas_call(
        expert_grads_kernel,
        grid=(hidden // step,),
        in_specs=[spec_all((slots, width)), spec_all((slots, width)), tall, tall],
        out_specs=[
            pl.BlockSpec((width, step), lambda i: (0, i)),
            pl.BlockSpec((step, width), lambda i: (i, 0)),
        ],
        out_shape=[
            jax.ShapeDtypeStruct((width, hidden), BF16),
            jax.ShapeDtypeStruct((hidden, width), BF16),
        ],
        compiler_params=params(),
        cost_estimate=cost(4 * slots * width * hidden, 4 * slots * hidden + 4 * width * hidden),
        name="expert_grads",
    )(x, scaled, active, grad_pre)


def middle_back_kernel(
    experts, cap, back_ref, gate_grads_ref, hidden_ref, cot_ref, mixed_ref, wo_ref,
    gain_ref, bias_ref, proj_ref, embed_ref, route_ref,
    grad_hidden_ref, grad_mixed_ref, delta_ref, dwo_ref, small_ref, dproj_ref, dembed_ref,
    slot_ref, low_ref,
):
    tokens, width = hidden_ref.shape
    slots = back_ref.shape[0]
    rows = 256
    slot_ref[...] = jnp.broadcast_to(slot_col_of(route_ref[...], experts, cap), slot_ref.shape)
    small_ref[...] = jnp.zeros_like(small_ref)
    dproj_ref[...] = jnp.zeros_like(dproj_ref)
    dembed_ref[...] = jnp.zeros_like(dembed_ref)
    heads = width // HEAD_DIM
    pairs = heads // 2
    head_of = iota((8 * pairs, width), 1) // HEAD_DIM
    line = iota((8 * pairs, width), 0)
    head_lines = jnp.where(head_of == line // 8 * 2 + line % 8, 1.0, 0.0)
    head_lines = jnp.where(line % 8 < 2, head_lines, 0.0)

    def row_block(i, carry):
        at = pl.ds(pl.multiple_of(i * rows, rows), rows)
        place = slot_ref[at, 0:1]
        pick = iota((rows, slots), 1) == place
        grad = mm(one_hot(pick), back_ref[...])
        gate_grad = jnp.zeros((rows, 1), F32)
        for e in range(slots // rows):
            gate_grad = gate_grad + jnp.sum(
                jnp.where(pick[:, e * rows : (e + 1) * rows], gate_grads_ref[e, 0:1, :], 0.0),
                1,
                keepdims=True,
            )
        unit, scale = norm_parts(hidden_ref[at, :])
        normed = unit * gain_ref[...] + bias_ref[...]
        proj = proj_ref[...]
        embed = embed_ref[...]
        gate, probs, chosen, low, low_squares, low_scale, low_unit, _, _, table = router_parts(
            normed, proj, embed, route_ref[at, :], experts
        )
        grad_logits = gate_grad * gate * (chosen - probs) / SHARPNESS
        grad_unit = jnp.dot(grad_logits, table, precision=EXACT, preferred_element_type=F32)
        dembed_ref[...] += mm_rows(grad_logits, low_unit, EXACT)
        grad_low = clipped_back(grad_unit, low, low_scale, low_squares)
        dproj_ref[...] += mm_rows(normed, grad_low, EXACT)
        grad = grad + mm_cols(grad_low, proj, EXACT)
        small_ref[0:1, :] += jnp.sum(grad * unit, 0, keepdims=True)
        small_ref[1:2, :] += jnp.sum(grad, 0, keepdims=True)
        grad_hidden = cot_ref[at, :].astype(F32) + norm_back(grad, gain_ref[...], unit, scale)
        grad_hidden_ref[at, :] = grad_hidden
        low_grad = grad_hidden.astype(BF16)
        low_ref[at, :] = low_grad
        grad_mixed = mm_cols(low_grad, wo_ref[...]).astype(BF16)
        grad_mixed_ref[at, :] = grad_mixed
        products = grad_mixed.astype(F32) * mixed_ref[at, :].astype(F32)
        lines = mm_cols(head_lines, products, EXACT)
        for p in range(pairs):
            delta_ref[p, :, at] = lines[8 * p : 8 * p + 8, :]
        return carry

    lax.fori_loop(0, tokens // rows, row_block, 0)
    embed = embed_ref[...]
    squares = jnp.sum(embed * embed, -1, keepdims=True)
    table_scale = lax.rsqrt(jnp.maximum(squares, 1.0))
    dembed_ref[...] = clipped_back(dembed_ref[...], embed, table_scale, squares)
    dwo_ref[...] = mm_rows(mixed_ref[...], low_ref[...])


def middle_back(
    back, gate_grads, hidden, cot, mixed, wo, gain, bias, proj, embed, route, experts, cap
):
    tokens, width = hidden.shape
    slots = back.shape[0]
    args = (back, gate_grads, hidden, cot, mixed, wo, gain, bias, proj, embed, route)
    return pl.pallas_call(
        functools.partial(middle_back_kernel, experts, cap),
        out_shape=[
            jax.ShapeDtypeStruct((tokens, width), F32),
            jax.ShapeDtypeStruct((tokens, width), BF16),
            jax.ShapeDtypeStruct((width // PAIR, 8, tokens), F32),
            jax.ShapeDtypeStruct((width, width), F32),
            jax.ShapeDtypeStruct((8, width), F32),
            jax.ShapeDtypeStruct(proj.shape, F32),
            jax.ShapeDtypeStruct(embed.shape, F32),
        ],
        scratch_shapes=[pltpu.VMEM((tokens, 128), jnp.int32), pltpu.VMEM((tokens, width), BF16)],
        compiler_params=params(),
        cost_estimate=cost(2 * tokens * width * (2 * width + slots), 20 * tokens * width),
        name="middle_back",
    )(*args)


def qkv_back_kernel(
    x_ref, gain_ref, bias_ref, grad_hidden_ref, dq_ref, dk_ref, dv_ref, wq_ref, wk_ref, wv_ref,
    grad_ref, dwq_ref, dwk_ref, dwv_ref, small_ref, low_ref,
):
    tokens, width = x_ref.shape
    rows = 256
    small_ref[...] = jnp.zeros_like(small_ref)

    def row_block(i, carry):
        at = pl.ds(pl.multiple_of(i * rows, rows), rows)
        unit, scale = norm_parts(x_ref[at, :].astype(F32))
        low_ref[at, :] = (unit * gain_ref[...] + bias_ref[...]).astype(BF16)
        grad = (
            mm_cols(dq_ref[at, :], wq_ref[...])
            + mm_cols(dk_ref[at, :], wk_ref[...])
            + mm_cols(dv_ref[at, :], wv_ref[...])
        )
        small_ref[0:1, :] += jnp.sum(grad * unit, 0, keepdims=True)
        small_ref[1:2, :] += jnp.sum(grad, 0, keepdims=True)
        grad_ref[at, :] = grad_hidden_ref[at, :] + norm_back(grad, gain_ref[...], unit, scale)
        return carry

    lax.fori_loop(0, tokens // rows, row_block, 0)
    low = low_ref[...]
    dwq_ref[...] = mm_rows(low, dq_ref[...])
    dwk_ref[...] = mm_rows(low, dk_ref[...])
    dwv_ref[...] = mm_rows(low, dv_ref[...])


def qkv_back(x, gain, bias, grad_hidden, dq, dk, dv, wq, wk, wv):
    tokens, width = x.shape
    square = jax.ShapeDtypeStruct((width, width), F32)
    return pl.pallas_call(
        qkv_back_kernel,
        out_shape=[
            jax.ShapeDtypeStruct((tokens, width), F32),
            square,
            square,
            square,
            jax.ShapeDtypeStruct((8, width), F32),
        ],
        scratch_shapes=[pltpu.VMEM((tokens, width), BF16)],
        compiler_params=params(),
        cost_estimate=cost(12 * tokens * width * width, 20 * tokens * width),
        name="qkv_back",
    )(x, gain, bias, grad_hidden, dq, dk, dv, wq, wk, wv)


def output_kernel(experts, cap, made_ref, hidden_ref, gate_ref, route_ref, out_ref, slot_ref):
    tokens, width = hidden_ref.shape
    slots = made_ref.shape[0]
    rows = 256
    slot_ref[...] = jnp.broadcast_to(slot_col_of(route_ref[...], experts, cap), slot_ref.shape)

    def row_block(i, carry):
        at = pl.ds(pl.multiple_of(i * rows, rows), rows)
        pick = one_hot(iota((rows, slots), 1) == slot_ref[at, 0:1])
        produced = mm(pick, made_ref[...])
        out_ref[at, :] = (hidden_ref[at, :] + gate_ref[at, 0:1] * produced).astype(BF16)
        return carry

    lax.fori_loop(0, tokens // rows, row_block, 0)


def layer_output(made, hidden, gate, route, experts, cap):
    tokens, width = hidden.shape
    return pl.pallas_call(
        functools.partial(output_kernel, experts, cap),
        out_shape=jax.ShapeDtypeStruct((tokens, width), BF16),
        scratch_shapes=[pltpu.VMEM((tokens, 128), jnp.int32)],
        compiler_params=params(),
        cost_estimate=cost(2 * tokens * width * made.shape[0], 10 * tokens * width),
        name="layer_output",
    )(made, hidden, gate, route)


def exchange(array, experts):
    split = array.reshape(experts, array.shape[0] // experts, *array.shape[1:])
    return lax.all_to_all(split, "expert", split_axis=0, concat_axis=0, tiled=True).reshape(
        array.shape
    )


def lines_out(lines, experts, cap):
    return lines[:, 0, :].reshape(experts, cap)


def lines_in(rows):
    flat = rows.reshape(-1, 1, 256)
    return jnp.broadcast_to(flat, (flat.shape[0], 8, 256))


def on_device(
    tokens,
    segment_ids,
    routes,
    norm1_gain,
    norm1_bias,
    query_weight,
    w_key,
    w_value,
    w_output,
    norm2_gain,
    norm2_bias,
    router_proj,
    expert_embed,
    expert_in,
    expert_out,
    cotangent,
):
    count, width = tokens.shape
    experts = lax.axis_size("expert")
    cap = 2 * count // experts
    longest = segment_ids.shape[1] // 2
    route_row = routes.reshape(1, count)
    seg_col = segment_ids.reshape(count, 1)
    gain1, bias1 = norm1_gain[None], norm1_bias[None]
    gain2, bias2 = norm2_gain[None], norm2_bias[None]
    space = router_proj.shape[1]
    proj = jnp.pad(router_proj, ((0, 0), (0, 128 - space)))
    embed = jnp.pad(expert_embed, ((0, 128 - experts), (0, 128 - space)))

    up_slots = gather_slots(route_row, cotangent, experts, cap)
    up_here = exchange(up_slots, experts)
    q, k, v = qkv(tokens, gain1, bias1, query_weight, w_key, w_value)
    mixed, probs = attention(q, k, v, seg_col, longest)
    hidden, gate, slots, gates = middle(
        mixed, tokens, w_output, gain2, bias2, proj, embed, routes, route_row, experts, cap
    )
    x_here = exchange(slots, experts)
    gates_here = lines_in(exchange(lines_out(gates, experts, cap), experts))
    made, back, gate_grads, active, grad_pre, scaled = expert(
        x_here, up_here, gates_here, expert_in[0], expert_out[0]
    )
    back_home = exchange(back, experts)
    gate_grads_home = lines_in(exchange(lines_out(gate_grads, experts, cap), experts))
    grad_in, grad_out = expert_grads(x_here, scaled, active, grad_pre)
    made_home = exchange(made, experts)
    grad_in = lax.psum_scatter(grad_in[None], "dp", scatter_dimension=2, tiled=True)
    grad_out = lax.psum_scatter(grad_out[None], "dp", scatter_dimension=1, tiled=True)
    grad_hidden, grad_mixed, delta, dwo, small2, dproj, dembed = middle_back(
        back_home, gate_grads_home, hidden, cotangent, mixed, w_output, gain2, bias2,
        proj, embed, routes, experts, cap,
    )
    dq, dk, dv = attention_back(q, k, v, grad_mixed, probs, delta, longest)
    grad_input, dwq, dwk, dwv, small1 = qkv_back(
        tokens, gain1, bias1, grad_hidden, dq, dk, dv, query_weight, w_key, w_value
    )
    output = layer_output(made_home, hidden, gate, routes, experts, cap)
    summed = lax.psum(
        (
            small1[0],
            small1[1],
            dwq,
            dwk,
            dwv,
            dwo,
            small2[0],
            small2[1],
            dproj[:, :space],
            dembed[:experts, :space],
        ),
        ("dp", "expert"),
    )
    return (output, grad_input, *summed, grad_in.astype(F32), grad_out.astype(F32))


def solution(mesh):
    split = P(("dp", "expert"), None)
    in_specs = (
        (split,) * 3 + (P(),) * 10 + (P("expert", None, None), P("expert", None, None), split)
    )
    out_specs = (
        (split, split) + (P(),) * 10 + (P("expert", None, "dp"), P("expert", "dp", None))
    )
    return jax.shard_map(
        on_device, mesh=mesh, in_specs=in_specs, out_specs=out_specs, check_vma=False
    )
```

time: 1040 us -> 730 us (0.70)
  matrix products: 352 us -> 0 us
  Pallas kernels: 0 us -> 241 us
  other arithmetic: 103 us -> 5.71 us
  local copies, waits for them, and re-layouts: 110 us -> 40.8 us
  blocking collectives: 193 us -> 138 us
  waiting for transfers between devices: 236 us -> 262 us
    dot_general x38 -> x0, matrix products: 352 us -> none  [the longest x1 63 us: on_device(): pre = jnp.dot(flat_rows, expert_in[0], preferred_element_type=jnp.float32)]
    pallas_call x0 -> x10, Pallas kernels: none -> 241 us  [the longest x1 59.3 us: expert(): pl.pallas_call(expert_kernel, grid=(slots // rows,), in_specs=[block, blo...]
    all_to_all x2, blocking collectives: 152 us -> 86.1 us  [exchange(): lax.all_to_all(split, 'expert', split_axis=0, concat_axis=0, tiled=True)]
    gather x6 -> x0, local copies, waits for them, and re-layouts: 57.3 us -> none  [the longest x2 22.3 us: on_device(): expert_result = returned[route, slot_rank].astype(jnp.float32)]
    convert_element_type x10 -> x2, other arithmetic: 56 us -> 5.71 us  [the longest x1 2.86 us: on_device(): grad_out.astype(F32)]
    reduce_sum x12 -> x0, other arithmetic: 32.3 us -> none  [the longest x2 24.6 us: forward_block(): total = jnp.sum(weights, -1, keepdims=True)]
    all_to_all x2 -> x4, waiting for transfers between devices: 116 us -> 139 us  [exchange(): lax.all_to_all(split, 'expert', split_axis=0, concat_axis=0, tiled=True)]
    psum x1, blocking collectives: 41.1 us -> 51.6 us  [on_device(): lax.psum((small1[0], small1[1], dwq, dwk, dwv, dwo, small2[0], small2[1],...]
  transfers between devices with their start and end apart: 5 -> 7, of which waited for: 3 -> 3; matrix products, arithmetic and copies ran while one was open for 29% -> 2% of each run, Pallas kernels for 0% -> 14%
where the time goes in v1:
time: 730 us; the launch traced here: 722 us
  waiting for transfers between devices  262 us (36%)
  Pallas kernels  241 us (33%)
  blocking collectives  138 us (19%)
  local copies, waits for them, and re-layouts  40.8 us (6%)
  starting transfers between devices  18.5 us (3%)
  between operations  16.1 us (2%)
    all_to_all x4, waiting for transfers between devices, exchange(): lax.all_to_all(split, 'expert', split_axis=0, concat_axis=0, tiled=True)  139 us
    psum x1, waiting for transfers between devices, on_device(): lax.psum((small1[0], small1[1], dwq, dwk, dwv, dwo, small2[0], small2[1],...  122 us
    all_to_all x2, blocking collectives, exchange(): lax.all_to_all(split, 'expert', split_axis=0, concat_axis=0, tiled=True)  86.1 us
    pallas_call x1, Pallas kernels, expert(): pl.pallas_call(expert_kernel, grid=(slots // rows,), in_specs=[block, blo...  59.3 us
    psum x1, blocking collectives, on_device(): lax.psum((small1[0], small1[1], dwq, dwk, dwv, dwo, small2[0], small2[1],...  51.6 us
    pallas_call x1, Pallas kernels, middle_back(): pl.pallas_call(functools.partial(middle_back_kernel, experts, cap), out_s...  37.9 us
    pallas_call x1, Pallas kernels, attention_back(): pl.pallas_call(functools.partial(attention_back_kernel, rows, longest), g...  30.2 us
    pallas_call x1, Pallas kernels, attention(): pl.pallas_call(functools.partial(attention_kernel, rows, longest), grid=(...  28.8 us
  transfers between devices with their start and end apart: 7, of which 3 were waited for; matrix products, arithmetic and copies ran while one was open for 2% of the time, Pallas kernels for 14%

profile of v1, /device:TPU:0, one launch (start us, length us, event | category | flops | bytes accessed | tf_op | source)
XLA Modules:
  0.0 722.3 jit_solution(7783821667284045855)
XLA Ops:
  9.5 1.3 broadcast_in_dim.34.gain_ref
  10.8 1.3 broadcast_in_dim.35.bias_ref
  12.1 1.0 copy.36
  13.0 1.3 pad.9.embed_ref
  15.1 1.7 copy.37.route_ref
  16.8 1.7 copy.35.seg_ref
  18.5 1.3 copy-done.5
  19.8 1.3 copy-done.6
  21.1 1.3 copy-done.7
  22.4 5.2 qkv.1
  27.6 1.1 copy-done.8
  28.7 1.1 copy-done.9
  29.9 1.1 copy-done.10
  31.0 28.8 %attention.1 = (bf16[1024,768]{1,0:T(8,128)(2,1)}, bf16[12,1024,1024]{2,1,0:T(8,128)(2,1)}) custom-call(bf16[1024,768]{1,0:T(8,128)(2,1)} %copy-done.8, bf16[1024,768]{1,0:T(8,128)(2,1)} %copy-done.9, bf16[1024,768]{1,0:T(8,128)(2,1)} %copy-done.10, s32[1024,1]{1,0:T(8,128)} %copy.35.seg_ref), custom_call_target="tpu_custom_call" | custom-call | flops 12884901888 | bytes 25165824 | tf_op jit(solution)/shard_map/attention/pallas_call | solution.py:199
  59.9 22.1 %middle.1 = (f32[1024,768]{1,0:T(8,128)}, f32[1024,128]{1,0:T(8,128)}, bf16[2048,768]{1,0:T(8,128)(2,1)}, f32[8,8,256]{2,1,0:T(8,128)}) custom-call(bf16[1024,768]{1,0:T(8,128)(2,1)} %get-tuple-element.49.mixed_ref, bf16[1024,768]{1,0:T(8,128)(2,1)} %x_ref.7, bf16[768,768]{1,0:T(8,128)(2,1)} %wo_ref.3, f32[1,768]{1,0:T(1,128)} %broadcast_in_dim.34.gain_ref, ...), custom_call_target="tpu_custom_call" | custom-call | flops 4429185024 | bytes 12582912 | tf_op jit(solution)/shard_map/middle/pallas_call | solution.py:344
  82.0 1.4 slice.24
  83.4 7.3 %all-to-all-start.2 = ((f32[8,1,256]{2,1,0:T(1,128)}), f32[8,1,256]{2,1,0:T(1,128)S(1)}, u32[]{:S(2)}, u32[]{:S(2)}) async-start(f32[8,1,256]{2,1,0:T(1,128)} %slice.24), calls=%async_computation.2 | async-start | bytes 16384 | tf_op jit(solution)/shard_map/all_to_all | solution.py:622
  90.7 1.4 copy-done.3
  92.1 5.1 gather_slots.1
  97.2 76.2 %all_to_all.30 = bf16[8,256,768]{2,1,0:T(8,128)(2,1)} all-to-all(bf16[8,256,768]{2,1,0:T(8,128)(2,1)S(1)} %bitcast.21), channel_id=1, replica_groups=mesh['dp'=4,'expert'=8] {'expert'}, dimensions={0} | all-to-all | bytes 6291456 | tf_op jit(solution)/shard_map/all_to_all | solution.py:622
  173.4 3.7 all-to-all-start
  177.3 69.8 %all-to-all-done = bf16[8,256,768]{2,1,0:T(8,128)(2,1)S(1)} async-done(((bf16[8,256,768]{2,1,0:T(8,128)(2,1)}), bf16[8,256,768]{2,1,0:T(8,128)(2,1)S(1)}, u32[]{:S(2)}, u32[]{:S(2)}) %all-to-all-start) | async-done | bytes 3145760 | tf_op jit(solution)/shard_map/all_to_all | solution.py:622
  247.8 1.0 copy-done.13
  248.8 59.3 %expert.1 = (bf16[2048,768]{1,0:T(8,128)(2,1)}, bf16[2048,768]{1,0:T(8,128)(2,1)}, f32[8,8,256]{2,1,0:T(8,128)}, bf16[2048,3072]{1,0:T(8,128)(2,1)}, bf16[2048,3...) custom-call(bf16[2048,768]{1,0:T(8,128)(2,1)} %bitcast.29, bf16[2048,768]{1,0:T(8,128)(2,1)} %bitcast.31, ...), custom_call_target="tpu_custom_call" | custom-call | flops 38654705664 | bytes 25165824 | tf_op jit(solution)/shard_map/expert/pallas_call | solution.py:406
  308.1 25.9 %expert_grads.1 = (bf16[768,3072]{1,0:T(8,128)(2,1)}, bf16[3072,768]{1,0:T(8,128)(2,1)}) custom-call(bf16[2048,768]{1,0:T(8,128)(2,1)} %bitcast.30, bf16[2048,768]{1,0:T(8,128)(2,1)} %get-tuple-element.73.scaled_ref, bf16[2048,3072]{1,0:T(8,128)(2,1)} %get-tuple-element.74.active_ref, bf16[2048,3072]{1,0:T(8,128)(2,1)} %get-tuple-element.75.grad_pre_ref), custom_call_target="tpu_custom_call" | custom-call | flops 19327352832 | bytes 34603008 | tf_op jit(solution)/shard_map/expert_grads/pallas_call | solution.py:435
  335.6 9.9 %all_to_all.31 = f32[8,1,256]{2,1,0:T(1,128)S(1)} all-to-all(f32[8,1,256]{2,1,0:T(1,128)S(1)} %slice.25), channel_id=1, replica_groups=mesh['dp'=4,'expert'=8] {'expert'}, dimensions={0} | all-to-all | bytes 16384 | tf_op jit(solution)/shard_map/all_to_all | solution.py:622
  345.6 3.6 all-to-all-start.4
  349.2 69.7 %all-to-all-done.4 = bf16[8,256,768]{2,1,0:T(8,128)(2,1)S(1)} async-done(((bf16[8,256,768]{2,1,0:T(8,128)(2,1)}), bf16[8,256,768]{2,1,0:T(8,128)(2,1)S(1)}, u32[]{:S(2)}, u32[]{:S(2)}) %all-to-all-start.4) | async-done | bytes 3145760 | tf_op jit(solution)/shard_map/all_to_all | solution.py:622
  418.9 1.7 copy-done.12
  420.5 3.6 all-to-all-start.3
  424.9 37.9 %middle_back.1 = (f32[1024,768]{1,0:T(8,128)}, bf16[1024,768]{1,0:T(8,128)(2,1)}, f32[6,8,1024]{2,1,0:T(8,128)}, f32[768,768]{1,0:T(8,128)}, f32[8,768]{1,0:T(8,...) custom-call(bf16[2048,768]{1,0:T(8,128)(2,1)} %bitcast.27, f32[8,8,256]{2,1,0:T(8,128)} %broadcast_in_dim.39.gate_grads_ref, ...), custom_call_target="tpu_custom_call" | custom-call | flops 5637144576 | bytes 15728640 | tf_op jit(solution)/shard_map/middle_back/pallas_call | solution.py:526
  462.7 30.2 %attention_back.1 = (bf16[1024,768]{1,0:T(8,128)(2,1)}, bf16[1024,768]{1,0:T(8,128)(2,1)}, bf16[1024,768]{1,0:T(8,128)(2,1)}) custom-call(bf16[1024,768]{1,0:T(8,128)(2,1)} %copy-done.8, bf16[1024,768]{1,0:T(8,128)(2,1)} %copy-done.9, bf16[1024,768]{1,0:T(8,128)(2,1)} %copy-done.10, bf16[1024,768]{1,0:T(8,128)(2,1)} %get-tuple-element.58.do_ref, ...), custom_call_target="tpu_custom_call" | custom-call | flops 25769803776 | bytes 25165824 | tf_op jit(solution)/shard_map/attention_back/pallas_call | solution.py:259
  492.9 16.1 %qkv_back.1 = (f32[1024,768]{1,0:T(8,128)}, f32[768,768]{1,0:T(8,128)}, f32[768,768]{1,0:T(8,128)}, f32[768,768]{1,0:T(8,128)}, f32[8,768]{1,0:T(8,128)}) custom-call(bf16[1024,768]{1,0:T(8,128)(2,1)} %x_ref.7, f32[1,768]{1,0:T(1,128)} %copy-done.1, f32[1,768]{1,0:T(1,128)} %copy-done.2, f32[1024,768]{1,0:T(8,128)} %get-tuple-element.57.grad_hidden_ref, ...), custom_call_target="tpu_custom_call" | custom-call | flops 7247757312 | bytes 15728640 | tf_op jit(solution)/shard_map/qkv_back/pallas_call | solution.py:576
  509.1 1.3 slice.31
  510.4 0.8 slice_reduce_fusion
  511.3 51.6 %all-reduce.2 = (f32[768]{0:T(1024)}, f32[768]{0:T(1024)}, f32[768]{0:T(1024)}, f32[768]{0:T(1024)}, f32[768,16]{1,0:T(8,128)}, /*index=5*/f32[8,16]{1,0:T(8,128)}) all-reduce(f32[768]{0:T(1024)S(1)} %get-tuple-element.120, f32[768]{0:T(1024)S(1)} %get-tuple-element.121, ...), channel_id=1, replica_groups=mesh['dp'=4,'expert'=8] {'dp','expert'}, use_global_device_ids=true, to_apply=%region_0.1 | all-reduce | flops 15488 | bytes 123904 | tf_op jit(solution)/shard_map/psum | solution.py:693
  562.9 1.8 copy.40
  564.7 1.6 copy-done.11
  566.3 10.4 %layer_output.1 = bf16[1024,768]{1,0:T(8,128)(2,1)} custom-call(bf16[2048,768]{1,0:T(8,128)(2,1)} %bitcast.26, f32[1024,768]{1,0:T(8,128)} %get-tuple-element.53.hidden_ref, f32[1024,128]{1,0:T(8,128)} %get-tuple-element.54.gate_ref, s32[1024,1]{1,0:T(8,128)} %copy.37.route_ref), custom_call_target="tpu_custom_call" | custom-call | flops 3221225472 | bytes 7864320 | tf_op jit(solution)/shard_map/layer_output/pallas_call | solution.py:610
  576.7 2.9 convert_element_type.10
  579.6 2.9 convert_element_type.11
  582.5 122.1 %all-reduce.6.cloned.1.call-done = (f32[768,768]{1,0:T(8,128)}, f32[768,768]{1,0:T(8,128)}, f32[768,768]{1,0:T(8,128)}, f32[768,768]{1,0:T(8,128)}) async-done(((f32[768,768]{1,0:T(8,128)}, f32[768,768]{1,0:T(8,128)}, f32[768,768]{1,0:T(8,128)}, f32[768,768]{1,0:T(8,128)}), (f32[768,768]{1,0:T(8,128)}, f32[768,768]{1,0:T(8,128)}, f32[768,768]{1,0:T(8,128)}, ...) | async-done | bytes 9437200 | tf_op jit(solution)/shard_map/psum | solution.py:693
  704.6 3.4 copy.51
  708.0 1.4 copy.52
  709.4 1.1 copy-done.15
  710.5 1.4 copy.53
  711.9 1.1 copy-done.14
  713.0 1.4 copy.54
  (42 shorter events, 5.5 us)
Async XLA Ops:
  8.0 10.5 %copy-start.4 = (bf16[1024,768]{1,0:T(8,128)(2,1)S(1)}, bf16[1024,768]{1,0:T(8,128)(2,1)}, u32[]{:S(2)}) copy-start(bf16[1024,768]{1,0:T(8,128)(2,1)} %x_ref.7) | copy-start | bytes 4718596
  8.8 18.7 %copy-start.1 = (f32[1,768]{1,0:T(1,128)}, f32[1,768]{1,0:T(1,128)S(1)}, u32[]{:S(2)}) copy-start(f32[1,768]{1,0:T(1,128)S(1)} %broadcast_in_dim.32.gain_ref) | copy-start | bytes 9220
  9.5 18.0 %copy-start.2 = (f32[1,768]{1,0:T(1,128)}, f32[1,768]{1,0:T(1,128)S(1)}, u32[]{:S(2)}) copy-start(f32[1,768]{1,0:T(1,128)S(1)} %broadcast_in_dim.33.bias_ref) | copy-start | bytes 9220
  18.5 1.3 copy-start.5
  19.8 1.3 copy-start.6
  21.1 1.3 copy-start.7
  27.6 1.1 copy-start.8
  28.7 1.1 copy-start.9
  29.9 1.1 copy-start.10
  59.9 30.9 %copy-start = (s32[1024,1]{0,1:T(1,128)S(1)}, s32[1024,1]{0,1:T(1,128)}, u32[]{:S(2)}) copy-start(s32[1024,1]{0,1:T(1,128)} %param.18) | copy-start | bytes 12292
  83.4 13.8 %all-to-all-start.2 = ((f32[8,1,256]{2,1,0:T(1,128)}), f32[8,1,256]{2,1,0:T(1,128)S(1)}, u32[]{:S(2)}, u32[]{:S(2)}) async-start(f32[8,1,256]{2,1,0:T(1,128)} %slice.24), calls=%async_computation.2 | async-start | bytes 16384 | tf_op jit(solution)/shard_map/all_to_all | solution.py:622
  90.7 1.4 copy-start.3
  173.4 73.7 %all-to-all-start = ((bf16[8,256,768]{2,1,0:T(8,128)(2,1)}), bf16[8,256,768]{2,1,0:T(8,128)(2,1)S(1)}, u32[]{:S(2)}, u32[]{:S(2)}) async-start(bf16[8,256,768]{2,1,0:T(8,128)(2,1)} %bitcast.28), calls=%async_computation | async-start | bytes 6291456 | tf_op jit(solution)/shard_map/all_to_all | solution.py:622
  177.1 399.7 %reduce-scatter.3.cloned.1.call-start = ((), (), s32[]{:S(2)}) async-start(), calls=%async_computation.8 | async-start | bytes 5898240 | tf_op jit(solution)/shard_map/reduce_scatter | solution.py:682
  247.1 1.7 copy-start.13
  334.0 245.6 %reduce-scatter.5.cloned.1.call-start = ((), (), s32[]{:S(2)}) async-start(), calls=%async_computation.9 | async-start | bytes 5898240 | tf_op jit(solution)/shard_map/reduce_scatter | solution.py:683
  345.6 73.3 %all-to-all-start.4 = ((bf16[8,256,768]{2,1,0:T(8,128)(2,1)}), bf16[8,256,768]{2,1,0:T(8,128)(2,1)S(1)}, u32[]{:S(2)}, u32[]{:S(2)}) async-start(bf16[8,256,768]{2,1,0:T(8,128)(2,1)} %bitcast.10), calls=%async_computation.4 | async-start | bytes 6291456 | tf_op jit(solution)/shard_map/all_to_all | solution.py:622
  418.9 1.7 copy-start.12
  420.5 144.1 %all-to-all-start.3 = ((bf16[8,256,768]{2,1,0:T(8,128)(2,1)}), bf16[8,256,768]{2,1,0:T(8,128)(2,1)S(1)}, u32[]{:S(2)}, u32[]{:S(2)}) async-start(bf16[8,256,768]{2,1,0:T(8,128)(2,1)} %bitcast.8), calls=%async_computation.3 | async-start | bytes 6291456 | tf_op jit(solution)/shard_map/all_to_all | solution.py:622
  424.2 280.4 %all-reduce.6.cloned.1.call-start = ((), (), s32[]{:S(2)}) async-start(), calls=%async_computation.10 | async-start | bytes 18874368 | tf_op jit(solution)/shard_map/psum | solution.py:693
  509.1 2.2 copy-start.17
  564.7 1.6 copy-start.11
  704.6 3.4 copy-start.16
  708.0 2.5 copy-start.15
  710.5 2.5 copy-start.14
Sparse Core Ops, SparseCore 0:
  334.2 46.8 reduce-scatter.2
  383.6 47.8 reduce-scatter.4
Sparse Core Ops, SparseCore 1:
  509.2 195.3 all-reduce.5

commit v2 on v1

--- a/solution.py
+++ b/solution.py
@@ -85,31 +85,20 @@
     return jnp.sum(jnp.where(eye, row, 0.0), 1, keepdims=True)
 
 
-def gather_kernel(experts, cap, route_ref, x_ref, out_ref, slot_ref):
-    step = pl.program_id(0)
-
-    @pl.when(step == 0)
-    def _():
-        slot = slot_row_of(route_ref[...], experts, cap)
-        slot_ref[...] = jnp.broadcast_to(slot, slot_ref.shape)
-
-    rows = out_ref.shape[0]
+def gather_kernel(experts, cap, route_ref, x_ref, *out_refs):
+    slot = slot_row_of(route_ref[...], experts, cap)
     tokens = x_ref.shape[0]
-    pick = one_hot(iota((rows, tokens), 0) + step * rows == slot_ref[0:1, :])
-    out_ref[...] = mm(pick, x_ref[...]).astype(BF16)
+    for e, out_ref in enumerate(out_refs):
+        pick = one_hot(iota((cap, tokens), 0) + e * cap == slot)
+        out_ref[...] = mm(pick, x_ref[...]).astype(BF16)
 
 
 def gather_slots(route_row, x, experts, cap):
     tokens, width = x.shape
     slots = experts * cap
-    rows = 256
     return pl.pallas_call(
         functools.partial(gather_kernel, experts, cap),
-        grid=(slots // rows,),
-        in_specs=[spec_all((1, tokens)), spec_all((tokens, width))],
-        out_specs=pl.BlockSpec((rows, width), lambda i: (i, 0)),
-        out_shape=jax.ShapeDtypeStruct((slots, width), BF16),
-        scratch_shapes=[pltpu.VMEM((8, tokens), jnp.int32)],
+        out_shape=[jax.ShapeDtypeStruct((cap, width), BF16)] * experts,
         compiler_params=params(32),
         cost_estimate=cost(2 * slots * tokens * width, 2 * width * (tokens + slots)),
         name="gather_slots",
@@ -299,7 +288,7 @@
 
 def middle_kernel(
     experts, cap, mixed_ref, x_ref, wo_ref, gain_ref, bias_ref, proj_ref, embed_ref,
-    route_ref, route_row_ref, hidden_ref, gate_ref, slots_ref, gates_ref, kept,
+    route_ref, place_row_ref, hidden_ref, gate_ref, slots_ref, gates_ref, kept,
 ):
     tokens, width = x_ref.shape
     rows = 256
@@ -322,32 +311,30 @@
         return carry
 
     lax.fori_loop(0, tokens // rows, row_block, 0)
-    slot = slot_row_of(route_row_ref[...], experts, cap)
-
-    def slot_block(i, carry):
-        at = pl.ds(pl.multiple_of(i * rows, rows), rows)
-        pick = one_hot(iota((rows, tokens), 0) + i * rows == slot)
+    slot = slot_row_of(place_row_ref[...], experts, cap)
+
+    def slot_block(e, carry):
+        pick = one_hot(iota((cap, tokens), 0) + e * cap == slot)
         got = mm(pick, kept[...])
-        slots_ref[at, :] = got[:, 0:width].astype(BF16)
-        gates_ref[pl.ds(i, 1), :, :] = jnp.broadcast_to(
-            as_row(jnp.sum(got[:, width : width + 128], 1, keepdims=True)), (8, rows)
-        )[None]
+        slots_ref[e] = got[:, 0:width].astype(BF16)
+        gates = as_row(jnp.sum(got[:, width : width + 128], 1, keepdims=True))
+        gates_ref[e] = jnp.broadcast_to(gates, (8, cap))
         return carry
 
-    lax.fori_loop(0, experts * cap // rows, slot_block, 0)
-
-
-def middle(mixed, x, wo, gain, bias, proj, embed, route, route_row, experts, cap):
+    lax.fori_loop(0, experts, slot_block, 0)
+
+
+def middle(mixed, x, wo, gain, bias, proj, embed, route, place_row, experts, cap):
     tokens, width = x.shape
     slots = experts * cap
-    args = (mixed, x, wo, gain, bias, proj, embed, route, route_row)
+    args = (mixed, x, wo, gain, bias, proj, embed, route, place_row)
     return pl.pallas_call(
         functools.partial(middle_kernel, experts, cap),
         out_shape=[
             jax.ShapeDtypeStruct((tokens, width), F32),
             jax.ShapeDtypeStruct((tokens, 128), F32),
-            jax.ShapeDtypeStruct((slots, width), BF16),
-            jax.ShapeDtypeStruct((slots // 256, 8, 256), F32),
+            jax.ShapeDtypeStruct((experts, cap, width), BF16),
+            jax.ShapeDtypeStruct((experts, 8, cap), F32),
         ],
         scratch_shapes=[pltpu.VMEM((tokens, width + 128), BF16)],
         compiler_params=params(),
@@ -369,97 +356,275 @@
     return phi_sum, pre * bell * 0.3989422804014327
 
 
-def expert_kernel(
-    x_ref, up_ref, gate_ref, w_in_ref, w_out_ref,
-    made_ref, back_ref, gate_grad_ref, active_ref, grad_pre_ref, scaled_ref,
-):
-    hidden = w_in_ref.shape[1]
+def expert_kernel(experts, x_axis, *refs):
+    x_ref, gates_ref, w_in_ref, w_out_ref = refs[:4]
+    up_refs = refs[4 : 4 + experts]
+    back_ref, gate_grads_ref = refs[4 + experts : 6 + experts]
+    rest = refs[6 + experts :]
+    made_refs = rest[:experts]
+    din_refs = rest[experts : experts + x_axis]
+    dout_refs = rest[experts + x_axis : experts + 2 * x_axis]
+    (
+        x_here, up_here, gates_here, back_here, gate_grads_here, made_here,
+        active, grad_pre, w_in, w_out, din_got, dout_got,
+        load_sem, x_send, x_recv, g_send, g_recv, b_send, b_recv, gg_send, gg_recv,
+        d_send, d_recv, store_sem,
+    ) = rest[experts + 2 * x_axis :]
+    cap, width = x_here.shape[1:]
+    hidden = w_in.shape[1]
+    me = lax.axis_index("expert")
+    dp = lax.axis_index("dp")
+    core = lax.rem(dp, 2)
+    mesh_ids = pl.DeviceIdType.MESH
+
+    barrier = pltpu.get_barrier_semaphore()
+
+    def greet(s, carry):
+        pl.semaphore_signal(
+            barrier, inc=1, device_id={"expert": lax.rem(me + s, experts)}, device_id_type=mesh_ids
+        )
+        return carry
+
+    lax.fori_loop(1, experts, greet, 0)
+    pl.semaphore_signal(
+        barrier, inc=1, device_id={"dp": dp + 1 - 2 * core}, device_id_type=mesh_ids
+    )
+    pl.semaphore_wait(barrier, experts)
+
+    def out_copy(s):
+        to = {"expert": lax.rem(me + s, experts)}
+        return (
+            pltpu.make_async_remote_copy(
+                x_ref.at[s], x_here.at[s], x_send.at[s], x_recv.at[s], to, mesh_ids
+            ),
+            pltpu.make_async_remote_copy(
+                gates_ref.at[s], gates_here.at[s], g_send.at[s], g_recv.at[s], to, mesh_ids
+            ),
+        )
+
+    def home_copy(s):
+        to = {"expert": lax.rem(me + experts - s, experts)}
+        return (
+            pltpu.make_async_remote_copy(
+                back_here.at[s], back_ref.at[s], b_send.at[s], b_recv.at[s], to, mesh_ids
+            ),
+            pltpu.make_async_remote_copy(
+                gate_grads_here.at[s], gate_grads_ref.at[s], gg_send.at[s], gg_recv.at[s], to, mesh_ids
+            ),
+        )
+
+    def send_out(s, carry):
+        for copy in out_copy(s):
+            copy.start()
+        return carry
+
+    lax.fori_loop(1, experts, send_out, 0)
+    loads = [
+        pltpu.make_async_copy(x_ref.at[0], x_here.at[0], load_sem.at[0]),
+        pltpu.make_async_copy(gates_ref.at[0], gates_here.at[0], load_sem.at[1]),
+        pltpu.make_async_copy(w_in_ref, w_in, load_sem.at[2]),
+        pltpu.make_async_copy(w_out_ref, w_out, load_sem.at[3]),
+    ]
+    for s, up_ref in enumerate(up_refs):
+        loads.append(pltpu.make_async_copy(up_ref, up_here.at[s], load_sem.at[4 + s]))
+    for load in loads:
+        load.start()
+    for load in loads:
+        load.wait()
+
     step = 512
-    gate = as_col(gate_ref[0, 0:1, :])
-    up = up_ref[...].astype(F32)
-    scaled = (up * gate).astype(BF16)
-    scaled_ref[...] = scaled
-    x = x_ref[...]
-    for at in range(0, hidden, step):
-        part = slice(at, at + step)
-        pre = mm(x, w_in_ref[:, part])
-        grad_active = mm_cols(scaled, w_out_ref[part, :])
-        phi_sum, slope = gelu_parts(pre)
-        active_ref[:, part] = (pre * phi_sum).astype(BF16)
-        grad_pre_ref[:, part] = (grad_active * (phi_sum + slope)).astype(BF16)
-    made = mm(active_ref[...], w_out_ref[...]).astype(BF16)
-    made_ref[...] = made
-    gate_grad = jnp.sum(up * made.astype(F32), 1, keepdims=True)
-    gate_grad_ref[...] = jnp.broadcast_to(as_row(gate_grad), (8, x.shape[0]))[None]
-    back_ref[...] = mm_cols(grad_pre_ref[...], w_in_ref[...]).astype(BF16)
-
-
-def expert(x, up, gates, w_in, w_out):
-    slots, width = x.shape
+
+    def chunk(s, carry):
+        @pl.when(s > 0)
+        def _():
+            for copy in out_copy(s):
+                copy.wait_recv()
+
+        at_rows = pl.ds(pl.multiple_of(s * cap, cap), cap)
+        gate = as_col(gates_here[s][0:1, :])
+        up = up_here[s].astype(F32)
+        scaled = (up * gate).astype(BF16)
+        x = x_here[s]
+        for at in range(0, hidden, step):
+            part = slice(at, at + step)
+            pre = mm(x, w_in[:, part])
+            grad_active = mm_cols(scaled, w_out[part, :])
+            phi_sum, slope = gelu_parts(pre)
+            active[at_rows, part] = (pre * phi_sum).astype(BF16)
+            grad_pre[at_rows, part] = (grad_active * (phi_sum + slope)).astype(BF16)
+        made = mm(active[at_rows, :], w_out[...]).astype(BF16)
+        made_here[s] = made
+        gate_grad = jnp.sum(up * made.astype(F32), 1, keepdims=True)
+        gate_grads_here[s] = jnp.broadcast_to(as_row(gate_grad), (8, cap))
+        up_here[s] = scaled
+        back_here[s] = mm_cols(grad_pre[at_rows, :], w_in[...]).astype(BF16)
+
+        @pl.when(s > 0)
+        def _():
+            for copy in home_copy(s):
+                copy.start()
+
+        return carry
+
+    lax.fori_loop(0, experts, chunk, 0)
+    stores = [
+        pltpu.make_async_copy(back_here.at[0], back_ref.at[0], store_sem.at[0]),
+        pltpu.make_async_copy(gate_grads_here.at[0], gate_grads_ref.at[0], store_sem.at[1]),
+    ]
+    for s, made_ref in enumerate(made_refs):
+        stores.append(pltpu.make_async_copy(made_here.at[s], made_ref, store_sem.at[2 + s]))
+    for store in stores:
+        store.start()
+
+    block = hidden // (2 * x_axis)
+    slots = experts * cap
+    other = {"dp": dp + 1 - 2 * core}
+    x_all = x_here.reshape(slots, width)
+    up_all = up_here.reshape(slots, width)
+
+    def block_start(k, for_core):
+        x_at = lax.rem(dp // 2 + k, x_axis)
+        return pl.multiple_of((2 * x_at + for_core) * block, 128)
+
+    def din_out(k):
+        return w_in.at[:, k * block : (k + 1) * block]
+
+    def dout_out(k):
+        return w_out.at[k * block : (k + 1) * block]
+
+    def core_copies(k):
+        return (
+            pltpu.make_async_remote_copy(
+                din_out(k), din_got.at[k], d_send.at[k], d_recv.at[k], other, mesh_ids
+            ),
+            pltpu.make_async_remote_copy(
+                dout_out(k),
+                dout_got.at[k],
+                d_send.at[x_axis + k],
+                d_recv.at[x_axis + k],
+                other,
+                mesh_ids,
+            ),
+        )
+
+    tile = 256 if block % 256 == 0 else 128
+
+    def weight_grads(k, for_core, out, got):
+        start = block_start(k, for_core)
+        columns = slice(out * block, (out + 1) * block)
+        for at in range(0, width, tile):
+            part = slice(at, at + tile)
+            value = mm_rows(x_all[:, part], grad_pre[:, pl.ds(start, block)])
+            if got is not None:
+                value = value + din_got[got, part, :].astype(F32)
+            w_in[part, columns] = value.astype(BF16)
+        for at in range(0, block, tile):
+            value = mm_rows(active[:, pl.ds(pl.multiple_of(start + at, 128), tile)], up_all[...])
+            if got is not None:
+                value = value + dout_got[got, at : at + tile, :].astype(F32)
+            w_out[out * block + at : out * block + at + tile, :] = value.astype(BF16)
+
+    for k in range(x_axis):
+        weight_grads(k, 1 - core, k, None)
+        for copy in core_copies(k):
+            copy.start()
+    for k in range(x_axis):
+        for copy in core_copies(k):
+            copy.wait_recv()
+        weight_grads(k, core, x_axis + k, k)
+        for i, (src, ref) in enumerate(
+            ((din_out(x_axis + k), din_refs[k]), (dout_out(x_axis + k), dout_refs[k]))
+        ):
+            store = pltpu.make_async_copy(src, ref, store_sem.at[2 + experts + 2 * k + i])
+            store.start()
+            stores.append(store)
+    for store in stores:
+        store.wait()
+    for k in range(x_axis):
+        for copy in core_copies(k):
+            copy.wait_send()
+
+    def finish(s, carry):
+        for copy in out_copy(s):
+            copy.wait_send()
+        for copy in home_copy(s):
+            copy.wait()
+        return carry
+
+    lax.fori_loop(1, experts, finish, 0)
+
+
+def expert(x, gates, up, w_in, w_out, dp_size):
+    experts, cap, width = x.shape
     hidden = w_in.shape[1]
-    rows = 256
-    block = pl.BlockSpec((rows, width), lambda i: (i, 0))
-    wide = pl.BlockSpec((rows, hidden), lambda i: (i, 0))
-    line = pl.BlockSpec((1, 8, rows), lambda i: (i, 0, 0))
-    made = jax.ShapeDtypeStruct((slots, width), BF16)
-    made_wide = jax.ShapeDtypeStruct((slots, hidden), BF16)
-    return pl.pallas_call(
-        expert_kernel,
-        grid=(slots // rows,),
-        in_specs=[block, block, line, spec_all((width, hidden)), spec_all((hidden, width))],
-        out_specs=[block, block, line, wide, wide, block],
-        out_shape=[
-            made,
-            made,
-            jax.ShapeDtypeStruct((slots // rows, 8, rows), F32),
-            made_wide,
-            made_wide,
-            made,
-        ],
-        compiler_params=params(),
-        cost_estimate=cost(8 * slots * width * hidden, 4 * slots * hidden),
+    slots = experts * cap
+    x_axis = dp_size // 2
+    block = hidden // dp_size
+    anywhere = pl.BlockSpec(memory_space=pl.ANY)
+    rows = jax.ShapeDtypeStruct((cap, width), BF16)
+    out_shape = (
+        [
+            jax.ShapeDtypeStruct((experts, cap, width), BF16),
+            jax.ShapeDtypeStruct((experts, 8, cap), F32),
+        ]
+        + [rows] * experts
+        + [jax.ShapeDtypeStruct((width, block), BF16)] * x_axis
+        + [jax.ShapeDtypeStruct((block, width), BF16)] * x_axis
+    )
+    chunks = pltpu.VMEM((experts, cap, width), BF16)
+    lines = pltpu.VMEM((experts, 8, cap), F32)
+    sems = pltpu.SemaphoreType.DMA
+    out = pl.pallas_call(
+        functools.partial(expert_kernel, experts, x_axis),
+        in_specs=[anywhere] * (4 + experts),
+        out_specs=[anywhere] * len(out_shape),
+        out_shape=out_shape,
+        scratch_shapes=[
+            chunks,
+            chunks,
+            lines,
+            chunks,
+            lines,
+            chunks,
+            pltpu.VMEM((slots, hidden), BF16),
+            pltpu.VMEM((slots, hidden), BF16),
+            pltpu.VMEM((width, hidden), BF16),
+            pltpu.VMEM((hidden, width), BF16),
+            pltpu.VMEM((x_axis, width, block), BF16),
+            pltpu.VMEM((x_axis, block, width), BF16),
+            sems((4 + experts,)),
+        ]
+        + [sems((experts,))] * 8
+        + [sems((2 * x_axis,))] * 2
+        + [sems((2 + experts + 2 * x_axis,))],
+        compiler_params=pltpu.CompilerParams(
+            vmem_limit_bytes=63 * MIB, collective_id=0, has_side_effects=True
+        ),
+        cost_estimate=cost(12 * slots * width * hidden, 8 * width * hidden),
         name="expert",
-    )(x, up, gates, w_in, w_out)
-
-
-def expert_grads_kernel(x_ref, scaled_ref, active_ref, grad_pre_ref, din_ref, dout_ref):
-    din_ref[...] = mm_rows(x_ref[...], grad_pre_ref[...]).astype(BF16)
-    dout_ref[...] = mm_rows(active_ref[...], scaled_ref[...]).astype(BF16)
-
-
-def expert_grads(x, scaled, active, grad_pre):
-    slots, width = x.shape
-    hidden = active.shape[1]
-    step = 512
-    tall = pl.BlockSpec((slots, step), lambda i: (0, i))
-    return pl.pallas_call(
-        expert_grads_kernel,
-        grid=(hidden // step,),
-        in_specs=[spec_all((slots, width)), spec_all((slots, width)), tall, tall],
-        out_specs=[
-            pl.BlockSpec((width, step), lambda i: (0, i)),
-            pl.BlockSpec((step, width), lambda i: (i, 0)),
-        ],
-        out_shape=[
-            jax.ShapeDtypeStruct((width, hidden), BF16),
-            jax.ShapeDtypeStruct((hidden, width), BF16),
-        ],
-        compiler_params=params(),
-        cost_estimate=cost(4 * slots * width * hidden, 4 * slots * hidden + 4 * width * hidden),
-        name="expert_grads",
-    )(x, scaled, active, grad_pre)
+    )(x, gates, w_in, w_out, *up)
+    back, gate_grads = out[:2]
+    made = out[2 : 2 + experts]
+    din = out[2 + experts : 2 + experts + x_axis]
+    dout = out[2 + experts + x_axis :]
+    return back, gate_grads, made, din, dout
+
+
+def store_tiles(out_ref, value):
+    for tile in range(out_ref.shape[0]):
+        out_ref[tile] = value[:, tile * 128 : (tile + 1) * 128].astype(BF16)
 
 
 def middle_back_kernel(
     experts, cap, back_ref, gate_grads_ref, hidden_ref, cot_ref, mixed_ref, wo_ref,
-    gain_ref, bias_ref, proj_ref, embed_ref, route_ref,
-    grad_hidden_ref, grad_mixed_ref, delta_ref, dwo_ref, small_ref, dproj_ref, dembed_ref,
-    slot_ref, low_ref,
+    gain_ref, bias_ref, proj_ref, embed_ref, route_ref, place_ref,
+    grad_hidden_ref, grad_mixed_ref, delta_ref, dwo_ref, small_ref,
+    slot_ref, low_ref, dproj_ref, dembed_ref,
 ):
     tokens, width = hidden_ref.shape
     slots = back_ref.shape[0]
     rows = 256
-    slot_ref[...] = jnp.broadcast_to(slot_col_of(route_ref[...], experts, cap), slot_ref.shape)
+    slot_ref[...] = jnp.broadcast_to(slot_col_of(place_ref[...], experts, cap), slot_ref.shape)
     small_ref[...] = jnp.zeros_like(small_ref)
     dproj_ref[...] = jnp.zeros_like(dproj_ref)
     dembed_ref[...] = jnp.zeros_like(dembed_ref)
@@ -476,9 +641,9 @@
         pick = iota((rows, slots), 1) == place
         grad = mm(one_hot(pick), back_ref[...])
         gate_grad = jnp.zeros((rows, 1), F32)
-        for e in range(slots // rows):
+        for e in range(experts):
             gate_grad = gate_grad + jnp.sum(
-                jnp.where(pick[:, e * rows : (e + 1) * rows], gate_grads_ref[e, 0:1, :], 0.0),
+                jnp.where(pick[:, e * cap : (e + 1) * cap], gate_grads_ref[e, 0:1, :], 0.0),
                 1,
                 keepdims=True,
             )
@@ -493,7 +658,7 @@
         grad_unit = jnp.dot(grad_logits, table, precision=EXACT, preferred_element_type=F32)
         dembed_ref[...] += mm_rows(grad_logits, low_unit, EXACT)
         grad_low = clipped_back(grad_unit, low, low_scale, low_squares)
-        dproj_ref[...] += mm_rows(normed, grad_low, EXACT)
+        dproj_ref[...] += mm_rows(grad_low, normed, EXACT)
         grad = grad + mm_cols(grad_low, proj, EXACT)
         small_ref[0:1, :] += jnp.sum(grad * unit, 0, keepdims=True)
         small_ref[1:2, :] += jnp.sum(grad, 0, keepdims=True)
@@ -513,28 +678,36 @@
     embed = embed_ref[...]
     squares = jnp.sum(embed * embed, -1, keepdims=True)
     table_scale = lax.rsqrt(jnp.maximum(squares, 1.0))
-    dembed_ref[...] = clipped_back(dembed_ref[...], embed, table_scale, squares)
-    dwo_ref[...] = mm_rows(mixed_ref[...], low_ref[...])
+    dembed = clipped_back(dembed_ref[...], embed, table_scale, squares)
+    lines_proj = small_ref.shape[0] - 8 - max(8, experts)
+    small_ref[8 : 8 + lines_proj, :] = dproj_ref[0:lines_proj, :]
+    small_ref[8 + lines_proj :, 0:128] = dembed[0 : max(8, experts), :]
+    store_tiles(dwo_ref, mm_rows(mixed_ref[...], low_ref[...]))
 
 
 def middle_back(
-    back, gate_grads, hidden, cot, mixed, wo, gain, bias, proj, embed, route, experts, cap
+    back, gate_grads, hidden, cot, mixed, wo, gain, bias, proj, embed, route, place, space,
+    experts, cap,
 ):
     tokens, width = hidden.shape
-    slots = back.shape[0]
-    args = (back, gate_grads, hidden, cot, mixed, wo, gain, bias, proj, embed, route)
+    slots = experts * cap
+    back = back.reshape(slots, width)
+    args = (back, gate_grads, hidden, cot, mixed, wo, gain, bias, proj, embed, route, place)
     return pl.pallas_call(
         functools.partial(middle_back_kernel, experts, cap),
         out_shape=[
             jax.ShapeDtypeStruct((tokens, width), F32),
             jax.ShapeDtypeStruct((tokens, width), BF16),
             jax.ShapeDtypeStruct((width // PAIR, 8, tokens), F32),
-            jax.ShapeDtypeStruct((width, width), F32),
-            jax.ShapeDtypeStruct((8, width), F32),
-            jax.ShapeDtypeStruct(proj.shape, F32),
-            jax.ShapeDtypeStruct(embed.shape, F32),
+            jax.ShapeDtypeStruct((width // 128, width, 128), BF16),
+            jax.ShapeDtypeStruct((8 + space + max(8, experts), width), F32),
         ],
-        scratch_shapes=[pltpu.VMEM((tokens, 128), jnp.int32), pltpu.VMEM((tokens, width), BF16)],
+        scratch_shapes=[
+            pltpu.VMEM((tokens, 128), jnp.int32),
+            pltpu.VMEM((tokens, width), BF16),
+            pltpu.VMEM((128, width), F32),
+            pltpu.VMEM((128, 128), F32),
+        ],
         compiler_params=params(),
         cost_estimate=cost(2 * tokens * width * (2 * width + slots), 20 * tokens * width),
         name="middle_back",
@@ -565,14 +738,14 @@
 
     lax.fori_loop(0, tokens // rows, row_block, 0)
     low = low_ref[...]
-    dwq_ref[...] = mm_rows(low, dq_ref[...])
-    dwk_ref[...] = mm_rows(low, dk_ref[...])
-    dwv_ref[...] = mm_rows(low, dv_ref[...])
+    store_tiles(dwq_ref, mm_rows(low, dq_ref[...]))
+    store_tiles(dwk_ref, mm_rows(low, dk_ref[...]))
+    store_tiles(dwv_ref, mm_rows(low, dv_ref[...]))
 
 
 def qkv_back(x, gain, bias, grad_hidden, dq, dk, dv, wq, wk, wv):
     tokens, width = x.shape
-    square = jax.ShapeDtypeStruct((width, width), F32)
+    square = jax.ShapeDtypeStruct((width // 128, width, 128), BF16)
     return pl.pallas_call(
         qkv_back_kernel,
         out_shape=[
@@ -589,48 +762,338 @@
     )(x, gain, bias, grad_hidden, dq, dk, dv, wq, wk, wv)
 
 
-def output_kernel(experts, cap, made_ref, hidden_ref, gate_ref, route_ref, out_ref, slot_ref):
+def add_rows(rows, out_ref, out_at, terms):
+    step = 48
+
+    def body(i, carry):
+        at = i * step
+        total = None
+        for ref, start in terms:
+            value = ref[pl.ds(pl.multiple_of(start + at, 16), step), :].astype(F32)
+            total = value if total is None else total + value
+        out_ref[pl.ds(pl.multiple_of(out_at + at, 16), step), :] = total.astype(out_ref.dtype)
+        return carry
+
+    lax.fori_loop(0, rows // step, body, 0)
+
+
+def reduce_kernel(x_axis, experts, n, *refs):
+    grads = refs[:n]
+    small_ref = refs[n]
+    out_ref, small_out = refs[n + 1 : n + 3]
+    (
+        core_got, core_sum, plane_got, plane_sum, line_got,
+        small_got, core_send, core_recv, plane_send, plane_recv, line_send, line_recv,
+        line_back_send, line_back_recv, plane_back_send, plane_back_recv,
+        core_back_send, core_back_recv, small_send, small_recv,
+    ) = refs[n + 3 :]
+    dp = lax.axis_index("dp")
+    me = lax.axis_index("expert")
+    core = lax.rem(dp, 2)
+    x_at = dp // 2
+    low = lax.rem(me, 2)
+    high = me // 2
+    planes, lines = 2 * x_axis, experts // 2
+    mesh_ids = pl.DeviceIdType.MESH
+    rows = grads[0].shape[0]
+    half = rows // 2
+    quarter = half // planes
+    piece = quarter // lines
+    plane_at = x_at * 2 + low
+
+    other_core = {"dp": dp + 1 - 2 * core}
+
+    def plane_peer(j):
+        at = lax.rem(plane_at + j, planes)
+        return at, (2 * (at // 2) + core, 2 * high + lax.rem(at, 2))
+
+    def line_peer(j):
+        at = lax.rem(high + j, lines)
+        return at, {"expert": 2 * at + low}
+
+    barrier = pltpu.get_barrier_semaphore()
+    pl.semaphore_signal(barrier, inc=1, device_id=other_core, device_id_type=mesh_ids)
+    for j in range(1, planes):
+        pl.semaphore_signal(barrier, inc=1, device_id=plane_peer(j)[1], device_id_type=mesh_ids)
+    for j in range(1, lines):
+        pl.semaphore_signal(barrier, inc=1, device_id=line_peer(j)[1], device_id_type=mesh_ids)
+    pl.semaphore_wait(barrier, planes + lines - 1)
+
+    def remote(src, dst, send, recv, to):
+        return pltpu.make_async_remote_copy(src, dst, send, recv, to, mesh_ids)
+
+    def rows_at(start, size):
+        return pl.ds(pl.multiple_of(start, 16), size)
+
+    def core_copy(c):
+        src = grads[c].at[rows_at((1 - core) * half, half)]
+        return [remote(src, core_got.at[c], core_send.at[c], core_recv.at[c], other_core)]
+
+    def plane_copies(c):
+        made = []
+        for j in range(1, planes):
+            at, to = plane_peer(j)
+            src = core_sum.at[c, rows_at(at * quarter, quarter)]
+            made.append(
+                remote(src, plane_got.at[c, j], plane_send.at[c, j], plane_recv.at[c, j], to)
+            )
+        return made
+
+    def line_copies(c):
+        made = []
+        for j in range(1, lines):
+            at, to = line_peer(j)
+            src = plane_sum.at[c, rows_at(at * piece, piece)]
+            made.append(remote(src, line_got.at[c, j], line_send.at[c, j], line_recv.at[c, j], to))
+        return made
+
+    base = core * half + plane_at * quarter
+
+    def line_back(c):
+        at = rows_at(base + high * piece, piece)
+        made = []
+        for j in range(1, lines):
+            to = line_peer(j)[1]
+            made.append(
+                remote(
+                    out_ref.at[c, at],
+                    out_ref.at[c, at],
+                    line_back_send.at[c, j],
+                    line_back_recv.at[c, j],
+                    to,
+                )
+            )
+        return made
+
+    def plane_back(c):
+        at = rows_at(base, quarter)
+        made = []
+        for j in range(1, planes):
+            to = plane_peer(j)[1]
+            made.append(
+                remote(
+                    out_ref.at[c, at],
+                    out_ref.at[c, at],
+                    plane_back_send.at[c, j],
+                    plane_back_recv.at[c, j],
+                    to,
+                )
+            )
+        return made
+
+    def core_back(c):
+        at = rows_at(core * half, half)
+        return [
+            remote(
+                out_ref.at[c, at],
+                out_ref.at[c, at],
+                core_back_send.at[c],
+                core_back_recv.at[c],
+                other_core,
+            )
+        ]
+
+    def small_copies(stage):
+        made = []
+        if stage == 0:
+            made.append(
+                remote(
+                    small_got.at[0, 0],
+                    small_got.at[0, 1],
+                    small_send.at[0, 1],
+                    small_recv.at[0, 1],
+                    other_core,
+                )
+            )
+        else:
+            for j in range(1, planes if stage == 1 else lines):
+                to = plane_peer(j)[1] if stage == 1 else line_peer(j)[1]
+                made.append(
+                    remote(
+                        small_got.at[stage, 0],
+                        small_got.at[stage, j],
+                        small_send.at[stage, j],
+                        small_recv.at[stage, j],
+                        to,
+                    )
+                )
+        return made
+
+    def start(copies):
+        for copy in copies:
+            copy.start()
+
+    def received(copies):
+        for copy in copies:
+            copy.wait_recv()
+
+    def ordered(got, at, count):
+        total = None
+        for i in range(count):
+            value = got(lax.rem(at + count - i, count))
+            total = value if total is None else total + value
+        return total
+
+    def stage_run(stage, c):
+        if stage == 0:
+            start(core_copy(c))
+        elif stage == 1:
+            received(core_copy(c))
+            add_rows(
+                half, core_sum.at[c], 0, [(grads[c], core * half), (core_got.at[c], 0)]
+            )
+            start(plane_copies(c))
+        elif stage == 2:
+            received(plane_copies(c))
+            add_rows(
+                quarter,
+                plane_sum.at[c],
+                0,
+                [(core_sum.at[c], plane_at * quarter)]
+                + [(plane_got.at[c, j], 0) for j in range(1, planes)],
+            )
+            start(line_copies(c))
+        elif stage == 3:
+            received(line_copies(c))
+            add_rows(
+                piece,
+                out_ref.at[c],
+                base + high * piece,
+                [(plane_sum.at[c], high * piece)]
+                + [(line_got.at[c, j], 0) for j in range(1, lines)],
+            )
+            start(line_back(c))
+        elif stage == 4:
+            received(line_back(c))
+            start(plane_back(c))
+        elif stage == 5:
+            received(plane_back(c))
+            start(core_back(c))
+        else:
+            received(core_back(c))
+
+    def small_run(stage):
+        if stage == 0:
+            small_got[0, 0] = small_ref[...]
+            start(small_copies(0))
+        elif stage == 1:
+            received(small_copies(0))
+            small_got[1, 0] = small_got[0, 0] + small_got[0, 1]
+            start(small_copies(1))
+        elif stage == 2:
+            received(small_copies(1))
+            small_got[2, 0] = ordered(lambda j: small_got[1, j], plane_at, planes)
+            start(small_copies(2))
+        elif stage == 3:
+            received(small_copies(2))
+            small_out[...] = ordered(lambda j: small_got[2, j], high, lines)
+
+    for tick in range(n + 6):
+        for stage in reversed(range(7)):
+            c = tick - stage
+            if 0 <= c < n:
+                stage_run(stage, c)
+        if tick < 4:
+            small_run(tick)
+    for stage in range(3):
+        for copy in small_copies(stage):
+            copy.wait_send()
+    for c in range(n):
+        for made in (core_copy, plane_copies, line_copies, line_back, plane_back, core_back):
+            for copy in made(c):
+                copy.wait_send()
+
+
+def reduce_all(grads, small, dp_size, experts):
+    n = len(grads)
+    tiles, width, _ = grads[0].shape
+    rows = tiles * width
+    x_axis, lines, planes = dp_size // 2, experts // 2, dp_size
+    if rows % (48 * dp_size * experts):
+        out, small = lax.psum((jnp.stack(grads).astype(F32), small), ("dp", "expert"))
+        return out.astype(BF16), small
+    half = rows // 2
+    quarter = half // planes
+    piece = quarter // lines
+    most = max(planes, lines)
+    sems = pltpu.SemaphoreType.DMA
+    out, small = pl.pallas_call(
+        functools.partial(reduce_kernel, x_axis, experts, n),
+        in_specs=[pl.BlockSpec(memory_space=pltpu.VMEM)] * (n + 1),
+        out_specs=[pl.BlockSpec(memory_space=pltpu.VMEM)] * 2,
+        out_shape=[
+            jax.ShapeDtypeStruct((n, rows, 128), BF16),
+            jax.ShapeDtypeStruct(small.shape, F32),
+        ],
+        scratch_shapes=[
+            pltpu.VMEM((n, half, 128), BF16),
+            pltpu.VMEM((n, half, 128), BF16),
+            pltpu.VMEM((n, planes, quarter, 128), BF16),
+            pltpu.VMEM((n, quarter, 128), BF16),
+            pltpu.VMEM((n, lines, piece, 128), BF16),
+            pltpu.VMEM((3, most, *small.shape), F32),
+        ]
+        + [sems((n,))] * 2
+        + [sems((n, planes))] * 2
+        + [sems((n, lines))] * 4
+        + [sems((n, planes))] * 2
+        + [sems((n,))] * 2
+        + [sems((3, most))] * 2,
+        compiler_params=pltpu.CompilerParams(
+            vmem_limit_bytes=40 * MIB, collective_id=1, has_side_effects=True
+        ),
+        cost_estimate=cost(8 * n * rows * 128, 100e6),
+        name="reduce_all",
+    )(*[g.reshape(rows, 128) for g in grads], small)
+    return out.reshape(n, tiles, width, 128), small
+
+
+def finish_kernel(
+    experts, cap, hidden_ref, gate_ref, place_ref, sums_ref, *refs
+):
+    made_refs = refs[:experts]
+    out_ref = refs[experts]
+    grad_refs = refs[experts + 1 : experts + 5]
+    slot_ref = refs[-1]
     tokens, width = hidden_ref.shape
-    slots = made_ref.shape[0]
     rows = 256
-    slot_ref[...] = jnp.broadcast_to(slot_col_of(route_ref[...], experts, cap), slot_ref.shape)
+    slot_ref[...] = jnp.broadcast_to(slot_col_of(place_ref[...], experts, cap), slot_ref.shape)
 
     def row_block(i, carry):
         at = pl.ds(pl.multiple_of(i * rows, rows), rows)
-        pick = one_hot(iota((rows, slots), 1) == slot_ref[at, 0:1])
-        produced = mm(pick, made_ref[...])
+        produced = jnp.zeros((rows, width), F32)
+        for e in range(experts):
+            pick = one_hot(iota((rows, cap), 1) + e * cap == slot_ref[at, 0:1])
+            produced = produced + mm(pick, made_refs[e][...])
         out_ref[at, :] = (hidden_ref[at, :] + gate_ref[at, 0:1] * produced).astype(BF16)
         return carry
 
     lax.fori_loop(0, tokens // rows, row_block, 0)
-
-
-def layer_output(made, hidden, gate, route, experts, cap):
+    for w, ref in enumerate(grad_refs):
+        for tile in range(width // 128):
+            ref[:, tile * 128 : (tile + 1) * 128] = sums_ref[w, tile].astype(F32)
+
+
+def finish(made, hidden, gate, place, sums, experts, cap):
     tokens, width = hidden.shape
     return pl.pallas_call(
-        functools.partial(output_kernel, experts, cap),
-        out_shape=jax.ShapeDtypeStruct((tokens, width), BF16),
+        functools.partial(finish_kernel, experts, cap),
+        out_shape=[jax.ShapeDtypeStruct((tokens, width), BF16)]
+        + [jax.ShapeDtypeStruct((width, width), F32)] * 4,
         scratch_shapes=[pltpu.VMEM((tokens, 128), jnp.int32)],
         compiler_params=params(),
-        cost_estimate=cost(2 * tokens * width * made.shape[0], 10 * tokens * width),
-        name="layer_output",
-    )(made, hidden, gate, route)
-
-
-def exchange(array, experts):
-    split = array.reshape(experts, array.shape[0] // experts, *array.shape[1:])
-    return lax.all_to_all(split, "expert", split_axis=0, concat_axis=0, tiled=True).reshape(
-        array.shape
-    )
-
-
-def lines_out(lines, experts, cap):
-    return lines[:, 0, :].reshape(experts, cap)
-
-
-def lines_in(rows):
-    flat = rows.reshape(-1, 1, 256)
-    return jnp.broadcast_to(flat, (flat.shape[0], 8, 256))
+        cost_estimate=cost(2 * tokens * width * experts * cap, 10 * tokens * width),
+        name="finish",
+    )(hidden, gate, place, sums, *made)
+
+
+def shifted(blocks, axis, size, step=1):
+    moved = [blocks[0]]
+    for s in range(1, len(blocks)):
+        moved.append(
+            lax.ppermute(blocks[s], axis, [(i, (i + s * step) % size) for i in range(size)])
+        )
+    return moved
 
 
 def on_device(
@@ -653,9 +1116,11 @@
 ):
     count, width = tokens.shape
     experts = lax.axis_size("expert")
+    dp_size = lax.axis_size("dp")
     cap = 2 * count // experts
     longest = segment_ids.shape[1] // 2
-    route_row = routes.reshape(1, count)
+    place = lax.rem(routes - lax.axis_index("expert") + experts, experts)
+    place_row = place.reshape(1, count)
     seg_col = segment_ids.reshape(count, 1)
     gain1, bias1 = norm1_gain[None], norm1_bias[None]
     gain2, bias2 = norm2_gain[None], norm2_bias[None]
@@ -663,49 +1128,53 @@
     proj = jnp.pad(router_proj, ((0, 0), (0, 128 - space)))
     embed = jnp.pad(expert_embed, ((0, 128 - experts), (0, 128 - space)))
 
-    up_slots = gather_slots(route_row, cotangent, experts, cap)
-    up_here = exchange(up_slots, experts)
+    up = gather_slots(place_row, cotangent, experts, cap)
+    tokens, *up = lax.optimization_barrier((tokens, *up))
+    up = shifted(up, "expert", experts)
     q, k, v = qkv(tokens, gain1, bias1, query_weight, w_key, w_value)
     mixed, probs = attention(q, k, v, seg_col, longest)
     hidden, gate, slots, gates = middle(
-        mixed, tokens, w_output, gain2, bias2, proj, embed, routes, route_row, experts, cap
-    )
-    x_here = exchange(slots, experts)
-    gates_here = lines_in(exchange(lines_out(gates, experts, cap), experts))
-    made, back, gate_grads, active, grad_pre, scaled = expert(
-        x_here, up_here, gates_here, expert_in[0], expert_out[0]
-    )
-    back_home = exchange(back, experts)
-    gate_grads_home = lines_in(exchange(lines_out(gate_grads, experts, cap), experts))
-    grad_in, grad_out = expert_grads(x_here, scaled, active, grad_pre)
-    made_home = exchange(made, experts)
-    grad_in = lax.psum_scatter(grad_in[None], "dp", scatter_dimension=2, tiled=True)
-    grad_out = lax.psum_scatter(grad_out[None], "dp", scatter_dimension=1, tiled=True)
-    grad_hidden, grad_mixed, delta, dwo, small2, dproj, dembed = middle_back(
-        back_home, gate_grads_home, hidden, cotangent, mixed, w_output, gain2, bias2,
-        proj, embed, routes, experts, cap,
+        mixed, tokens, w_output, gain2, bias2, proj, embed, routes, place_row, experts, cap
+    )
+    back, gate_grads, made, din, dout = expert(
+        slots, gates, up, expert_in[0], expert_out[0], dp_size
+    )
+    din = shifted(din, "dp", dp_size, 2)
+    dout = shifted(dout, "dp", dp_size, 2)
+    made = [made[0]] + [
+        lax.ppermute(made[s], "expert", [(i, (i - s) % experts) for i in range(experts)])
+        for s in range(1, experts)
+    ]
+    grad_hidden, grad_mixed, delta, dwo, small2 = middle_back(
+        back, gate_grads, hidden, cotangent, mixed, w_output, gain2, bias2,
+        proj, embed, routes, place, space, experts, cap,
     )
     dq, dk, dv = attention_back(q, k, v, grad_mixed, probs, delta, longest)
     grad_input, dwq, dwk, dwv, small1 = qkv_back(
         tokens, gain1, bias1, grad_hidden, dq, dk, dv, query_weight, w_key, w_value
     )
-    output = layer_output(made_home, hidden, gate, routes, experts, cap)
-    summed = lax.psum(
-        (
-            small1[0],
-            small1[1],
-            dwq,
-            dwk,
-            dwv,
-            dwo,
-            small2[0],
-            small2[1],
-            dproj[:, :space],
-            dembed[:experts, :space],
-        ),
-        ("dp", "expert"),
-    )
-    return (output, grad_input, *summed, grad_in.astype(F32), grad_out.astype(F32))
+    sums, small = reduce_all(
+        [dwo, dwq, dwk, dwv], jnp.concatenate([small1, small2], 0), dp_size, experts
+    )
+    output, dwo, dwq, dwk, dwv = finish(made, hidden, gate, place, sums, experts, cap)
+    grad_in = sum(block.astype(F32) for block in din)
+    grad_out = sum(block.astype(F32) for block in dout)
+    return (
+        output,
+        grad_input,
+        small[0],
+        small[1],
+        dwq,
+        dwk,
+        dwv,
+        dwo,
+        small[8],
+        small[9],
+        small[16 : 16 + space].T,
+        small[16 + space : 16 + space + experts, :space],
+        grad_in[None],
+        grad_out[None],
+    )
 
 
 def solution(mesh):

time: 730 us -> 469 us (0.64)
  waiting for transfers between devices: 262 us -> 0.04 us
  Pallas kernels: 241 us -> 403 us
  blocking collectives: 138 us -> 0 us
  local copies, waits for them, and re-layouts: 40.8 us -> 25.1 us
  between operations: 16.1 us -> 1.27 us
    pallas_call x4, Pallas kernels: 101 us -> 266 us  [the longest x1 158 us: expert(): pl.pallas_call(functools.partial(expert_kernel, experts, x_axis), in_spec...]
    all_to_all x4 -> x0, waiting for transfers between devices: 139 us -> none  [exchange(): lax.all_to_all(split, 'expert', split_axis=0, concat_axis=0, tiled=True)]
    psum x1 -> x0, waiting for transfers between devices: 122 us -> none  [on_device(): lax.psum((small1[0], small1[1], dwq, dwk, dwv, dwo, small2[0], small2[1],...]
    all_to_all x2 -> x0, blocking collectives: 86.1 us -> none  [exchange(): lax.all_to_all(split, 'expert', split_axis=0, concat_axis=0, tiled=True)]
    psum x1 -> x0, blocking collectives: 51.6 us -> none  [on_device(): lax.psum((small1[0], small1[1], dwq, dwk, dwv, dwo, small2[0], small2[1],...]
    ppermute x0 -> x16, starting transfers between devices: none -> 25.7 us  [the longest x9 16 us: shifted(): lax.ppermute(blocks[s], axis, [(i, (i + s * step) % size) for i in range(...]
    all_to_all x4 -> x0, starting transfers between devices: 18.2 us -> none  [exchange(): lax.all_to_all(split, 'expert', split_axis=0, concat_axis=0, tiled=True)]
    unnamed x45 -> x88, local copies, waits for them, and re-layouts: 27.2 us -> 19.1 us
  transfers between devices with their start and end apart: 7 -> 16, of which waited for: 3 -> 0; matrix products, arithmetic and copies ran while one was open for 2% -> 2% of each run, Pallas kernels for 14% -> 52%
where the time goes in v2:
time: 469 us; the launch traced here: 461 us
  Pallas kernels  403 us (86%)
  starting transfers between devices  25.7 us (5%)
  local copies, waits for them, and re-layouts  25.1 us (5%)
  other arithmetic  5.87 us (1%)
    pallas_call x1, Pallas kernels, expert(): pl.pallas_call(functools.partial(expert_kernel, experts, x_axis), in_spec...  158 us
    pallas_call x1, Pallas kernels, reduce_all(): pl.pallas_call(functools.partial(reduce_kernel, x_axis, experts, n), in_s...  88.6 us
    pallas_call x1, Pallas kernels, middle_back(): pl.pallas_call(functools.partial(middle_back_kernel, experts, cap), out_s...  34.9 us
    pallas_call x1, Pallas kernels, attention_back(): pl.pallas_call(functools.partial(attention_back_kernel, rows, longest), g...  30.2 us
    pallas_call x1, Pallas kernels, attention(): pl.pallas_call(functools.partial(attention_kernel, rows, longest), grid=(...  28.9 us
    pallas_call x1, Pallas kernels, middle(): pl.pallas_call(functools.partial(middle_kernel, experts, cap), out_shape=...  22.1 us
    unnamed x88, local copies, waits for them, and re-layouts  19.1 us
    ppermute x9, starting transfers between devices, shifted(): lax.ppermute(blocks[s], axis, [(i, (i + s * step) % size) for i in range(...  16 us
  transfers between devices with their start and end apart: 16, of which 0 were waited for; matrix products, arithmetic and copies ran while one was open for 2% of the time, Pallas kernels for 52%

profile of v2, /device:TPU:0, one launch (start us, length us, event | category | flops | bytes accessed | tf_op | source)
XLA Modules:
  0.0 460.7 jit_solution(2574535439507788984)
XLA Ops:
  0.7 0.8 broadcast_compare_fusion
  2.0 0.9 fusion.1
  3.0 4.5 gather_slots.1
  7.5 0.8 copy-done.16
  8.2 3.0 collective-permute-start
  11.2 1.6 collective-permute-start.1
  12.8 2.5 collective-permute-start.2
  15.3 1.2 collective-permute-start.3
  16.5 2.6 collective-permute-start.4
  19.2 1.0 copy.55.seg_ref
  20.3 1.4 copy-done.9
  21.7 1.3 copy-done.10
  23.0 1.3 copy-done.11
  24.2 1.3 copy-done.12
  25.5 5.2 %qkv.1 = (bf16[1024,768]{1,0:T(8,128)(2,1)S(1)}, bf16[1024,768]{1,0:T(8,128)(2,1)S(1)}, bf16[1024,768]{1,0:T(8,128)(2,1)S(1)}) custom-call(bf16[1024,768]{1,0:T(8,128)(2,1)S(1)} %copy-done.9, f32[1,768]{1,0:T(1,128)S(1)} %broadcast_in_dim.18.gain_ref, f32[1,768]{1,0:T(1,128)S(1)} %broadcast_in_dim.19.bias_ref, bf16[768,768]{1,0:T(8,128)(2,1)S(1)} %copy-done.10, ...), custom_call_target="tpu_custom_call" | custom-call | flops 3623878656 | bytes 9830400 | tf_op jit(solution)/shard_map/qkv/pallas_call | solution.py:134
  30.7 1.1 copy-done.13
  31.9 1.1 copy-done.14
  33.0 1.1 copy-done.15
  34.2 28.9 %attention.1 = (bf16[1024,768]{1,0:T(8,128)(2,1)}, bf16[12,1024,1024]{2,1,0:T(8,128)(2,1)}) custom-call(bf16[1024,768]{1,0:T(8,128)(2,1)} %copy-done.13, bf16[1024,768]{1,0:T(8,128)(2,1)} %copy-done.14, bf16[1024,768]{1,0:T(8,128)(2,1)} %copy-done.15, s32[1024,1]{1,0:T(8,128)} %copy.55.seg_ref), custom_call_target="tpu_custom_call" | custom-call | flops 12884901888 | bytes 25165824 | tf_op jit(solution)/shard_map/attention/pallas_call | solution.py:188
  63.1 1.0 copy.57.route_ref
  65.5 0.6 pad.9.embed_ref
  66.1 0.8 pad.8.proj_ref
  66.9 1.3 collective-permute-start.5
  68.2 1.6 collective-permute-start.6
  69.8 22.1 %middle.1 = (f32[1024,768]{1,0:T(8,128)}, f32[1024,128]{1,0:T(8,128)}, bf16[8,256,768]{2,1,0:T(8,128)(2,1)}, f32[8,8,256]{2,1,0:T(8,128)}) custom-call(bf16[1024,768]{1,0:T(8,128)(2,1)} %get-tuple-element.86.mixed_ref, bf16[1024,768]{1,0:T(8,128)(2,1)} %x_ref.4, bf16[768,768]{1,0:T(8,128)(2,1)} %wo_ref.3, f32[1,768]{1,0:T(1,128)} %broadcast_in_dim.20.gain_ref, ...), custom_call_target="tpu_custom_call" | custom-call | flops 4429185024 | bytes 12582912 | tf_op jit(solution)/shard_map/middle/pallas_call | solution.py:331
  92.0 0.7 copy-done.40
  93.5 157.5 %expert.1 = (bf16[8,256,768]{2,1,0:T(8,128)(2,1)}, f32[8,8,256]{2,1,0:T(8,128)}, bf16[256,768]{1,0:T(8,128)(2,1)}, bf16[256,768]{1,0:T(8,128)(2,1)}, bf16[256,76...) custom-call(bf16[8,256,768]{2,1,0:T(8,128)(2,1)} %get-tuple-element., ...), custom_call_target="tpu_custom_call" | custom-call | flops 57982058496 | bytes 18874368 | tf_op jit(solution)/shard_map/expert/pallas_call | solution.py:577
  251.0 3.2 collective-permute-start.7
  254.2 3.0 collective-permute-start.10
  257.2 1.5 collective-permute-start.14
  258.7 34.9 %middle_back.1 = (f32[1024,768]{1,0:T(8,128)}, bf16[1024,768]{1,0:T(8,128)(2,1)}, f32[6,8,1024]{2,1,0:T(8,128)}, bf16[6,768,128]{2,1,0:T(8,128)(2,1)}, f32[32,768]{1,0:T(8,128)}) custom-call(bf16[2048,768]{1,0:T(8,128)(2,1)} %bitcast.26, f32[8,8,256]{2,1,0:T(8,128)} %get-tuple-element.100.gate_grads_ref, f32[1024,768]{1,0:T(8,128)} %get-tuple-element.87.hidden_ref, ...), custom_call_target="tpu_custom_call" | custom-call | flops 5637144576 | bytes 15728640 | tf_op jit(solution)/shard_map/middle_back/pallas_call | solution.py:696
  293.6 30.2 %attention_back.1 = (bf16[1024,768]{1,0:T(8,128)(2,1)}, bf16[1024,768]{1,0:T(8,128)(2,1)}, bf16[1024,768]{1,0:T(8,128)(2,1)}) custom-call(bf16[1024,768]{1,0:T(8,128)(2,1)} %copy-done.13, bf16[1024,768]{1,0:T(8,128)(2,1)} %copy-done.14, bf16[1024,768]{1,0:T(8,128)(2,1)} %copy-done.15, bf16[1024,768]{1,0:T(8,128)(2,1)} %get-tuple-element.103.do_ref, ...), custom_call_target="tpu_custom_call" | custom-call | flops 25769803776 | bytes 25165824 | tf_op jit(solution)/shard_map/attention_back/pallas_call | solution.py:248
  323.8 0.6 collective-permute-start.15
  324.5 15.8 %qkv_back.1 = (f32[1024,768]{1,0:T(8,128)}, bf16[6,768,128]{2,1,0:T(8,128)(2,1)}, bf16[6,768,128]{2,1,0:T(8,128)(2,1)}, bf16[6,768,128]{2,1,0:T(8,128)(2,1)}, f32[8,768]{1,0:T(8,128)}) custom-call(bf16[1024,768]{1,0:T(8,128)(2,1)} %x_ref.4, f32[1,768]{1,0:T(1,128)} %copy-done.6, f32[1,768]{1,0:T(1,128)} %copy-done.7, ...), custom_call_target="tpu_custom_call" | custom-call | flops 7247757312 | bytes 15728640 | tf_op jit(solution)/shard_map/qkv_back/pallas_call | solution.py:749
  340.4 2.0 collective-permute-start.12
  342.4 1.5 collective-permute-start.13
  343.9 0.7 pad_maximum_fusion.refs_4_
  344.7 1.3 copy-done.2
  345.9 1.3 copy-done.3
  347.2 1.3 copy-done.4
  348.5 88.6 %reduce_all.1 = (bf16[4,4608,128]{2,1,0:T(8,128)(2,1)S(1)}, f32[40,768]{1,0:T(8,128)S(1)}) custom-call(bf16[4608,128]{1,0:T(8,128)(2,1)S(1)} %bitcast.17, bf16[4608,128]{1,0:T(8,128)(2,1)S(1)} %bitcast.18, bf16[4608,128]{1,0:T(8,128)(2,1)S(1)} %bitcast.19, bf16[4608,128]{1,0:T(8,128)(2,1)S(1)} %bitcast.20, f32[40,768]{1,0:T(8,128)S(1)} %pad_maximum_fusion.refs_4_), custom_call_target="tpu_custom_call" | custom-call | flops 18874368 | bytes 100000000 | tf_op jit(solution)/shard_map/reduce_all/pallas_call | solution.py:1020
  437.1 2.2 copy-done
  439.9 0.6 slice_reduce_fusion
  440.5 0.6 slice_bitcast_fusion
  441.2 0.7 copy-done.23
  442.2 15.0 %finish.1 = (bf16[1024,768]{1,0:T(8,128)(2,1)}, f32[768,768]{1,0:T(8,128)}, f32[768,768]{1,0:T(8,128)}, f32[768,768]{1,0:T(8,128)}, f32[768,768]{1,0:T(8,128)}) custom-call(f32[1024,768]{1,0:T(8,128)} %get-tuple-element.87.hidden_ref, f32[1024,128]{1,0:T(8,128)} %get-tuple-element.88.gate_ref, s32[1024,1]{1,0:T(8,128)} %get-tuple-element.139.place_ref, ...), custom_call_target="tpu_custom_call" | custom-call | flops 3221225472 | bytes 7864320 | tf_op jit(solution)/shard_map/finish/pallas_call | solution.py:1079
  457.1 1.7 add_bitcast_fusion.1
  458.8 1.7 add_bitcast_fusion
  (99 shorter events, 3.7 us)
Async XLA Ops:
  0.6 2.3 copy-start.8
  2.9 4.5 copy-start.5
  3.0 16.2 %copy-start.31 = (f32[768]{0:T(1024)S(1)}, f32[768]{0:T(1024)}, u32[]{:S(2)}) copy-start(f32[768]{0:T(1024)} %param.19) | copy-start | bytes 9220
  3.0 16.2 %copy-start.32 = (f32[768]{0:T(1024)S(1)}, f32[768]{0:T(1024)}, u32[]{:S(2)}) copy-start(f32[768]{0:T(1024)} %param.20) | copy-start | bytes 9220
  3.0 16.3 %copy-start.29 = (s32[1,1024]{1,0:T(1,128)S(1)}, s32[1,1024]{1,0:T(1,128)}, u32[]{:S(2)}) copy-start(s32[1,1024]{1,0:T(1,128)} %param.17) | copy-start | bytes 12292
  8.2 58.6 %collective-permute-start = (bf16[256,768]{1,0:T(8,128)(2,1)}, bf16[256,768]{1,0:T(8,128)(2,1)S(1)}, u32[]{:S(2)}, u32[]{:S(2)}) collective-permute-start(bf16[256,768]{1,0:T(8,128)(2,1)} %get-tuple-element.92), channel_id=1, source_target_pairs={{0,1},{1,2},{2,3},{3,4},{4,5},{5,6},{6,7},{7,0},{8,9},{9,10},{10,1... | collective-permute-start | bytes 1179656 | tf_op jit(solution)/shard_map/ppermute | solution.py:1094
  11.2 57.0 %collective-permute-start.1 = (bf16[256,768]{1,0:T(8,128)(2,1)}, bf16[256,768]{1,0:T(8,128)(2,1)S(1)}, u32[]{:S(2)}, u32[]{:S(2)}) collective-permute-start(bf16[256,768]{1,0:T(8,128)(2,1)} %get-tuple-element.93), channel_id=1, source_target_pairs={{0,2},{1,3},{2,4},{3,5},{4,6},{5,7},{6,0},{7,1},{8,10},{9,11},{10,... | collective-permute-start | bytes 1179656 | tf_op jit(solution)/shard_map/ppermute | solution.py:1094
  12.8 79.2 %collective-permute-start.2 = (bf16[256,768]{1,0:T(8,128)(2,1)}, bf16[256,768]{1,0:T(8,128)(2,1)S(1)}, u32[]{:S(2)}, u32[]{:S(2)}) collective-permute-start(bf16[256,768]{1,0:T(8,128)(2,1)} %get-tuple-element.94), channel_id=1, source_target_pairs={{0,3},{1,4},{2,5},{3,6},{4,7},{5,0},{6,1},{7,2},{8,11},{9,12},{10,... | collective-permute-start | bytes 1179656 | tf_op jit(solution)/shard_map/ppermute | solution.py:1094
  15.3 76.6 %collective-permute-start.3 = (bf16[256,768]{1,0:T(8,128)(2,1)S(1)}, bf16[256,768]{1,0:T(8,128)(2,1)}, u32[]{:S(2)}, u32[]{:S(2)}) collective-permute-start(bf16[256,768]{1,0:T(8,128)(2,1)S(1)} %get-tuple-element.95), channel_id=1, source_target_pairs={{0,4},{1,5},{2,6},{3,7},{4,0},{5,1},{6,2},{7,3},{8,12},{9,13},{10,... | collective-permute-start | bytes 1179656 | tf_op jit(solution)/shard_map/ppermute | solution.py:1094
  16.5 75.4 %collective-permute-start.4 = (bf16[256,768]{1,0:T(8,128)(2,1)S(1)}, bf16[256,768]{1,0:T(8,128)(2,1)}, u32[]{:S(2)}, u32[]{:S(2)}) collective-permute-start(bf16[256,768]{1,0:T(8,128)(2,1)S(1)} %get-tuple-element.96), channel_id=1, source_target_pairs={{0,5},{1,6},{2,7},{3,0},{4,1},{5,2},{6,3},{7,4},{8,13},{9,14},{10,... | collective-permute-start | bytes 1179656 | tf_op jit(solution)/shard_map/ppermute | solution.py:1094
  19.2 11.5 %copy-start.6 = (f32[1,768]{1,0:T(1,128)}, f32[1,768]{1,0:T(1,128)S(1)}, u32[]{:S(2)}) copy-start(f32[1,768]{1,0:T(1,128)S(1)} %broadcast_in_dim.18.gain_ref) | copy-start | bytes 9220
  19.2 11.5 %copy-start.7 = (f32[1,768]{1,0:T(1,128)}, f32[1,768]{1,0:T(1,128)S(1)}, u32[]{:S(2)}) copy-start(f32[1,768]{1,0:T(1,128)S(1)} %broadcast_in_dim.19.bias_ref) | copy-start | bytes 9220
  20.3 1.4 copy-start.9
  21.7 1.3 copy-start.10
  23.0 1.3 copy-start.11
  24.2 1.3 copy-start.12
  34.2 28.9 %copy-start.28 = (s32[1024,1]{0,1:T(1,128)S(1)}, s32[1024,1]{0,1:T(1,128)}, u32[]{:S(2)}) copy-start(s32[1024,1]{0,1:T(1,128)} %param.18) | copy-start | bytes 12292
  34.2 30.0 %copy-start.33 = (f32[768]{0:T(1024)S(1)}, f32[768]{0:T(1024)}, u32[]{:S(2)}) copy-start(f32[768]{0:T(1024)} %param.25) | copy-start | bytes 9220
  34.2 30.5 %copy-start.34 = (f32[768]{0:T(1024)S(1)}, f32[768]{0:T(1024)}, u32[]{:S(2)}) copy-start(f32[768]{0:T(1024)} %param.26) | copy-start | bytes 9220
  34.2 31.1 %copy-start.27 = (f32[768,16]{0,1:T(8,128)S(1)}, f32[768,16]{0,1:T(8,128)}, u32[]{:S(2)}) copy-start(f32[768,16]{0,1:T(8,128)} %param.27) | copy-start | bytes 147460
  34.2 31.3 %copy-start.30 = (f32[8,16]{1,0:T(8,128)S(1)}, f32[8,16]{1,0:T(8,128)}, u32[]{:S(2)}) copy-start(f32[8,16]{1,0:T(8,128)} %param.28) | copy-start | bytes 1540
  66.9 25.0 %copy-start.38 = (bf16[256,768]{1,0:T(8,128)(2,1)}, bf16[256,768]{1,0:T(8,128)(2,1)S(1)}, u32[]{:S(2)}) copy-start(bf16[256,768]{1,0:T(8,128)(2,1)S(1)} %collective-permute-done.refs_5_) | copy-start | bytes 1179652
  66.9 25.1 %collective-permute-start.5 = (bf16[256,768]{1,0:T(8,128)(2,1)S(1)}, bf16[256,768]{1,0:T(8,128)(2,1)S(1)}, u32[]{:S(2)}, u32[]{:S(2)}) collective-permute-start(bf16[256,768]{1,0:T(8,128)(2,1)S(1)} %get-tuple-element.97), channel_id=1, source_target_pairs={{0,6},{1,7},{2,0},{3,1},{4,2},{5,3},{6,4},{7,5},{8,14},{9,15},{10,... | collective-permute-start | bytes 1179656 | tf_op jit(solution)/shard_map/ppermute | solution.py:1094
  68.2 23.7 %copy-start.39 = (bf16[256,768]{1,0:T(8,128)(2,1)}, bf16[256,768]{1,0:T(8,128)(2,1)S(1)}, u32[]{:S(2)}) copy-start(bf16[256,768]{1,0:T(8,128)(2,1)S(1)} %collective-permute-done.1.refs_6_) | copy-start | bytes 1179652
  68.2 23.8 %collective-permute-start.6 = (bf16[256,768]{1,0:T(8,128)(2,1)S(1)}, bf16[256,768]{1,0:T(8,128)(2,1)S(1)}, u32[]{:S(2)}, u32[]{:S(2)}) collective-permute-start(bf16[256,768]{1,0:T(8,128)(2,1)S(1)} %get-tuple-element.98), channel_id=1, source_target_pairs={{0,7},{1,0},{2,1},{3,2},{4,3},{5,4},{6,5},{7,6},{8,15},{9,8},{10,9... | collective-permute-start | bytes 1179656 | tf_op jit(solution)/shard_map/ppermute | solution.py:1094
  251.0 72.8 %collective-permute-start.7 = (bf16[256,768]{1,0:T(8,128)(2,1)}, bf16[256,768]{1,0:T(8,128)(2,1)S(1)}, u32[]{:S(2)}, u32[]{:S(2)}) collective-permute-start(bf16[256,768]{1,0:T(8,128)(2,1)} %get-tuple-element.116), channel_id=1, source_target_pairs={{0,7},{1,0},{2,1},{3,2},{4,3},{5,4},{6,5},{7,6},{8,15},{9,8},{10,9... | collective-permute-start | bytes 1179656 | tf_op jit(solution)/shard_map/ppermute | solution.py:1145
  254.2 86.1 %collective-permute-start.8 = (bf16[256,768]{1,0:T(8,128)(2,1)}, bf16[256,768]{1,0:T(8,128)(2,1)S(1)}, u32[]{:S(2)}, u32[]{:S(2)}) collective-permute-start(bf16[256,768]{1,0:T(8,128)(2,1)} %get-tuple-element.117), channel_id=1, source_target_pairs={{0,6},{1,7},{2,0},{3,1},{4,2},{5,3},{6,4},{7,5},{8,14},{9,15},{10,... | collective-permute-start | bytes 1179656 | tf_op jit(solution)/shard_map/ppermute | solution.py:1145
  254.2 86.2 %collective-permute-start.9 = (bf16[256,768]{1,0:T(8,128)(2,1)}, bf16[256,768]{1,0:T(8,128)(2,1)S(1)}, u32[]{:S(2)}, u32[]{:S(2)}) collective-permute-start(bf16[256,768]{1,0:T(8,128)(2,1)} %get-tuple-element.118), channel_id=1, source_target_pairs={{0,5},{1,6},{2,7},{3,0},{4,1},{5,2},{6,3},{7,4},{8,13},{9,14},{10,... | collective-permute-start | bytes 1179656 | tf_op jit(solution)/shard_map/ppermute | solution.py:1145
  254.2 88.2 %collective-permute-start.10 = (bf16[256,768]{1,0:T(8,128)(2,1)}, bf16[256,768]{1,0:T(8,128)(2,1)S(1)}, u32[]{:S(2)}, u32[]{:S(2)}) collective-permute-start(bf16[256,768]{1,0:T(8,128)(2,1)} %get-tuple-element.119), channel_id=1, source_target_pairs={{0,4},{1,5},{2,6},{3,7},{4,0},{5,1},{6,2},{7,3},{8,12},{9,13},{10,... | collective-permute-start | bytes 1179656 | tf_op jit(solution)/shard_map/ppermute | solution.py:1145
  257.2 199.9 %collective-permute-start.14 = (bf16[768,768]{1,0:T(8,128)(2,1)}, bf16[768,768]{1,0:T(8,128)(2,1)S(1)}, u32[]{:S(2)}, u32[]{:S(2)}) collective-permute-start(bf16[768,768]{1,0:T(8,128)(2,1)} %get-tuple-element.131), channel_id=1, source_target_pairs={{0,16},{8,24},{16,0},{24,8},{1,17},{9,25},{17,1},{25,9},{2,18},{10... | collective-permute-start | bytes 3538952 | tf_op jit(solution)/shard_map/ppermute | solution.py:1094
  293.6 30.2 %copy-start.35 = (bf16[768,768]{1,0:T(8,128)(2,1)S(1)}, bf16[768,768]{1,0:T(8,128)(2,1)}, u32[]{:S(2)}) copy-start(bf16[768,768]{1,0:T(8,128)(2,1)} %get-tuple-element.133) | copy-start | bytes 3538948
  323.8 16.5 %copy-start.19 = (bf16[256,768]{1,0:T(8,128)(2,1)}, bf16[256,768]{1,0:T(8,128)(2,1)S(1)}, u32[]{:S(2)}) copy-start(bf16[256,768]{1,0:T(8,128)(2,1)S(1)} %collective-permute-done.7.refs_1_) | copy-start | bytes 1179652
  323.8 135.0 %collective-permute-start.15 = (bf16[768,768]{1,0:T(8,128)(2,1)S(1)}, bf16[768,768]{1,0:T(8,128)(2,1)S(1)}, u32[]{:S(2)}, u32[]{:S(2)}) collective-permute-start(bf16[768,768]{1,0:T(8,128)(2,1)S(1)} %copy-done.35), channel_id=1, source_target_pairs={{0,16},{8,24},{16,0},{24,8},{1,17},{9,25},{17,1},{25,9},{2,18},{10... | collective-permute-start | bytes 3538952 | tf_op jit(solution)/shard_map/ppermute | solution.py:1094
  324.5 16.0 %copy-start.37 = (bf16[256,768]{1,0:T(8,128)(2,1)S(1)}, bf16[256,768]{1,0:T(8,128)(2,1)}, u32[]{:S(2)}) copy-start(bf16[256,768]{1,0:T(8,128)(2,1)} %get-tuple-element.121) | copy-start | bytes 1179652
  324.5 17.9 %copy-start.36 = (bf16[256,768]{1,0:T(8,128)(2,1)S(1)}, bf16[256,768]{1,0:T(8,128)(2,1)}, u32[]{:S(2)}) copy-start(bf16[256,768]{1,0:T(8,128)(2,1)} %get-tuple-element.122) | copy-start | bytes 1179652
  324.5 19.5 %copy-start.26 = (f32[32,768]{1,0:T(8,128)S(1)}, f32[32,768]{1,0:T(8,128)}, u32[]{:S(2)}) copy-start(f32[32,768]{1,0:T(8,128)} %get-tuple-element.113) | copy-start | bytes 294916
  324.5 20.2 %copy-start.1 = (bf16[6,768,128]{2,1,0:T(8,128)(2,1)S(1)}, bf16[6,768,128]{2,1,0:T(8,128)(2,1)}, u32[]{:S(2)}) copy-start(bf16[6,768,128]{2,1,0:T(8,128)(2,1)} %get-tuple-element.101) | copy-start | bytes 3538948
  340.3 96.8 %copy-start.20 = (bf16[256,768]{1,0:T(8,128)(2,1)}, bf16[256,768]{1,0:T(8,128)(2,1)S(1)}, u32[]{:S(2)}) copy-start(bf16[256,768]{1,0:T(8,128)(2,1)S(1)} %collective-permute-done.8.refs_2_) | copy-start | bytes 1179652
  340.3 100.8 %collective-permute-start.11 = (bf16[256,768]{1,0:T(8,128)(2,1)}, bf16[256,768]{1,0:T(8,128)(2,1)S(1)}, u32[]{:S(2)}, u32[]{:S(2)}) collective-permute-start(bf16[256,768]{1,0:T(8,128)(2,1)} %get-tuple-element.120), channel_id=1, source_target_pairs={{0,3},{1,4},{2,5},{3,6},{4,7},{5,0},{6,1},{7,2},{8,11},{9,12},{10,... | collective-permute-start | bytes 1179656 | tf_op jit(solution)/shard_map/ppermute | solution.py:1145
  340.4 96.7 %copy-start.21 = (bf16[256,768]{1,0:T(8,128)(2,1)}, bf16[256,768]{1,0:T(8,128)(2,1)S(1)}, u32[]{:S(2)}) copy-start(bf16[256,768]{1,0:T(8,128)(2,1)S(1)} %collective-permute-done.9.refs_3_) | copy-start | bytes 1179652
  340.4 100.7 %collective-permute-start.12 = (bf16[256,768]{1,0:T(8,128)(2,1)S(1)}, bf16[256,768]{1,0:T(8,128)(2,1)S(1)}, u32[]{:S(2)}, u32[]{:S(2)}) collective-permute-start(bf16[256,768]{1,0:T(8,128)(2,1)S(1)} %copy-done.37), channel_id=1, source_target_pairs={{0,2},{1,3},{2,4},{3,5},{4,6},{5,7},{6,0},{7,1},{8,10},{9,11},{10,... | collective-permute-start | bytes 1179656 | tf_op jit(solution)/shard_map/ppermute | solution.py:1145
  342.4 94.7 %copy-start.22 = (bf16[256,768]{1,0:T(8,128)(2,1)}, bf16[256,768]{1,0:T(8,128)(2,1)S(1)}, u32[]{:S(2)}) copy-start(bf16[256,768]{1,0:T(8,128)(2,1)S(1)} %collective-permute-done.10.refs_4_) | copy-start | bytes 1179652
  342.4 98.8 %collective-permute-start.13 = (bf16[256,768]{1,0:T(8,128)(2,1)S(1)}, bf16[256,768]{1,0:T(8,128)(2,1)S(1)}, u32[]{:S(2)}, u32[]{:S(2)}) collective-permute-start(bf16[256,768]{1,0:T(8,128)(2,1)S(1)} %copy-done.36), channel_id=1, source_target_pairs={{0,1},{1,2},{2,3},{3,4},{4,5},{5,6},{6,7},{7,0},{8,9},{9,10},{10,1... | collective-permute-start | bytes 1179656 | tf_op jit(solution)/shard_map/ppermute | solution.py:1145
  344.7 1.3 copy-start.2
  347.2 1.3 copy-start.4
  437.1 2.2 copy-start
  442.2 15.0 %copy-start.18 = (bf16[768,768]{1,0:T(8,128)(2,1)S(1)}, bf16[768,768]{1,0:T(8,128)(2,1)}, u32[]{:S(2)}) copy-start(bf16[768,768]{1,0:T(8,128)(2,1)} %get-tuple-element.130) | copy-start | bytes 3538948
  457.1 1.7 copy-start.17
  (11 other events, 10.5 us)

commit v3 on v2

--- a/solution.py
+++ b/solution.py
@@ -361,15 +361,15 @@
     up_refs = refs[4 : 4 + experts]
     back_ref, gate_grads_ref = refs[4 + experts : 6 + experts]
     rest = refs[6 + experts :]
-    made_refs = rest[:experts]
-    din_refs = rest[experts : experts + x_axis]
-    dout_refs = rest[experts + x_axis : experts + 2 * x_axis]
+    made_ref = rest[0]
+    din_refs = rest[1 : 1 + x_axis]
+    dout_refs = rest[1 + x_axis : 1 + 2 * x_axis]
     (
         x_here, up_here, gates_here, back_here, gate_grads_here, made_here,
         active, grad_pre, w_in, w_out, din_got, dout_got,
         load_sem, x_send, x_recv, g_send, g_recv, b_send, b_recv, gg_send, gg_recv,
         d_send, d_recv, store_sem,
-    ) = rest[experts + 2 * x_axis :]
+    ) = rest[1 + 2 * x_axis :]
     cap, width = x_here.shape[1:]
     hidden = w_in.shape[1]
     me = lax.axis_index("expert")
@@ -471,8 +471,11 @@
         pltpu.make_async_copy(back_here.at[0], back_ref.at[0], store_sem.at[0]),
         pltpu.make_async_copy(gate_grads_here.at[0], gate_grads_ref.at[0], store_sem.at[1]),
     ]
-    for s, made_ref in enumerate(made_refs):
-        stores.append(pltpu.make_async_copy(made_here.at[s], made_ref, store_sem.at[2 + s]))
+    for s in range(experts):
+        home = lax.rem(me + experts - s, experts)
+        stores.append(
+            pltpu.make_async_copy(made_here.at[s], made_ref.at[home], store_sem.at[2 + s])
+        )
     for store in stores:
         store.start()
 
@@ -561,13 +564,9 @@
     x_axis = dp_size // 2
     block = hidden // dp_size
     anywhere = pl.BlockSpec(memory_space=pl.ANY)
-    rows = jax.ShapeDtypeStruct((cap, width), BF16)
+    rows = jax.ShapeDtypeStruct((experts, cap, width), BF16)
     out_shape = (
-        [
-            jax.ShapeDtypeStruct((experts, cap, width), BF16),
-            jax.ShapeDtypeStruct((experts, 8, cap), F32),
-        ]
-        + [rows] * experts
+        [rows, jax.ShapeDtypeStruct((experts, 8, cap), F32), rows]
         + [jax.ShapeDtypeStruct((width, block), BF16)] * x_axis
         + [jax.ShapeDtypeStruct((block, width), BF16)] * x_axis
     )
@@ -603,10 +602,9 @@
         cost_estimate=cost(12 * slots * width * hidden, 8 * width * hidden),
         name="expert",
     )(x, gates, w_in, w_out, *up)
-    back, gate_grads = out[:2]
-    made = out[2 : 2 + experts]
-    din = out[2 + experts : 2 + experts + x_axis]
-    dout = out[2 + experts + x_axis :]
+    back, gate_grads, made = out[:3]
+    din = out[3 : 3 + x_axis]
+    dout = out[3 + x_axis :]
     return back, gate_grads, made, din, dout
 
 
@@ -777,16 +775,26 @@
     lax.fori_loop(0, rows // step, body, 0)
 
 
-def reduce_kernel(x_axis, experts, n, *refs):
-    grads = refs[:n]
-    small_ref = refs[n]
-    out_ref, small_out = refs[n + 1 : n + 3]
-    (
-        core_got, core_sum, plane_got, plane_sum, line_got,
-        small_got, core_send, core_recv, plane_send, plane_recv, line_send, line_recv,
-        line_back_send, line_back_recv, plane_back_send, plane_back_recv,
-        core_back_send, core_back_recv, small_send, small_recv,
-    ) = refs[n + 3 :]
+def can_reduce(width, dp_size, experts):
+    return (width // 128) % 2 == 0 and (width // 128) * width % (48 * dp_size * experts) == 0
+
+
+def tail_kernel(
+    x_axis, experts, longest,
+    q_ref, k_ref, v_ref, do_ref, delta_ref, x_ref, gain_ref, bias_ref,
+    wq_ref, wk_ref, wv_ref, small_ref, probs_ref, grad_hidden_hbm, dwo_ref,
+    grad_ref, out_ref, small_out,
+    dq_all, dk_all, dv_all, normed_t, prob_buf, dk_sum, dv_sum, grads, grad_hidden, small_in,
+    core_got, core_sum, plane_got, plane_sum, line_got, small_got,
+    load_sem, prob_sem,
+    core_send, core_recv, plane_send, plane_recv, line_send, line_recv,
+    line_back_send, line_back_recv, plane_back_send, plane_back_recv,
+    core_back_send, core_back_recv, small_send, small_recv,
+):
+    tokens, width = x_ref.shape
+    pairs = width // PAIR
+    n = grads.shape[0]
+    block_rows = 256
     dp = lax.axis_index("dp")
     me = lax.axis_index("expert")
     core = lax.rem(dp, 2)
@@ -795,7 +803,7 @@
     high = me // 2
     planes, lines = 2 * x_axis, experts // 2
     mesh_ids = pl.DeviceIdType.MESH
-    rows = grads[0].shape[0]
+    rows = grads.shape[1]
     half = rows // 2
     quarter = half // planes
     piece = quarter // lines
@@ -826,7 +834,7 @@
         return pl.ds(pl.multiple_of(start, 16), size)
 
     def core_copy(c):
-        src = grads[c].at[rows_at((1 - core) * half, half)]
+        src = grads.at[c, rows_at((1 - core) * half, half)]
         return [remote(src, core_got.at[c], core_send.at[c], core_recv.at[c], other_core)]
 
     def plane_copies(c):
@@ -940,7 +948,7 @@
         elif stage == 1:
             received(core_copy(c))
             add_rows(
-                half, core_sum.at[c], 0, [(grads[c], core * half), (core_got.at[c], 0)]
+                half, core_sum.at[c], 0, [(grads.at[c], core * half), (core_got.at[c], 0)]
             )
             start(plane_copies(c))
         elif stage == 2:
@@ -974,7 +982,7 @@
 
     def small_run(stage):
         if stage == 0:
-            small_got[0, 0] = small_ref[...]
+            small_got[0, 0] = small_in[...]
             start(small_copies(0))
         elif stage == 1:
             received(small_copies(0))
@@ -988,50 +996,201 @@
             received(small_copies(2))
             small_out[...] = ordered(lambda j: small_got[2, j], high, lines)
 
-    for tick in range(n + 6):
+
+    def prob_copy(p, slot):
+        return pltpu.make_async_copy(
+            probs_ref.at[pl.ds(2 * p, 2)], prob_buf.at[slot], prob_sem.at[slot]
+        )
+
+    loads = [
+        pltpu.make_async_copy(dwo_ref, grads.at[0], load_sem.at[0]),
+        pltpu.make_async_copy(grad_hidden_hbm, grad_hidden, load_sem.at[1]),
+    ]
+    prob_copy(0, 0).start()
+    for load in loads:
+        load.start()
+    for at in range(0, tokens, block_rows):
+        part = slice(at, at + block_rows)
+        unit, _ = norm_parts(x_ref[part, :].astype(F32))
+        normed = unit * gain_ref[...] + bias_ref[...]
+        normed_t[:, part] = normed.T.astype(BF16)
+    loads[0].wait()
+    stage_run(0, 0)
+    scale = HEAD_DIM**-0.5
+    lane = iota((tokens, PAIR), 1)
+    own = (lane < HEAD_DIM, lane >= HEAD_DIM)
+    zero = jnp.zeros((), BF16)
+
+    def pair_step(p, carry):
+        slot = lax.rem(p, 2)
+        prob_copy(p, slot).wait()
+
+        @pl.when(p < pairs - 1)
+        def _():
+            prob_copy(p + 1, 1 - slot).start()
+
+        lanes = pl.ds(pl.multiple_of(p * PAIR, PAIR), PAIR)
+        dk_sum[...] = jnp.zeros_like(dk_sum)
+        dv_sum[...] = jnp.zeros_like(dv_sum)
+        for block in range(tokens // block_rows):
+            first, last = key_window(block, block_rows, tokens, longest)
+            mine = slice(block * block_rows, (block + 1) * block_rows)
+            values = v_ref[first:last, lanes]
+            keys = k_ref[first:last, lanes]
+            queries = q_ref[mine, lanes]
+            grad_out = do_ref[mine, lanes]
+            dq = jnp.zeros((block_rows, PAIR), F32)
+            dk = jnp.zeros((last - first, PAIR), F32)
+            dv = jnp.zeros((last - first, PAIR), F32)
+            for h in range(2):
+                do_h = jnp.where(own[h][mine], grad_out, zero)
+                q_h = jnp.where(own[h][mine], queries, zero)
+                k_h = jnp.where(own[h][first:last], keys, zero)
+                probs = prob_buf[slot, h, first:last, mine]
+                grad_probs = mm_cols(values, do_h)
+                grad_scores = (
+                    probs.astype(F32) * (grad_probs - delta_ref[p, h : h + 1, mine])
+                ).astype(BF16)
+                dq = dq + mm_rows(grad_scores, k_h)
+                dk = dk + mm(grad_scores, q_h)
+                dv = dv + mm(probs, do_h)
+            dq_all[mine, lanes] = (dq * scale).astype(BF16)
+            dk_sum[first:last, :] += dk
+            dv_sum[first:last, :] += dv
+        dk_all[:, lanes] = (dk_sum[...] * scale).astype(BF16)
+        dv_all[:, lanes] = dv_sum[...].astype(BF16)
+        j = p // 2
+
+        @pl.when(lax.rem(p, 2) == 0)
+        def _():
+            @pl.when(j >= 2)
+            def _():
+                stage_run(5, j - 2)
+
+            @pl.when(j >= 1)
+            def _():
+                stage_run(3, j - 1)
+
+            stage_run(1, j)
+
+        @pl.when(lax.rem(p, 2) == 1)
+        def _():
+            both = pl.ds(pl.multiple_of(j * 2 * PAIR, PAIR), 2 * PAIR)
+            for w, ref in enumerate((dq_all, dk_all, dv_all)):
+                made = mm(normed_t[...], ref[:, both]).astype(BF16)
+                for i in range(2):
+                    start_at = (2 * w + i) * width
+                    grads[j + 1, start_at : start_at + width, :] = made[:, i * 128 : (i + 1) * 128]
+            stage_run(0, j + 1)
+
+            @pl.when(j >= 2)
+            def _():
+                stage_run(6, j - 2)
+
+            @pl.when(j >= 1)
+            def _():
+                stage_run(4, j - 1)
+
+            stage_run(2, j)
+
+        return carry
+
+    lax.fori_loop(0, pairs, pair_step, 0)
+    loads[1].wait()
+    small_in[0:8, :] = jnp.zeros((8, width), F32)
+    small_in[8:, :] = small_ref[...]
+
+    def row_block(i):
+        at = slice(i * block_rows, (i + 1) * block_rows)
+        unit, unit_scale = norm_parts(x_ref[at, :].astype(F32))
+        grad = (
+            mm_cols(dq_all[at, :], wq_ref[...])
+            + mm_cols(dk_all[at, :], wk_ref[...])
+            + mm_cols(dv_all[at, :], wv_ref[...])
+        )
+        small_in[0:1, :] += jnp.sum(grad * unit, 0, keepdims=True)
+        small_in[1:2, :] += jnp.sum(grad, 0, keepdims=True)
+        grad_ref[at, :] = grad_hidden[at, :] + norm_back(grad, gain_ref[...], unit, unit_scale)
+
+    blocks = tokens // block_rows
+    done = 0
+    small_at = 0
+    for tick in range(pairs + 1, pairs + 7):
+        if done < blocks:
+            row_block(done)
+            done += 1
         for stage in reversed(range(7)):
-            c = tick - stage
-            if 0 <= c < n:
-                stage_run(stage, c)
-        if tick < 4:
-            small_run(tick)
+            for c in range(n):
+                if tick - 2 * c == stage:
+                    stage_run(stage, c)
+        if done == blocks and small_at < 4:
+            small_run(small_at)
+            small_at += 1
+    while done < blocks:
+        row_block(done)
+        done += 1
+    while small_at < 4:
+        small_run(small_at)
+        small_at += 1
     for stage in range(3):
         for copy in small_copies(stage):
             copy.wait_send()
-    for c in range(n):
+
+    def sent(c, carry):
         for made in (core_copy, plane_copies, line_copies, line_back, plane_back, core_back):
             for copy in made(c):
                 copy.wait_send()
-
-
-def reduce_all(grads, small, dp_size, experts):
-    n = len(grads)
-    tiles, width, _ = grads[0].shape
-    rows = tiles * width
+        return carry
+
+    lax.fori_loop(0, n, sent, 0)
+
+
+def tail(
+    q, k, v, grad_mixed, probs, delta, x, gain, bias, grad_hidden, wq, wk, wv, dwo, small2,
+    longest, dp_size, experts,
+):
+    tokens, width = x.shape
+    pairs = width // PAIR
+    n = 1 + pairs // 2
+    rows = width // 128 * width
     x_axis, lines, planes = dp_size // 2, experts // 2, dp_size
-    if rows % (48 * dp_size * experts):
-        out, small = lax.psum((jnp.stack(grads).astype(F32), small), ("dp", "expert"))
-        return out.astype(BF16), small
     half = rows // 2
     quarter = half // planes
     piece = quarter // lines
     most = max(planes, lines)
+    small_shape = (8 + small2.shape[0], width)
     sems = pltpu.SemaphoreType.DMA
-    out, small = pl.pallas_call(
-        functools.partial(reduce_kernel, x_axis, experts, n),
-        in_specs=[pl.BlockSpec(memory_space=pltpu.VMEM)] * (n + 1),
-        out_specs=[pl.BlockSpec(memory_space=pltpu.VMEM)] * 2,
+    local = pl.BlockSpec(memory_space=pltpu.VMEM)
+    anywhere = pl.BlockSpec(memory_space=pl.ANY)
+    low = pltpu.VMEM((tokens, width), BF16)
+    return pl.pallas_call(
+        functools.partial(tail_kernel, x_axis, experts, longest),
+        in_specs=[local] * 12 + [anywhere] * 3,
+        out_specs=[local] * 3,
         out_shape=[
+            jax.ShapeDtypeStruct((tokens, width), F32),
             jax.ShapeDtypeStruct((n, rows, 128), BF16),
-            jax.ShapeDtypeStruct(small.shape, F32),
+            jax.ShapeDtypeStruct(small_shape, F32),
         ],
         scratch_shapes=[
+            low,
+            low,
+            low,
+            pltpu.VMEM((width, tokens), BF16),
+            pltpu.VMEM((2, 2, tokens, tokens), BF16),
+            pltpu.VMEM((tokens, PAIR), F32),
+            pltpu.VMEM((tokens, PAIR), F32),
+            pltpu.VMEM((n, rows, 128), BF16),
+            pltpu.VMEM((tokens, width), F32),
+            pltpu.VMEM(small_shape, F32),
             pltpu.VMEM((n, half, 128), BF16),
             pltpu.VMEM((n, half, 128), BF16),
             pltpu.VMEM((n, planes, quarter, 128), BF16),
             pltpu.VMEM((n, quarter, 128), BF16),
             pltpu.VMEM((n, lines, piece, 128), BF16),
-            pltpu.VMEM((3, most, *small.shape), F32),
+            pltpu.VMEM((3, most, *small_shape), F32),
+            sems((2,)),
+            sems((2,)),
         ]
         + [sems((n,))] * 2
         + [sems((n, planes))] * 2
@@ -1040,51 +1199,63 @@
         + [sems((n,))] * 2
         + [sems((3, most))] * 2,
         compiler_params=pltpu.CompilerParams(
-            vmem_limit_bytes=40 * MIB, collective_id=1, has_side_effects=True
+            vmem_limit_bytes=60 * MIB, collective_id=1, has_side_effects=True
         ),
-        cost_estimate=cost(8 * n * rows * 128, 100e6),
-        name="reduce_all",
-    )(*[g.reshape(rows, 128) for g in grads], small)
-    return out.reshape(n, tiles, width, 128), small
-
-
-def finish_kernel(
-    experts, cap, hidden_ref, gate_ref, place_ref, sums_ref, *refs
-):
-    made_refs = refs[:experts]
-    out_ref = refs[experts]
-    grad_refs = refs[experts + 1 : experts + 5]
-    slot_ref = refs[-1]
+        cost_estimate=cost(16 * pairs * tokens * tokens * 256, 4 * pairs * tokens * tokens),
+        name="tail",
+    )(
+        q, k, v, grad_mixed, delta, x, gain, bias, wq, wk, wv, small2,
+        probs, grad_hidden, dwo.reshape(rows, 128),
+    )
+
+
+def finish_kernel(experts, cap, x_axis, made_ref, hidden_ref, gate_ref, route_ref, sums_ref, *refs):
+    din_refs = refs[:x_axis]
+    dout_refs = refs[x_axis : 2 * x_axis]
+    out_ref, dwo_ref, dwq_ref, dwk_ref, dwv_ref, din_ref, dout_ref, slot_ref = refs[2 * x_axis :]
     tokens, width = hidden_ref.shape
     rows = 256
-    slot_ref[...] = jnp.broadcast_to(slot_col_of(place_ref[...], experts, cap), slot_ref.shape)
+    slot_ref[...] = jnp.broadcast_to(slot_col_of(route_ref[...], experts, cap), slot_ref.shape)
+    slots = experts * cap
 
     def row_block(i, carry):
         at = pl.ds(pl.multiple_of(i * rows, rows), rows)
-        produced = jnp.zeros((rows, width), F32)
-        for e in range(experts):
-            pick = one_hot(iota((rows, cap), 1) + e * cap == slot_ref[at, 0:1])
-            produced = produced + mm(pick, made_refs[e][...])
+        pick = one_hot(iota((rows, slots), 1) == slot_ref[at, 0:1])
+        produced = mm(pick, made_ref[...])
         out_ref[at, :] = (hidden_ref[at, :] + gate_ref[at, 0:1] * produced).astype(BF16)
         return carry
 
     lax.fori_loop(0, tokens // rows, row_block, 0)
-    for w, ref in enumerate(grad_refs):
-        for tile in range(width // 128):
-            ref[:, tile * 128 : (tile + 1) * 128] = sums_ref[w, tile].astype(F32)
-
-
-def finish(made, hidden, gate, place, sums, experts, cap):
+    for tile in range(width // 128):
+        lanes = slice(tile * 128, (tile + 1) * 128)
+        dwo_ref[:, lanes] = sums_ref[0, tile * width : (tile + 1) * width, :].astype(F32)
+        for w, ref in enumerate((dwq_ref, dwk_ref, dwv_ref)):
+            start = (2 * w + tile % 2) * width
+            ref[:, lanes] = sums_ref[1 + tile // 2, start : start + width, :].astype(F32)
+    for out, parts in ((din_ref, din_refs), (dout_ref, dout_refs)):
+        total = parts[0][...].astype(F32)
+        for part in parts[1:]:
+            total = total + part[...].astype(F32)
+        out[...] = total
+
+
+def finish(made, hidden, gate, route, sums, din, dout, experts, cap):
     tokens, width = hidden.shape
+    square = jax.ShapeDtypeStruct((width, width), F32)
     return pl.pallas_call(
-        functools.partial(finish_kernel, experts, cap),
+        functools.partial(finish_kernel, experts, cap, len(din)),
         out_shape=[jax.ShapeDtypeStruct((tokens, width), BF16)]
-        + [jax.ShapeDtypeStruct((width, width), F32)] * 4,
+        + [square] * 4
+        + [jax.ShapeDtypeStruct(din[0].shape, F32), jax.ShapeDtypeStruct(dout[0].shape, F32)],
         scratch_shapes=[pltpu.VMEM((tokens, 128), jnp.int32)],
         compiler_params=params(),
         cost_estimate=cost(2 * tokens * width * experts * cap, 10 * tokens * width),
         name="finish",
-    )(hidden, gate, place, sums, *made)
+    )(made.reshape(-1, width), hidden, gate, route, sums, *din, *dout)
+
+
+def exchange(blocks, axis):
+    return lax.all_to_all(blocks, axis, split_axis=0, concat_axis=0, tiled=True)
 
 
 def shifted(blocks, axis, size, step=1):
@@ -1141,24 +1312,30 @@
     )
     din = shifted(din, "dp", dp_size, 2)
     dout = shifted(dout, "dp", dp_size, 2)
-    made = [made[0]] + [
-        lax.ppermute(made[s], "expert", [(i, (i - s) % experts) for i in range(experts)])
-        for s in range(1, experts)
-    ]
+    made = exchange(made, "expert")
     grad_hidden, grad_mixed, delta, dwo, small2 = middle_back(
         back, gate_grads, hidden, cotangent, mixed, w_output, gain2, bias2,
         proj, embed, routes, place, space, experts, cap,
     )
-    dq, dk, dv = attention_back(q, k, v, grad_mixed, probs, delta, longest)
-    grad_input, dwq, dwk, dwv, small1 = qkv_back(
-        tokens, gain1, bias1, grad_hidden, dq, dk, dv, query_weight, w_key, w_value
+    if can_reduce(width, dp_size, experts):
+        grad_input, sums, small = tail(
+            q, k, v, grad_mixed, probs, delta, tokens, gain1, bias1, grad_hidden,
+            query_weight, w_key, w_value, dwo, small2, longest, dp_size, experts,
+        )
+    else:
+        dq, dk, dv = attention_back(q, k, v, grad_mixed, probs, delta, longest)
+        grad_input, dwq, dwk, dwv, small1 = qkv_back(
+            tokens, gain1, bias1, grad_hidden, dq, dk, dv, query_weight, w_key, w_value
+        )
+        chunks = [dwo]
+        for at in range(0, width // 128, 2):
+            chunks.append(jnp.concatenate([dw[at : at + 2] for dw in (dwq, dwk, dwv)], 0))
+        small = jnp.concatenate([small1, small2], 0)
+        sums, small = lax.psum((jnp.stack(chunks).astype(F32), small), ("dp", "expert"))
+        sums = sums.astype(BF16).reshape(len(chunks), -1, 128)
+    output, dwo, dwq, dwk, dwv, grad_in, grad_out = finish(
+        made, hidden, gate, routes, sums, din, dout, experts, cap
     )
-    sums, small = reduce_all(
-        [dwo, dwq, dwk, dwv], jnp.concatenate([small1, small2], 0), dp_size, experts
-    )
-    output, dwo, dwq, dwk, dwv = finish(made, hidden, gate, place, sums, experts, cap)
-    grad_in = sum(block.astype(F32) for block in din)
-    grad_out = sum(block.astype(F32) for block in dout)
     return (
         output,
         grad_input,

time: 469 us -> 442 us (0.942)
  the two profiles are of different devices: /device:TPU:0 before, /device:TPU:15 now
where the time goes in v3:
time: 442 us; the launch traced here: 435 us
  Pallas kernels  372 us (84%)
  starting transfers between devices  35.8 us (8%)
  local copies, waits for them, and re-layouts  23.7 us (5%)
    pallas_call x1, Pallas kernels, expert(): pl.pallas_call(functools.partial(expert_kernel, experts, x_axis), in_spec...  140 us
    pallas_call x1, Pallas kernels, tail(): pl.pallas_call(functools.partial(tail_kernel, x_axis, experts, longest),...  119 us
    pallas_call x1, Pallas kernels, middle_back(): pl.pallas_call(functools.partial(middle_back_kernel, experts, cap), out_s...  34.9 us
    pallas_call x1, Pallas kernels, attention(): pl.pallas_call(functools.partial(attention_kernel, rows, longest), grid=(...  28.9 us
    all_to_all x1, starting transfers between devices, exchange(): return lax.all_to_all(blocks, axis, split_axis=0, concat_axis=0, tiled=True)  25.6 us
    pallas_call x1, Pallas kernels, middle(): pl.pallas_call(functools.partial(middle_kernel, experts, cap), out_shape=...  22.1 us
    pallas_call x1, Pallas kernels, finish(): pl.pallas_call(functools.partial(finish_kernel, experts, cap, len(din)),...  17.7 us
    unnamed x57, local copies, waits for them, and re-layouts  15.4 us
  transfers between devices with their start and end apart: 10, of which 0 were waited for; matrix products, arithmetic and copies ran while one was open for 2% of the time, Pallas kernels for 48%

profile of v3, /device:TPU:15, one launch (start us, length us, event | category | flops | bytes accessed | tf_op | source)
XLA Modules:
  0.0 434.7 jit_solution(15778814404659484800)
XLA Ops:
  0.6 0.0 copy-start.3
  0.7 0.8 broadcast_compare_fusion
  1.5 0.3 copy.56
  1.8 0.2 copy.53
  2.0 0.9 fusion.1
  3.0 0.0 copy-start.16
  3.0 4.5 %gather_slots.1 = (bf16[256,768]{1,0:T(8,128)(2,1)S(1)}, bf16[256,768]{1,0:T(8,128)(2,1)}, bf16[256,768]{1,0:T(8,128)(2,1)}, bf16[256,768]{1,0:T(8,128)(2,1)}, b...) custom-call(s32[1,1024]{1,0:T(1,128)S(1)} %bitcast.11, ...), custom_call_target="tpu_custom_call" | custom-call | flops 3221225472 | bytes 4718592 | tf_op jit(solution)/shard_map/gather_slots/pallas_call | solution.py:99
  7.5 0.8 copy-done.11
  8.3 1.2 collective-permute-start
  9.5 1.3 collective-permute-start.1
  10.8 1.0 collective-permute-start.2
  11.8 1.3 collective-permute-start.3
  13.1 1.0 collective-permute-start.4
  14.1 0.0 copy-start.1
  14.2 1.0 copy.57.seg_ref
  15.2 1.4 copy-done.4
  16.6 1.3 copy-done.5
  17.9 1.3 copy-done.6
  19.2 1.3 copy-done.7
  20.4 5.2 %qkv.1 = (bf16[1024,768]{1,0:T(8,128)(2,1)S(1)}, bf16[1024,768]{1,0:T(8,128)(2,1)S(1)}, bf16[1024,768]{1,0:T(8,128)(2,1)S(1)}) custom-call(bf16[1024,768]{1,0:T(8,128)(2,1)S(1)} %copy-done.4, f32[1,768]{1,0:T(1,128)S(1)} %broadcast_in_dim.18.gain_ref, f32[1,768]{1,0:T(1,128)S(1)} %broadcast_in_dim.19.bias_ref, bf16[768,768]{1,0:T(8,128)(2,1)S(1)} %copy-done.5, ...), custom_call_target="tpu_custom_call" | custom-call | flops 3623878656 | bytes 9830400 | tf_op jit(solution)/shard_map/qkv/pallas_call | solution.py:134
  25.7 1.1 copy-done.8
  26.8 1.1 copy-done.9
  27.9 1.1 copy-done.10
  29.1 28.9 %attention.1 = (bf16[1024,768]{1,0:T(8,128)(2,1)}, bf16[12,1024,1024]{2,1,0:T(8,128)(2,1)}) custom-call(bf16[1024,768]{1,0:T(8,128)(2,1)} %copy-done.8, bf16[1024,768]{1,0:T(8,128)(2,1)} %copy-done.9, bf16[1024,768]{1,0:T(8,128)(2,1)} %copy-done.10, s32[1024,1]{1,0:T(8,128)} %copy.57.seg_ref), custom_call_target="tpu_custom_call" | custom-call | flops 12884901888 | bytes 25165824 | tf_op jit(solution)/shard_map/attention/pallas_call | solution.py:188
  58.0 1.0 copy.59.route_ref
  59.0 0.6 broadcast_in_dim.20.gain_ref
  59.6 0.6 broadcast_in_dim.21.bias_ref
  60.2 0.2 copy.58
  60.4 0.6 pad.9.embed_ref
  61.0 0.8 pad.8.proj_ref
  61.8 1.2 collective-permute-start.5
  63.0 1.7 collective-permute-start.6
  64.6 22.1 %middle.1 = (f32[1024,768]{1,0:T(8,128)}, f32[1024,128]{1,0:T(8,128)}, bf16[8,256,768]{2,1,0:T(8,128)(2,1)}, f32[8,8,256]{2,1,0:T(8,128)}) custom-call(bf16[1024,768]{1,0:T(8,128)(2,1)} %get-tuple-element.74.mixed_ref, bf16[1024,768]{1,0:T(8,128)(2,1)} %x_ref.4, bf16[768,768]{1,0:T(8,128)(2,1)} %wo_ref.3, f32[1,768]{1,0:T(1,128)} %broadcast_in_dim.20.gain_ref, ...), custom_call_target="tpu_custom_call" | custom-call | flops 4429185024 | bytes 12582912 | tf_op jit(solution)/shard_map/middle/pallas_call | solution.py:331
  86.9 0.7 copy-done.24
  87.6 0.1 copy-done.25
  87.7 0.6 copy-done.26
  88.3 139.5 %expert.1 = (bf16[8,256,768]{2,1,0:T(8,128)(2,1)}, f32[8,8,256]{2,1,0:T(8,128)}, bf16[8,256,768]{2,1,0:T(8,128)(2,1)}, bf16[768,768]{1,0:T(8,128)(2,1)}, bf16[76...) custom-call(bf16[8,256,768]{2,1,0:T(8,128)(2,1)} %get-tuple-element.75.refs_0_, ...), custom_call_target="tpu_custom_call" | custom-call | flops 57982058496 | bytes 18874368 | tf_op jit(solution)/shard_map/expert/pallas_call | solution.py:576
  227.9 25.6 %all-to-all-start = ((bf16[8,256,768]{2,1,0:T(8,128)(2,1)}), bf16[8,256,768]{2,1,0:T(8,128)(2,1)S(1)}, u32[]{:S(2)}, u32[]{:S(2)}) async-start(bf16[8,256,768]{2,1,0:T(8,128)(2,1)} %get-tuple-element.85), calls=%async_computation | async-start | bytes 6291456 | tf_op jit(solution)/shard_map/all_to_all | solution.py:1258
  253.5 0.2 collective-permute-start.7
  253.7 1.2 collective-permute-start.8
  255.0 34.9 %middle_back.1 = (f32[1024,768]{1,0:T(8,128)}, bf16[1024,768]{1,0:T(8,128)(2,1)}, f32[6,8,1024]{2,1,0:T(8,128)}, bf16[6,768,128]{2,1,0:T(8,128)(2,1)}, f32[32,768]{1,0:T(8,128)}) custom-call(bf16[2048,768]{1,0:T(8,128)(2,1)} %bitcast.19, f32[8,8,256]{2,1,0:T(8,128)} %get-tuple-element.89.gate_grads_ref, f32[1024,768]{1,0:T(8,128)} %get-tuple-element.86.hidden_ref, ...), custom_call_target="tpu_custom_call" | custom-call | flops 5637144576 | bytes 15728640 | tf_op jit(solution)/shard_map/middle_back/pallas_call | solution.py:694
  289.9 119.3 %tail.1 = (f32[1024,768]{1,0:T(8,128)}, bf16[4,4608,128]{2,1,0:T(8,128)(2,1)}, f32[40,768]{1,0:T(8,128)}) custom-call(bf16[1024,768]{1,0:T(8,128)(2,1)} %copy-done.8, bf16[1024,768]{1,0:T(8,128)(2,1)} %copy-done.9, bf16[1024,768]{1,0:T(8,128)(2,1)} %copy-done.10, bf16[1024,768]{1,0:T(8,128)(2,1)} %get-tuple-element.90.do_ref, ...), custom_call_target="tpu_custom_call" | custom-call | flops 25769803776 | bytes 25165824 | tf_op jit(solution)/shard_map/tail/pallas_call | solution.py:1166
  409.1 1.3 slice.23
  410.4 1.5 slice_reduce_fusion
  411.9 1.4 slice_bitcast_fusion
  413.3 1.6 copy-done.12
  414.9 17.7 %finish.1 = (bf16[1024,768]{1,0:T(8,128)(2,1)}, f32[768,768]{1,0:T(8,128)}, f32[768,768]{1,0:T(8,128)}, f32[768,768]{1,0:T(8,128)}, f32[768,768]{1,0:T(8,128)}, /*index=5*/f32[768,768]{1,0:T(8,128)}, f32[768,768]{1,0:T(8,128)}) custom-call(bf16[2048,768]{1,0:T(8,128)(2,1)} %bitcast.13, f32[1024,768]{1,0:T(8,128)} %get-tuple-element.86.hidden_ref, ...), custom_call_target="tpu_custom_call" | custom-call | flops 3221225472 | bytes 7864320 | tf_op jit(solution)/shard_map/finish/pallas_call | solution.py:1245
  432.7 1.7 copy.63
  (51 shorter events, 0.1 us)
Async XLA Ops:
  0.6 2.3 copy-start.3
  3.0 4.5 %copy-start = (s32[1024]{0:T(1024)}, s32[1024]{0:T(1024)S(1)}, u32[]{:S(2)}) copy-start(s32[1024]{0:T(1024)S(1)} %get-tuple-element.114) | copy-start | bytes 12292
  3.0 11.2 %copy-start.18 = (f32[768]{0:T(1024)S(1)}, f32[768]{0:T(1024)}, u32[]{:S(2)}) copy-start(f32[768]{0:T(1024)} %param.19) | copy-start | bytes 9220
  3.0 11.2 %copy-start.19 = (f32[768]{0:T(1024)S(1)}, f32[768]{0:T(1024)}, u32[]{:S(2)}) copy-start(f32[768]{0:T(1024)} %param.20) | copy-start | bytes 9220
  3.0 11.2 %copy-start.16 = (s32[1,1024]{1,0:T(1,128)S(1)}, s32[1,1024]{1,0:T(1,128)}, u32[]{:S(2)}) copy-start(s32[1,1024]{1,0:T(1,128)} %param.17) | copy-start | bytes 12292
  7.5 0.8 copy-start.11
  8.3 53.5 %collective-permute-start = (bf16[256,768]{1,0:T(8,128)(2,1)}, bf16[256,768]{1,0:T(8,128)(2,1)S(1)}, u32[]{:S(2)}, u32[]{:S(2)}) collective-permute-start(bf16[256,768]{1,0:T(8,128)(2,1)} %get-tuple-element.78), channel_id=1, source_target_pairs={{0,1},{1,2},{2,3},{3,4},{4,5},{5,6},{6,7},{7,0},{8,9},{9,10},{10,1... | collective-permute-start | bytes 1179656 | tf_op jit(solution)/shard_map/ppermute | solution.py:1265
  9.5 53.5 %collective-permute-start.1 = (bf16[256,768]{1,0:T(8,128)(2,1)}, bf16[256,768]{1,0:T(8,128)(2,1)S(1)}, u32[]{:S(2)}, u32[]{:S(2)}) collective-permute-start(bf16[256,768]{1,0:T(8,128)(2,1)} %get-tuple-element.79), channel_id=1, source_target_pairs={{0,2},{1,3},{2,4},{3,5},{4,6},{5,7},{6,0},{7,1},{8,10},{9,11},{10,... | collective-permute-start | bytes 1179656 | tf_op jit(solution)/shard_map/ppermute | solution.py:1265
  10.8 76.0 %collective-permute-start.2 = (bf16[256,768]{1,0:T(8,128)(2,1)}, bf16[256,768]{1,0:T(8,128)(2,1)S(1)}, u32[]{:S(2)}, u32[]{:S(2)}) collective-permute-start(bf16[256,768]{1,0:T(8,128)(2,1)} %get-tuple-element.80), channel_id=1, source_target_pairs={{0,3},{1,4},{2,5},{3,6},{4,7},{5,0},{6,1},{7,2},{8,11},{9,12},{10,... | collective-permute-start | bytes 1179656 | tf_op jit(solution)/shard_map/ppermute | solution.py:1265
  11.8 75.1 %collective-permute-start.3 = (bf16[256,768]{1,0:T(8,128)(2,1)S(1)}, bf16[256,768]{1,0:T(8,128)(2,1)}, u32[]{:S(2)}, u32[]{:S(2)}) collective-permute-start(bf16[256,768]{1,0:T(8,128)(2,1)S(1)} %get-tuple-element.81), channel_id=1, source_target_pairs={{0,4},{1,5},{2,6},{3,7},{4,0},{5,1},{6,2},{7,3},{8,12},{9,13},{10,... | collective-permute-start | bytes 1179656 | tf_op jit(solution)/shard_map/ppermute | solution.py:1265
  13.1 73.7 %collective-permute-start.4 = (bf16[256,768]{1,0:T(8,128)(2,1)S(1)}, bf16[256,768]{1,0:T(8,128)(2,1)}, u32[]{:S(2)}, u32[]{:S(2)}) collective-permute-start(bf16[256,768]{1,0:T(8,128)(2,1)S(1)} %get-tuple-element.82), channel_id=1, source_target_pairs={{0,5},{1,6},{2,7},{3,0},{4,1},{5,2},{6,3},{7,4},{8,13},{9,14},{10,... | collective-permute-start | bytes 1179656 | tf_op jit(solution)/shard_map/ppermute | solution.py:1265
  14.1 11.5 %copy-start.1 = (f32[1,768]{1,0:T(1,128)}, f32[1,768]{1,0:T(1,128)S(1)}, u32[]{:S(2)}) copy-start(f32[1,768]{1,0:T(1,128)S(1)} %broadcast_in_dim.18.gain_ref) | copy-start | bytes 9220
  14.2 11.5 %copy-start.2 = (f32[1,768]{1,0:T(1,128)}, f32[1,768]{1,0:T(1,128)S(1)}, u32[]{:S(2)}) copy-start(f32[1,768]{1,0:T(1,128)S(1)} %broadcast_in_dim.19.bias_ref) | copy-start | bytes 9220
  15.2 1.4 copy-start.4
  16.6 1.3 copy-start.5
  17.9 1.3 copy-start.6
  19.2 1.3 copy-start.7
  25.7 1.1 copy-start.8
  26.8 1.1 copy-start.9
  27.9 1.1 copy-start.10
  29.1 28.9 %copy-start.15 = (s32[1024,1]{0,1:T(1,128)S(1)}, s32[1024,1]{0,1:T(1,128)}, u32[]{:S(2)}) copy-start(s32[1024,1]{0,1:T(1,128)} %param.18) | copy-start | bytes 12292
  29.1 30.0 %copy-start.20 = (f32[768]{0:T(1024)S(1)}, f32[768]{0:T(1024)}, u32[]{:S(2)}) copy-start(f32[768]{0:T(1024)} %param.25) | copy-start | bytes 9220
  29.1 30.5 %copy-start.21 = (f32[768]{0:T(1024)S(1)}, f32[768]{0:T(1024)}, u32[]{:S(2)}) copy-start(f32[768]{0:T(1024)} %param.26) | copy-start | bytes 9220
  29.1 31.1 %copy-start.14 = (f32[768,16]{0,1:T(8,128)S(1)}, f32[768,16]{0,1:T(8,128)}, u32[]{:S(2)}) copy-start(f32[768,16]{0,1:T(8,128)} %param.27) | copy-start | bytes 147460
  29.1 31.3 %copy-start.17 = (f32[8,16]{1,0:T(8,128)S(1)}, f32[8,16]{1,0:T(8,128)}, u32[]{:S(2)}) copy-start(f32[8,16]{1,0:T(8,128)} %param.28) | copy-start | bytes 1540
  61.8 25.0 %copy-start.22 = (bf16[256,768]{1,0:T(8,128)(2,1)}, bf16[256,768]{1,0:T(8,128)(2,1)S(1)}, u32[]{:S(2)}) copy-start(bf16[256,768]{1,0:T(8,128)(2,1)S(1)} %collective-permute-done.refs_5_) | copy-start | bytes 1179652
  61.8 25.1 %collective-permute-start.5 = (bf16[256,768]{1,0:T(8,128)(2,1)S(1)}, bf16[256,768]{1,0:T(8,128)(2,1)S(1)}, u32[]{:S(2)}, u32[]{:S(2)}) collective-permute-start(bf16[256,768]{1,0:T(8,128)(2,1)S(1)} %get-tuple-element.83), channel_id=1, source_target_pairs={{0,6},{1,7},{2,0},{3,1},{4,2},{5,3},{6,4},{7,5},{8,14},{9,15},{10,... | collective-permute-start | bytes 1179656 | tf_op jit(solution)/shard_map/ppermute | solution.py:1265
  63.0 23.8 %copy-start.23 = (bf16[256,768]{1,0:T(8,128)(2,1)}, bf16[256,768]{1,0:T(8,128)(2,1)S(1)}, u32[]{:S(2)}) copy-start(bf16[256,768]{1,0:T(8,128)(2,1)S(1)} %collective-permute-done.1.refs_6_) | copy-start | bytes 1179652
  63.0 23.9 %collective-permute-start.6 = (bf16[256,768]{1,0:T(8,128)(2,1)S(1)}, bf16[256,768]{1,0:T(8,128)(2,1)S(1)}, u32[]{:S(2)}, u32[]{:S(2)}) collective-permute-start(bf16[256,768]{1,0:T(8,128)(2,1)S(1)} %get-tuple-element.84), channel_id=1, source_target_pairs={{0,7},{1,0},{2,1},{3,2},{4,3},{5,4},{6,5},{7,6},{8,15},{9,8},{10,9... | collective-permute-start | bytes 1179656 | tf_op jit(solution)/shard_map/ppermute | solution.py:1265
  86.8 0.7 copy-start.24
  86.9 0.8 copy-start.25
  87.6 0.8 copy-start.26
  227.9 185.4 %all-to-all-start = ((bf16[8,256,768]{2,1,0:T(8,128)(2,1)}), bf16[8,256,768]{2,1,0:T(8,128)(2,1)S(1)}, u32[]{:S(2)}, u32[]{:S(2)}) async-start(bf16[8,256,768]{2,1,0:T(8,128)(2,1)} %get-tuple-element.85), calls=%async_computation | async-start | bytes 6291456 | tf_op jit(solution)/shard_map/all_to_all | solution.py:1258
  253.5 159.8 %collective-permute-start.7 = (bf16[768,768]{1,0:T(8,128)(2,1)}, bf16[768,768]{1,0:T(8,128)(2,1)}, u32[]{:S(2)}, u32[]{:S(2)}) collective-permute-start(bf16[768,768]{1,0:T(8,128)(2,1)} %get-tuple-element.98), channel_id=1, source_target_pairs={{0,16},{8,24},{16,0},{24,8},{1,17},{9,25},{17,1},{25,9},{2,18},{10... | collective-permute-start | bytes 3538952 | tf_op jit(solution)/shard_map/ppermute | solution.py:1265
  253.7 159.6 %collective-permute-start.8 = (bf16[768,768]{1,0:T(8,128)(2,1)}, bf16[768,768]{1,0:T(8,128)(2,1)}, u32[]{:S(2)}, u32[]{:S(2)}) collective-permute-start(bf16[768,768]{1,0:T(8,128)(2,1)} %get-tuple-element.100), channel_id=1, source_target_pairs={{0,16},{8,24},{16,0},{24,8},{1,17},{9,25},{17,1},{25,9},{2,18},{10... | collective-permute-start | bytes 3538952 | tf_op jit(solution)/shard_map/ppermute | solution.py:1265
  413.3 1.6 copy-start.12
  414.9 17.7 %copy-start.13 = (f32[1024,768]{1,0:T(8,128)S(1)}, f32[1024,768]{1,0:T(8,128)}, u32[]{:S(2)}) copy-start(f32[1024,768]{1,0:T(8,128)} %get-tuple-element.133) | copy-start | bytes 9437188

commit v4 on v3

v4 whole, which is shorter than its diff:
```python
import functools

import jax
import jax.numpy as jnp
from jax import lax
from jax.experimental import pallas as pl
from jax.experimental.pallas import tpu as pltpu
from jax.sharding import PartitionSpec as P

HEAD_DIM = 64
PAIR = 2 * HEAD_DIM
SHARPNESS = 0.25
EXACT = lax.Precision.HIGHEST
BF16 = jnp.bfloat16
F32 = jnp.float32
FAR = -1e30
MIB = 1 << 20
WINDOW = 4
PARTS = 4
OUTPUT_TICK = 4
PARTS_EARLY = 16
PARTS_LOOP = 2
PARTS_DRAIN = 2


def mm(left, right):
    return jnp.dot(left, right, preferred_element_type=F32)


def mm_rows(left, right, precision=None):
    return lax.dot_general(
        left, right, (((0,), (0,)), ((), ())), precision=precision, preferred_element_type=F32
    )


def mm_cols(left, right, precision=None):
    return lax.dot_general(
        left, right, (((1,), (1,)), ((), ())), precision=precision, preferred_element_type=F32
    )


def iota(shape, axis):
    return lax.broadcasted_iota(jnp.int32, shape, axis)


def one_hot(condition):
    return jnp.where(condition, 1.0, 0.0).astype(BF16)


def params(limit=56):
    return pltpu.CompilerParams(vmem_limit_bytes=limit * MIB)


def cost(flops, moved, trans=0):
    return pl.CostEstimate(flops=int(flops), bytes_accessed=int(moved), transcendentals=int(trans))


def spec_all(shape):
    zeros = (0,) * len(shape)
    return pl.BlockSpec(shape, lambda *ids: zeros)


def slot_row_of(route_row, experts, cap):
    tokens = route_row.shape[1]
    padded = max(8, experts)
    hits = one_hot(iota((padded, tokens), 0) == route_row)
    earlier = one_hot(iota((tokens, tokens), 0) < iota((tokens, tokens), 1))
    ranks = mm(hits, earlier)
    rank = jnp.sum(ranks * hits.astype(F32), 0, keepdims=True)
    return route_row * cap + rank.astype(jnp.int32)


def as_row(col):
    rows = col.shape[0]
    eye = iota((rows, rows), 0) == iota((rows, rows), 1)
    return jnp.sum(jnp.where(eye, col, 0.0), 0, keepdims=True)


def as_col(row):
    rows = row.shape[1]
    eye = iota((rows, rows), 0) == iota((rows, rows), 1)
    return jnp.sum(jnp.where(eye, row, 0.0), 1, keepdims=True)


def norm_parts(values):
    average = jnp.mean(values, -1, keepdims=True)
    centred = values - average
    spread = jnp.mean(centred * centred, -1, keepdims=True)
    scale = lax.rsqrt(spread + 1e-05)
    return centred * scale, scale


def norm_back(grad, gain, unit, scale):
    grad_unit = grad * gain
    inner = jnp.mean(grad_unit * unit, -1, keepdims=True)
    return scale * (grad_unit - jnp.mean(grad_unit, -1, keepdims=True) - unit * inner)


def key_window(block, rows, tokens, longest):
    first = max(0, (block * rows - longest + 1) // 128 * 128)
    last = min(tokens, -(-(block * rows + rows - 1 + longest) // 128) * 128)
    return first, last


def attention_back_kernel(
    rows, longest, q_ref, k_ref, v_ref, do_ref, prob_ref, delta_ref,
    dq_ref, dk_ref, dv_ref, dk_sum, dv_sum,
):
    tokens = q_ref.shape[0]
    lane = iota((tokens, PAIR), 1)
    own = (lane < HEAD_DIM, lane >= HEAD_DIM)
    zero = jnp.zeros((), BF16)
    scale = HEAD_DIM**-0.5
    dk_sum[...] = jnp.zeros_like(dk_sum)
    dv_sum[...] = jnp.zeros_like(dv_sum)
    for block in range(tokens // rows):
        first, last = key_window(block, rows, tokens, longest)
        mine = slice(block * rows, (block + 1) * rows)
        values = v_ref[first:last, :]
        dq = jnp.zeros((rows, PAIR), F32)
        dk = jnp.zeros((last - first, PAIR), F32)
        dv = jnp.zeros((last - first, PAIR), F32)
        for h in range(2):
            do_h = jnp.where(own[h][mine], do_ref[mine, :], zero)
            q_h = jnp.where(own[h][mine], q_ref[mine, :], zero)
            k_h = jnp.where(own[h][first:last], k_ref[first:last, :], zero)
            probs = prob_ref[h, first:last, mine]
            grad_probs = mm_cols(values, do_h)
            grad_scores = (
                probs.astype(F32) * (grad_probs - delta_ref[0, h : h + 1, mine])
            ).astype(BF16)
            dq = dq + mm_rows(grad_scores, k_h)
            dk = dk + mm(grad_scores, q_h)
            dv = dv + mm(probs, do_h)
        dq_ref[mine, :] = (dq * scale).astype(BF16)
        dk_sum[first:last, :] += dk
        dv_sum[first:last, :] += dv
    dk_ref[...] = (dk_sum[...] * scale).astype(BF16)
    dv_ref[...] = dv_sum[...].astype(BF16)


def attention_back(q, k, v, grad_mixed, probs, delta, longest):
    tokens, width = q.shape
    pairs = width // PAIR
    rows = 256
    block = pl.BlockSpec((tokens, PAIR), lambda p: (0, p))
    made = jax.ShapeDtypeStruct((tokens, width), BF16)
    return pl.pallas_call(
        functools.partial(attention_back_kernel, rows, longest),
        grid=(pairs,),
        in_specs=[block] * 4
        + [
            pl.BlockSpec((2, tokens, tokens), lambda p: (p, 0, 0)),
            pl.BlockSpec((1, 8, tokens), lambda p: (p, 0, 0)),
        ],
        out_specs=[block] * 3,
        out_shape=[made] * 3,
        scratch_shapes=[pltpu.VMEM((tokens, PAIR), F32)] * 2,
        compiler_params=params(),
        cost_estimate=cost(8 * 2 * pairs * tokens * tokens * 256, 4 * pairs * tokens * tokens),
        name="attention_back",
    )(q, k, v, grad_mixed, probs, delta)


def router_parts(normed, proj_parts, embed, route, experts):
    high, rest = split_two(normed)
    both = mm(high, proj_parts[...])
    low = both[:, 0:128] + (both[:, 128:256] + mm(rest, proj_parts[:, 0:128]))
    low_squares = jnp.sum(low * low, -1, keepdims=True)
    low_scale = lax.rsqrt(jnp.maximum(low_squares, 1.0))
    low_unit = low * low_scale
    squares = jnp.sum(embed * embed, -1, keepdims=True)
    table_scale = lax.rsqrt(jnp.maximum(squares, 1.0))
    table = embed * table_scale
    logits = mm_cols(low_unit, table, EXACT) / SHARPNESS
    lane = iota(logits.shape, 1)
    logits = jnp.where(lane < experts, logits, FAR)
    weights = jnp.exp(logits - jnp.max(logits, -1, keepdims=True))
    probs = weights / jnp.sum(weights, -1, keepdims=True)
    chosen = jnp.where(lane == route, 1.0, 0.0)
    gate = jnp.sum(probs * chosen, -1, keepdims=True)
    return gate, probs, chosen, low, low_squares, low_scale, low_unit, squares, table_scale, table


def clipped_back(grad_unit, raw, scale, squares):
    share = jnp.where(squares > 1.0, 1.0, jnp.where(squares == 1.0, 0.5, 0.0))
    inner = jnp.sum(grad_unit * raw, -1, keepdims=True)
    return scale * grad_unit - share * scale * scale * scale * inner * raw


def col_of(row):
    return as_col(row.astype(F32)).astype(jnp.int32)


def split_two(value):
    high = value.astype(BF16)
    return high, (value - high.astype(F32)).astype(BF16)


def forward_kernel(
    experts, cap, longest,
    route_ref, seg_ref, cot_ref, x_ref, vecs_ref, tables_ref, wq_ref, wk_ref, wv_ref, wo_ref,
    q_ref, k_ref, v_ref, mixed_ref, probs_ref, hidden_ref, gate_ref, slots_ref, gates_ref,
    lines_ref, up_ref,
    weights, q_all, k_all, v_all, mixed_all, prob_buf, hidden_all, gate_all, slots_all,
    gates_all, lines_all, up_all, kept, tags, proj_parts,
    load_sem, store_sem, prob_sem, up_send, up_recv,
):
    tokens, width = x_ref.shape
    pairs = width // PAIR
    rows = 256
    blocks = tokens // rows
    me = lax.axis_index("expert")
    mesh_ids = pl.DeviceIdType.MESH
    loads = [
        pltpu.make_async_copy(ref, weights.at[i], load_sem.at[i])
        for i, ref in enumerate((wq_ref, wk_ref, wv_ref, wo_ref))
    ]
    for load in loads:
        load.start()
    barrier = pltpu.get_barrier_semaphore()

    def greet(s, carry):
        pl.semaphore_signal(
            barrier, inc=1, device_id={"expert": lax.rem(me + s, experts)}, device_id_type=mesh_ids
        )
        return carry

    lax.fori_loop(1, experts, greet, 0)

    route = route_ref[...]
    place = lax.rem(route - me + experts, experts)
    slot = slot_row_of(place, experts, cap)
    lines_all[...] = jnp.zeros_like(lines_all)
    lines_all[0:1, :] = slot
    lines_all[1:2, :] = slot + (route - place) * cap
    lines_all[2:3, :] = route
    pl.semaphore_wait(barrier, experts - 1)

    def up_copy(s):
        to = {"expert": lax.rem(me + s, experts)}
        return pltpu.make_async_remote_copy(
            up_all.at[s], up_ref.at[s], up_send.at[s], up_recv.at[s], to, mesh_ids
        )

    def up_block(s, carry):
        pick = one_hot(iota((cap, tokens), 0) + s * cap == lines_all[0:1, :])
        up_all[s] = mm(pick, cot_ref[...]).astype(BF16)

        @pl.when(s > 0)
        def _():
            up_copy(s).start()

        return carry

    lax.fori_loop(0, experts, up_block, 0)
    stores = []

    def store(src, dst):
        copy = pltpu.make_async_copy(src, dst, store_sem.at[len(stores)])
        copy.start()
        stores.append(copy)

    store(up_all.at[0], up_ref.at[0])
    store(lines_all, lines_ref)
    for load in loads:
        load.wait()

    def qkv_block(i, carry):
        at = pl.ds(pl.multiple_of(i * rows, rows), rows)
        unit, _ = norm_parts(x_ref[at, :].astype(F32))
        normed = (unit * vecs_ref[0:1, :] + vecs_ref[1:2, :]).astype(BF16)
        for w, ref in enumerate((q_all, k_all, v_all)):
            ref[at, :] = mm(normed, weights[w]).astype(BF16)
        lane = iota((rows, PAIR), 1)
        seg = col_of(seg_ref[0:1, at])
        for h in range(2):
            other = (1 - h) * HEAD_DIM
            tags[h, at, :] = jnp.where(lane - other == seg, 1.0, 0.0).astype(BF16)
            k_tag = jnp.where(lane - other == seg, 0.0, FAR)
            k_tag = jnp.where((lane >= other) & (lane < other + 8), k_tag, 0.0)
            tags[2 + h, at, :] = k_tag.astype(BF16)
        return carry

    lax.fori_loop(0, blocks, qkv_block, 0)
    store(q_all, q_ref)
    store(k_all, k_ref)
    store(v_all, v_ref)

    lane = iota((tokens, PAIR), 1)
    own = (lane < HEAD_DIM, lane >= HEAD_DIM)

    def prob_copy(p, at):
        return pltpu.make_async_copy(prob_buf.at[at], probs_ref.at[pl.ds(2 * p, 2)], prob_sem.at[at])

    def pair_step(p, carry):
        buffer = lax.rem(p, 2)

        @pl.when(p >= 2)
        def _():
            prob_copy(p - 2, buffer).wait()

        lanes = pl.ds(pl.multiple_of(p * PAIR, PAIR), PAIR)
        queries = q_all[:, lanes] * jnp.asarray(HEAD_DIM**-0.5, BF16)
        keys = k_all[:, lanes]
        q_h = [jnp.where(own[h], queries, tags[h]) for h in range(2)]
        k_h = [jnp.where(own[h], keys, tags[2 + h]) for h in range(2)]
        for block in range(blocks):
            first, last = key_window(block, rows, tokens, longest)
            mine = slice(block * rows, (block + 1) * rows)
            out = []
            for h in range(2):
                scores = mm_cols(k_h[h][first:last], q_h[h][mine])
                largest = jnp.max(scores, 0, keepdims=True)
                weighted = jnp.exp(scores - largest)
                total = jnp.sum(weighted, 0, keepdims=True)
                probs = (weighted * (1.0 / total)).astype(BF16)
                prob_buf[buffer, h, first:last, mine] = probs
                out.append(mm_rows(probs, v_all[first:last, lanes]))
            mixed_all[mine, lanes] = jnp.where(own[0][mine], out[0], out[1]).astype(BF16)
        prob_copy(p, buffer).start()
        return carry

    lax.fori_loop(0, pairs, pair_step, 0)
    store(mixed_all, mixed_ref)
    high, rest = split_two(tables_ref[0:width, :])
    proj_parts[:, 0:128] = high
    proj_parts[:, 128:256] = rest

    def row_block(i, carry):
        at = pl.ds(pl.multiple_of(i * rows, rows), rows)
        hidden = x_ref[at, :].astype(F32) + mm(mixed_all[at, :], weights[3])
        hidden_all[at, :] = hidden
        unit, _ = norm_parts(hidden)
        normed = unit * vecs_ref[2:3, :] + vecs_ref[3:4, :]
        route_col = col_of(lines_all[2:3, at])
        gate = router_parts(normed, proj_parts, tables_ref[width:, :], route_col, experts)[0]
        gate_all[at, :] = jnp.broadcast_to(gate, (rows, 128))
        high = gate.astype(BF16).astype(F32)
        mid = (gate - high).astype(BF16).astype(F32)
        rest = gate - high - mid
        lane = iota((rows, 128), 1)
        split = jnp.where(lane == 0, high, jnp.where(lane == 1, mid, jnp.where(lane == 2, rest, 0.0)))
        kept[at, 0:width] = normed.astype(BF16)
        kept[at, width : width + 128] = split.astype(BF16)
        return carry

    lax.fori_loop(0, blocks, row_block, 0)
    store(hidden_all, hidden_ref)
    store(gate_all, gate_ref)

    def slot_block(e, carry):
        pick = one_hot(iota((cap, tokens), 0) + e * cap == lines_all[0:1, :])
        got = mm(pick, kept[...])
        slots_all[e] = got[:, 0:width].astype(BF16)
        gates = as_row(jnp.sum(got[:, width : width + 128], 1, keepdims=True))
        gates_all[e] = jnp.broadcast_to(gates, (8, cap))
        return carry

    lax.fori_loop(0, experts, slot_block, 0)
    store(slots_all, slots_ref)
    store(gates_all, gates_ref)
    for p in (pairs - 2, pairs - 1):
        prob_copy(p, p % 2).wait()
    for copy in stores:
        copy.wait()

    def arrived(s, carry):
        up_copy(s).wait()
        return carry

    lax.fori_loop(1, experts, arrived, 0)


def forward(route_row, seg_row, cot, x, vecs, tables, wq, wk, wv, wo, longest, experts, cap):
    tokens, width = x.shape
    pairs = width // PAIR
    local = pl.BlockSpec(memory_space=pltpu.VMEM)
    anywhere = pl.BlockSpec(memory_space=pl.ANY)
    low = jax.ShapeDtypeStruct((tokens, width), BF16)
    chunks = jax.ShapeDtypeStruct((experts, cap, width), BF16)
    out_shape = [
        low,
        low,
        low,
        low,
        jax.ShapeDtypeStruct((2 * pairs, tokens, tokens), BF16),
        jax.ShapeDtypeStruct((tokens, width), F32),
        jax.ShapeDtypeStruct((tokens, 128), F32),
        chunks,
        jax.ShapeDtypeStruct((experts, 8, cap), F32),
        jax.ShapeDtypeStruct((8, tokens), jnp.int32),
        chunks,
    ]
    low_buf = pltpu.VMEM((tokens, width), BF16)
    sems = pltpu.SemaphoreType.DMA
    return pl.pallas_call(
        functools.partial(forward_kernel, experts, cap, longest),
        in_specs=[local] * 6 + [anywhere] * 4,
        out_specs=[anywhere] * len(out_shape),
        out_shape=out_shape,
        scratch_shapes=[
            pltpu.VMEM((4, width, width), BF16),
            low_buf,
            low_buf,
            low_buf,
            low_buf,
            pltpu.VMEM((2, 2, tokens, tokens), BF16),
            pltpu.VMEM((tokens, width), F32),
            pltpu.VMEM((tokens, 128), F32),
            pltpu.VMEM((experts, cap, width), BF16),
            pltpu.VMEM((experts, 8, cap), F32),
            pltpu.VMEM((8, tokens), jnp.int32),
            pltpu.VMEM((experts, cap, width), BF16),
            pltpu.VMEM((tokens, width + 128), BF16),
            pltpu.VMEM((4, tokens, PAIR), BF16),
            pltpu.VMEM((width, 256), BF16),
            sems((4,)),
            sems((10,)),
            sems((2,)),
            sems((experts,)),
            sems((experts,)),
        ],
        compiler_params=pltpu.CompilerParams(
            vmem_limit_bytes=60 * MIB, collective_id=2, has_side_effects=True
        ),
        cost_estimate=cost(8 * pairs * tokens * tokens * 256, 4 * pairs * tokens * tokens),
        name="forward",
    )(route_row, seg_row, cot, x, vecs, tables, wq, wk, wv, wo)


def distance(experts, i):
    near = (i + 1) // 2
    return lax.rem(i % 2 * near + (1 - i % 2) * (experts - near), experts)


def gelu_parts(pre):
    size = jnp.abs(pre)
    t = pl.reciprocal(1.0 + 0.23164189298 * size, approx=False)
    bell = jnp.exp(-0.5 * pre * pre)
    tail = t * (
        0.127414796
        + t * (-0.142248368 + t * (0.7107068705 + t * (-0.7265760135 + t * 0.5307027145)))
    )
    tail = tail * bell
    phi_sum = jnp.where(pre >= 0, 1.0 - tail, tail)
    return phi_sum, pre * bell * 0.3989422804014327


def expert_kernel(experts, x_axis, *refs):
    x_ref, gates_ref, w_in_ref, w_out_ref, up_ref = refs[:5]
    back_ref, gate_grads_ref = refs[5:7]
    rest = refs[7:]
    made_ref = rest[0]
    din_refs = rest[1 : 1 + x_axis]
    dout_refs = rest[1 + x_axis : 1 + 2 * x_axis]
    (
        x_here, up_here, gates_here, back_here, gate_grads_here, made_here,
        active, grad_pre, w_in, w_out, din_got, dout_got,
        load_sem, x_send, x_recv, g_send, g_recv, b_send, b_recv, gg_send, gg_recv,
        d_send, d_recv, e_send, e_recv, store_sem,
    ) = rest[1 + 2 * x_axis :]
    cap, width = x_here.shape[1:]
    hidden = w_in.shape[1]
    me = lax.axis_index("expert")
    dp = lax.axis_index("dp")
    core = lax.rem(dp, 2)
    mesh_ids = pl.DeviceIdType.MESH

    barrier = pltpu.get_barrier_semaphore()

    def greet(s, carry):
        pl.semaphore_signal(
            barrier, inc=1, device_id={"expert": lax.rem(me + s, experts)}, device_id_type=mesh_ids
        )
        return carry

    lax.fori_loop(1, experts, greet, 0)
    pl.semaphore_signal(
        barrier, inc=1, device_id={"dp": dp + 1 - 2 * core}, device_id_type=mesh_ids
    )

    def x_peer(k):
        return {"dp": 2 * lax.rem(dp // 2 + k, x_axis) + core}

    for k in range(1, x_axis):
        pl.semaphore_signal(barrier, inc=1, device_id=x_peer(k), device_id_type=mesh_ids)
    pl.semaphore_wait(barrier, experts + x_axis - 1)

    def out_copy(s):
        to = {"expert": lax.rem(me + s, experts)}
        return (
            pltpu.make_async_remote_copy(
                x_ref.at[s], x_here.at[s], x_send.at[s], x_recv.at[s], to, mesh_ids
            ),
            pltpu.make_async_remote_copy(
                gates_ref.at[s], gates_here.at[s], g_send.at[s], g_recv.at[s], to, mesh_ids
            ),
        )

    def home_copy(s):
        to = {"expert": lax.rem(me + experts - s, experts)}
        return (
            pltpu.make_async_remote_copy(
                back_here.at[s], back_ref.at[s], b_send.at[s], b_recv.at[s], to, mesh_ids
            ),
            pltpu.make_async_remote_copy(
                gate_grads_here.at[s], gate_grads_ref.at[s], gg_send.at[s], gg_recv.at[s], to, mesh_ids
            ),
        )

    nth = functools.partial(distance, experts)
    window = min(WINDOW, experts - 1)

    def send_out(i, carry):
        for copy in out_copy(nth(i)):
            copy.start()
        return carry

    lax.fori_loop(1, 1 + window, send_out, 0)
    loads = [
        pltpu.make_async_copy(x_ref.at[0], x_here.at[0], load_sem.at[0]),
        pltpu.make_async_copy(gates_ref.at[0], gates_here.at[0], load_sem.at[1]),
        pltpu.make_async_copy(w_in_ref, w_in, load_sem.at[2]),
        pltpu.make_async_copy(w_out_ref, w_out, load_sem.at[3]),
    ]
    loads.append(pltpu.make_async_copy(up_ref, up_here, load_sem.at[4]))
    for load in loads:
        load.start()
    for load in loads:
        load.wait()

    step = 512

    def send_home(i, carry):
        for copy in home_copy(nth(i)):
            copy.start()
        return carry

    def chunk(i, carry):
        s = nth(i)

        @pl.when(i > 0)
        def _():
            for copy in out_copy(s):
                copy.wait_recv()

            @pl.when(i + window < experts)
            def _():
                send_out(i + window, 0)

        @pl.when(i == experts - 1)
        def _():
            lax.fori_loop(1, experts - 1, send_home, 0)

        at_rows = pl.ds(pl.multiple_of(s * cap, cap), cap)
        gate = as_col(gates_here[s][0:1, :])
        up = up_here[s].astype(F32)
        scaled = (up * gate).astype(BF16)
        x = x_here[s]
        for at in range(0, hidden, step):
            part = slice(at, at + step)
            pre = mm(x, w_in[:, part])
            grad_active = mm_cols(scaled, w_out[part, :])
            phi_sum, slope = gelu_parts(pre)
            active[at_rows, part] = (pre * phi_sum).astype(BF16)
            grad_pre[at_rows, part] = (grad_active * (phi_sum + slope)).astype(BF16)
        made = mm(active[at_rows, :], w_out[...]).astype(BF16)
        made_here[s] = made
        gate_grad = jnp.sum(up * made.astype(F32), 1, keepdims=True)
        gate_grads_here[s] = jnp.broadcast_to(as_row(gate_grad), (8, cap))
        up_here[s] = scaled
        back_here[s] = mm_cols(grad_pre[at_rows, :], w_in[...]).astype(BF16)

        return carry

    lax.fori_loop(0, experts, chunk, 0)
    send_home(experts - 1, 0)
    stores = [
        pltpu.make_async_copy(back_here.at[0], back_ref.at[0], store_sem.at[0]),
        pltpu.make_async_copy(gate_grads_here.at[0], gate_grads_ref.at[0], store_sem.at[1]),
    ]
    for s in range(experts):
        home = lax.rem(me + experts - s, experts)
        stores.append(
            pltpu.make_async_copy(made_here.at[s], made_ref.at[home], store_sem.at[2 + s])
        )
    for store in stores:
        store.start()

    block = hidden // (2 * x_axis)
    slots = experts * cap
    other = {"dp": dp + 1 - 2 * core}
    x_all = x_here.reshape(slots, width)
    up_all = up_here.reshape(slots, width)

    def block_start(k, for_core):
        x_at = lax.rem(dp // 2 + k, x_axis)
        return pl.multiple_of((2 * x_at + for_core) * block, 128)

    def din_out(k):
        return w_in.at[:, k * block : (k + 1) * block]

    def dout_out(k):
        return w_out.at[k * block : (k + 1) * block]

    def core_copies(k):
        return (
            pltpu.make_async_remote_copy(
                din_out(k), din_got.at[k], d_send.at[k], d_recv.at[k], other, mesh_ids
            ),
            pltpu.make_async_remote_copy(
                dout_out(k),
                dout_got.at[k],
                d_send.at[x_axis + k],
                d_recv.at[x_axis + k],
                other,
                mesh_ids,
            ),
        )

    tile = 256 if block % 256 == 0 else 128

    def in_grads(k, for_core, out, got):
        start = block_start(k, for_core)
        columns = slice(out * block, (out + 1) * block)
        for at in range(0, width, tile):
            part = slice(at, at + tile)
            value = mm_rows(x_all[:, part], grad_pre[:, pl.ds(start, block)])
            if got is not None:
                value = value + din_got[got, part, :].astype(F32)
            w_in[part, columns] = value.astype(BF16)

    def out_grads(k, for_core, out, got):
        start = block_start(k, for_core)
        for at in range(0, block, tile):
            value = mm_rows(active[:, pl.ds(pl.multiple_of(start + at, 128), tile)], up_all[...])
            if got is not None:
                value = value + dout_got[got, at : at + tile, :].astype(F32)
            w_out[out * block + at : out * block + at + tile, :] = value.astype(BF16)

    def x_copies(k):
        return (
            pltpu.make_async_remote_copy(
                din_out(x_axis + k), din_refs[k], e_send.at[k], e_recv.at[k], x_peer(k), mesh_ids
            ),
            pltpu.make_async_remote_copy(
                dout_out(x_axis + k),
                dout_refs[k],
                e_send.at[x_axis + k],
                e_recv.at[x_axis + k],
                x_peer(k),
                mesh_ids,
            ),
        )

    for k in [*range(1, x_axis), 0]:
        in_copy, out_copy_k = core_copies(k)
        in_grads(k, 1 - core, k, None)
        in_copy.start()
        out_grads(k, 1 - core, k, None)
        out_copy_k.start()
        in_copy.wait_recv()
        in_grads(k, core, x_axis + k, k)
        if k:
            x_copies(k)[0].start()
        out_copy_k.wait_recv()
        out_grads(k, core, x_axis + k, k)
        if k:
            x_copies(k)[1].start()
    for i, (src, ref) in enumerate(
        ((din_out(x_axis), din_refs[0]), (dout_out(x_axis), dout_refs[0]))
    ):
        store = pltpu.make_async_copy(src, ref, store_sem.at[2 + experts + i])
        store.start()
        stores.append(store)
    for k in range(1, x_axis):
        for copy in x_copies(k):
            copy.wait()
    for store in stores:
        store.wait()
    for k in range(x_axis):
        for copy in core_copies(k):
            copy.wait_send()

    def finish(s, carry):
        for copy in out_copy(s):
            copy.wait_send()
        for copy in home_copy(s):
            copy.wait()
        return carry

    lax.fori_loop(1, experts, finish, 0)


def expert(x, gates, up, w_in, w_out, dp_size):
    experts, cap, width = x.shape
    hidden = w_in.shape[1]
    slots = experts * cap
    x_axis = dp_size // 2
    block = hidden // dp_size
    anywhere = pl.BlockSpec(memory_space=pl.ANY)
    rows = jax.ShapeDtypeStruct((experts, cap, width), BF16)
    out_shape = (
        [rows, jax.ShapeDtypeStruct((experts, 8, cap), F32), rows]
        + [jax.ShapeDtypeStruct((width, block), BF16)] * x_axis
        + [jax.ShapeDtypeStruct((block, width), BF16)] * x_axis
    )
    chunks = pltpu.VMEM((experts, cap, width), BF16)
    lines = pltpu.VMEM((experts, 8, cap), F32)
    sems = pltpu.SemaphoreType.DMA
    out = pl.pallas_call(
        functools.partial(expert_kernel, experts, x_axis),
        in_specs=[anywhere] * 5,
        out_specs=[anywhere] * len(out_shape),
        out_shape=out_shape,
        scratch_shapes=[
            chunks,
            chunks,
            lines,
            chunks,
            lines,
            chunks,
            pltpu.VMEM((slots, hidden), BF16),
            pltpu.VMEM((slots, hidden), BF16),
            pltpu.VMEM((width, hidden), BF16),
            pltpu.VMEM((hidden, width), BF16),
            pltpu.VMEM((x_axis, width, block), BF16),
            pltpu.VMEM((x_axis, block, width), BF16),
            sems((5,)),
        ]
        + [sems((experts,))] * 8
        + [sems((2 * x_axis,))] * 4
        + [sems((4 + experts,))],
        compiler_params=pltpu.CompilerParams(
            vmem_limit_bytes=63 * MIB, collective_id=0, has_side_effects=True
        ),
        cost_estimate=cost(12 * slots * width * hidden, 8 * width * hidden),
        name="expert",
    )(x, gates, w_in, w_out, up)
    back, gate_grads, made = out[:3]
    din = out[3 : 3 + x_axis]
    dout = out[3 + x_axis :]
    return back, gate_grads, made, din, dout


def store_tiles(out_ref, value):
    for tile in range(out_ref.shape[0]):
        out_ref[tile] = value[:, tile * 128 : (tile + 1) * 128].astype(BF16)


def middle_back_kernel(
    experts, cap, back_ref, gate_grads_ref, lines_ref, hidden_ref, cot_ref, mixed_ref, wo_ref,
    gain_ref, bias_ref, proj_ref, embed_ref,
    grad_hidden_ref, grad_mixed_ref, delta_ref, dwo_ref, small_ref,
    dwo_sum, dproj_sum, dembed_sum, gate_parts, proj_parts,
):
    step = pl.program_id(0)
    rows, width = hidden_ref.shape
    slots = back_ref.shape[0]

    @pl.when(step == 0)
    def _():
        small_ref[...] = jnp.zeros_like(small_ref)
        dwo_sum[...] = jnp.zeros_like(dwo_sum)
        dproj_sum[...] = jnp.zeros_like(dproj_sum)
        dembed_sum[...] = jnp.zeros_like(dembed_sum)
        high, rest = split_two(proj_ref[...])
        proj_parts[:, 0:128] = high
        proj_parts[:, 128:256] = rest
        line = iota((16, cap), 0)
        for e in range(experts):
            grads = gate_grads_ref[e, 0:1, :]
            high = grads.astype(BF16).astype(F32)
            mid = (grads - high).astype(BF16).astype(F32)
            rest = grads - high - mid
            split = jnp.where(line == 0, high, jnp.where(line == 1, mid, rest))
            gate_parts[:, e * cap : (e + 1) * cap] = jnp.where(line < 3, split, 0.0).astype(BF16)

    heads = width // HEAD_DIM
    pairs = heads // 2
    head_of = iota((8 * pairs, width), 1) // HEAD_DIM
    line = iota((8 * pairs, width), 0)
    head_lines = one_hot((head_of == line // 8 * 2 + line % 8) & (line % 8 < 2))
    pick = one_hot(iota((rows, slots), 1) == col_of(lines_ref[0:1, :]))
    grad = mm(pick, back_ref[...])
    gate_grad = jnp.sum(mm_cols(pick, gate_parts[...]), 1, keepdims=True)
    unit, scale = norm_parts(hidden_ref[...])
    normed = unit * gain_ref[...] + bias_ref[...]
    gate, probs, chosen, low, low_squares, low_scale, low_unit, _, _, table = router_parts(
        normed, proj_parts, embed_ref[...], col_of(lines_ref[2:3, :]), experts
    )
    grad_logits = (gate_grad * gate * (chosen - probs) / SHARPNESS).astype(BF16)
    grad_unit = mm(grad_logits, table.astype(BF16))
    dembed_sum[...] += mm_rows(grad_logits, low_unit.astype(BF16))
    grad_low = clipped_back(grad_unit, low, low_scale, low_squares).astype(BF16)
    dproj_sum[...] += mm_rows(grad_low, normed.astype(BF16))
    grad = grad + mm_cols(grad_low, proj_parts[:, 0:128])
    small_ref[0:1, :] += jnp.sum(grad * unit, 0, keepdims=True)
    small_ref[1:2, :] += jnp.sum(grad, 0, keepdims=True)
    grad_hidden = cot_ref[...].astype(F32) + norm_back(grad, gain_ref[...], unit, scale)
    grad_hidden_ref[...] = grad_hidden
    low_grad = grad_hidden.astype(BF16)
    grad_mixed = mm_cols(low_grad, wo_ref[...]).astype(BF16)
    grad_mixed_ref[...] = grad_mixed
    dwo_sum[...] += mm_rows(mixed_ref[...], low_grad)
    high, rest = split_two(grad_mixed.astype(F32) * mixed_ref[...].astype(F32))
    sums = mm_cols(head_lines, high) + mm_cols(head_lines, rest)
    for p in range(pairs):
        delta_ref[p] = sums[8 * p : 8 * p + 8, :]

    @pl.when(step == pl.num_programs(0) - 1)
    def _():
        embed = embed_ref[...]
        squares = jnp.sum(embed * embed, -1, keepdims=True)
        table_scale = lax.rsqrt(jnp.maximum(squares, 1.0))
        dembed = clipped_back(dembed_sum[...], embed, table_scale, squares)
        lines_proj = small_ref.shape[0] - 8 - max(8, experts)
        small_ref[8 : 8 + lines_proj, :] = dproj_sum[0:lines_proj, :]
        small_ref[8 + lines_proj :, 0:128] = dembed[0 : max(8, experts), :]
        store_tiles(dwo_ref, dwo_sum[...])


def middle_back(
    back, gate_grads, lines, hidden, cot, mixed, wo, gain, bias, proj, embed, space, experts, cap
):
    tokens, width = hidden.shape
    slots = experts * cap
    rows = 256
    back = back.reshape(slots, width)
    block = pl.BlockSpec((rows, width), lambda i: (i, 0))
    tiles = width // 128
    small_shape = (8 + space + max(8, experts), width)
    args = (back, gate_grads, lines, hidden, cot, mixed, wo, gain, bias, proj, embed)
    return pl.pallas_call(
        functools.partial(middle_back_kernel, experts, cap),
        grid=(tokens // rows,),
        in_specs=[
            spec_all(back.shape),
            spec_all(gate_grads.shape),
            pl.BlockSpec((8, rows), lambda i: (0, i)),
            block,
            block,
            block,
        ]
        + [spec_all(a.shape) for a in args[6:]],
        out_specs=[
            block,
            block,
            pl.BlockSpec((tiles, 8, rows), lambda i: (0, 0, i)),
            spec_all((tiles, width, 128)),
            spec_all(small_shape),
        ],
        out_shape=[
            jax.ShapeDtypeStruct((tokens, width), F32),
            jax.ShapeDtypeStruct((tokens, width), BF16),
            jax.ShapeDtypeStruct((tiles, 8, tokens), F32),
            jax.ShapeDtypeStruct((tiles, width, 128), BF16),
            jax.ShapeDtypeStruct(small_shape, F32),
        ],
        scratch_shapes=[
            pltpu.VMEM((width, width), F32),
            pltpu.VMEM((128, width), F32),
            pltpu.VMEM((128, 128), F32),
            pltpu.VMEM((16, slots), BF16),
            pltpu.VMEM((width, 256), BF16),
        ],
        compiler_params=params(),
        cost_estimate=cost(2 * tokens * width * (2 * width + slots), 20 * tokens * width),
        name="middle_back",
    )(*args)


def qkv_back_kernel(
    x_ref, gain_ref, bias_ref, grad_hidden_ref, dq_ref, dk_ref, dv_ref, wq_ref, wk_ref, wv_ref,
    grad_ref, dwq_ref, dwk_ref, dwv_ref, small_ref, low_ref,
):
    tokens, width = x_ref.shape
    rows = 256
    small_ref[...] = jnp.zeros_like(small_ref)

    def row_block(i, carry):
        at = pl.ds(pl.multiple_of(i * rows, rows), rows)
        unit, scale = norm_parts(x_ref[at, :].astype(F32))
        low_ref[at, :] = (unit * gain_ref[...] + bias_ref[...]).astype(BF16)
        grad = (
            mm_cols(dq_ref[at, :], wq_ref[...])
            + mm_cols(dk_ref[at, :], wk_ref[...])
            + mm_cols(dv_ref[at, :], wv_ref[...])
        )
        small_ref[0:1, :] += jnp.sum(grad * unit, 0, keepdims=True)
        small_ref[1:2, :] += jnp.sum(grad, 0, keepdims=True)
        grad_ref[at, :] = grad_hidden_ref[at, :] + norm_back(grad, gain_ref[...], unit, scale)
        return carry

    lax.fori_loop(0, tokens // rows, row_block, 0)
    low = low_ref[...]
    store_tiles(dwq_ref, mm_rows(low, dq_ref[...]))
    store_tiles(dwk_ref, mm_rows(low, dk_ref[...]))
    store_tiles(dwv_ref, mm_rows(low, dv_ref[...]))


def qkv_back(x, gain, bias, grad_hidden, dq, dk, dv, wq, wk, wv):
    tokens, width = x.shape
    square = jax.ShapeDtypeStruct((width // 128, width, 128), BF16)
    return pl.pallas_call(
        qkv_back_kernel,
        out_shape=[
            jax.ShapeDtypeStruct((tokens, width), F32),
            square,
            square,
            square,
            jax.ShapeDtypeStruct((8, width), F32),
        ],
        scratch_shapes=[pltpu.VMEM((tokens, width), BF16)],
        compiler_params=params(),
        cost_estimate=cost(12 * tokens * width * width, 20 * tokens * width),
        name="qkv_back",
    )(x, gain, bias, grad_hidden, dq, dk, dv, wq, wk, wv)


def add_rows(rows, out_ref, out_at, terms):
    step = next(step for step in (320, 160, 80, 48, 16) if rows % step == 0)

    def body(i, carry):
        at = i * step
        total = None
        for ref, start in terms:
            value = ref[pl.ds(pl.multiple_of(start + at, 16), step), :].astype(F32)
            total = value if total is None else total + value
        out_ref[pl.ds(pl.multiple_of(out_at + at, 16), step), :] = total.astype(out_ref.dtype)
        return carry

    lax.fori_loop(0, rows // step, body, 0)


def can_reduce(width, space, dp_size, experts):
    spare = chunk_rows(width, dp_size, experts) - 3 * width
    lines2 = 8 + space + max(8, experts)
    return (
        width // 128 % 2 == 0
        and 64 * dp_size * experts <= 3 * width
        and spare >= width // 128 * lines2
    )


def chunk_rows(width, dp_size, experts):
    unit = 16 * dp_size * experts
    return -(-3 * width // unit) * unit


def tail_kernel(
    x_axis, experts, longest,
    x_ref, vecs_ref, tables_ref, lines_ref, gate_grads_ref, gate_ref,
    q_hbm, k_hbm, v_hbm, wq_hbm, wk_hbm, wv_hbm, wo_hbm, probs_ref, back_hbm, hidden_hbm,
    cot_hbm, mixed_hbm, made_hbm,
    grad_hbm, sums_hbm, output_hbm, small_out, small_out2,
    q_ref, k_ref, v_ref, do_ref, weights, out_ref, made_home, hidden_part, delta_ref, small_ref,
    dproj_sum, dembed_sum, gate_parts, proj_parts,
    dq_all, dk_all, dv_all, normed_t, prob_buf, dk_sum, dv_sum, grads, grad_hidden, small_in,
    core_got, core_sum, plane_got, plane_sum, line_got, small_got,
    load_sem, prob_sem, sums_sem, grad_sem, hidden_sem, made_send, made_recv,
    core_send, core_recv, plane_send, plane_recv, line_send, line_recv,
    line_back_send, line_back_recv, plane_back_send, plane_back_recv,
    core_back_send, core_back_recv, small_send, small_recv,
):
    tokens, width = x_ref.shape
    pairs = width // PAIR
    n = grads.shape[0]
    block_rows = 256
    dp = lax.axis_index("dp")
    me = lax.axis_index("expert")
    core = lax.rem(dp, 2)
    x_at = dp // 2
    low = lax.rem(me, 2)
    high = me // 2
    planes, lines = 2 * x_axis, experts // 2
    mesh_ids = pl.DeviceIdType.MESH
    rows = grads.shape[1]
    half = rows // 2
    quarter = half // planes
    piece = quarter // lines
    plane_at = x_at * 2 + low

    other_core = {"dp": dp + 1 - 2 * core}

    def plane_peer(j):
        at = lax.rem(plane_at + j, planes)
        return at, (2 * (at // 2) + core, 2 * high + lax.rem(at, 2))

    def line_peer(j):
        at = lax.rem(high + j, lines)
        return at, {"expert": 2 * at + low}

    barrier = pltpu.get_barrier_semaphore()
    pl.semaphore_signal(barrier, inc=1, device_id=other_core, device_id_type=mesh_ids)
    for j in range(1, planes):
        pl.semaphore_signal(barrier, inc=1, device_id=plane_peer(j)[1], device_id_type=mesh_ids)
    for j in range(1, lines):
        pl.semaphore_signal(barrier, inc=1, device_id=line_peer(j)[1], device_id_type=mesh_ids)

    def expert_peer(j):
        return lax.rem(me + j, experts)

    for j in range(1, experts):
        pl.semaphore_signal(
            barrier, inc=1, device_id={"expert": expert_peer(j)}, device_id_type=mesh_ids
        )

    def remote(src, dst, send, recv, to):
        return pltpu.make_async_remote_copy(src, dst, send, recv, to, mesh_ids)

    def rows_at(start, size):
        return pl.ds(pl.multiple_of(start, 16), size)

    def core_copy(c):
        src = grads.at[c, rows_at((1 - core) * half, half)]
        return [remote(src, core_got.at[c], core_send.at[c], core_recv.at[c], other_core)]

    def plane_copies(c):
        made = []
        for j in range(1, planes):
            at, to = plane_peer(j)
            src = core_sum.at[c, rows_at(at * quarter, quarter)]
            made.append(
                remote(src, plane_got.at[c, j - 1], plane_send.at[c, j], plane_recv.at[c, j], to)
            )
        return made

    def line_copies(c):
        made = []
        for j in range(1, lines):
            at, to = line_peer(j)
            src = plane_sum.at[c, rows_at(at * piece, piece)]
            made.append(remote(src, line_got.at[c, j - 1], line_send.at[c, j], line_recv.at[c, j], to))
        return made

    base = core * half + plane_at * quarter

    def line_back(c):
        at = rows_at(base + high * piece, piece)
        made = []
        for j in range(1, lines):
            to = line_peer(j)[1]
            made.append(
                remote(
                    out_ref.at[c, at],
                    out_ref.at[c, at],
                    line_back_send.at[c, j],
                    line_back_recv.at[c, j],
                    to,
                )
            )
        return made

    def plane_back(c):
        at = rows_at(base, quarter)
        made = []
        for j in range(1, planes):
            to = plane_peer(j)[1]
            made.append(
                remote(
                    out_ref.at[c, at],
                    out_ref.at[c, at],
                    plane_back_send.at[c, j],
                    plane_back_recv.at[c, j],
                    to,
                )
            )
        return made

    def core_back(c):
        at = rows_at(core * half, half)
        return [
            remote(
                out_ref.at[c, at],
                out_ref.at[c, at],
                core_back_send.at[c],
                core_back_recv.at[c],
                other_core,
            )
        ]

    def small_copies(stage):
        made = []
        if stage == 0:
            made.append(
                remote(
                    small_got.at[0, 0],
                    small_got.at[0, 1],
                    small_send.at[0, 1],
                    small_recv.at[0, 1],
                    other_core,
                )
            )
        else:
            for j in range(1, planes if stage == 1 else lines):
                to = plane_peer(j)[1] if stage == 1 else line_peer(j)[1]
                made.append(
                    remote(
                        small_got.at[stage, 0],
                        small_got.at[stage, j],
                        small_send.at[stage, j],
                        small_recv.at[stage, j],
                        to,
                    )
                )
        return made

    def start(copies):
        for copy in copies:
            copy.start()

    def received(copies):
        for copy in copies:
            copy.wait_recv()

    def ordered(got, at, count):
        total = None
        for i in range(count):
            value = got(lax.rem(at + count - i, count))
            total = value if total is None else total + value
        return total

    def stage_run(stage, c):
        if stage == 0:
            start(core_copy(c))
        elif stage == 1:
            received(core_copy(c))
            add_rows(
                half, core_sum.at[c], 0, [(grads.at[c], core * half), (core_got.at[c], 0)]
            )
            start(plane_copies(c))
        elif stage == 2:
            received(plane_copies(c))
            add_rows(
                quarter,
                plane_sum.at[c],
                0,
                [(core_sum.at[c], plane_at * quarter)]
                + [(plane_got.at[c, j - 1], 0) for j in range(1, planes)],
            )
            start(line_copies(c))
        elif stage == 3:
            received(line_copies(c))
            add_rows(
                piece,
                out_ref.at[c],
                base + high * piece,
                [(plane_sum.at[c], high * piece)]
                + [(line_got.at[c, j - 1], 0) for j in range(1, lines)],
            )
            start(line_back(c))
        elif stage == 4:
            received(line_back(c))
            start(plane_back(c))
        elif stage == 5:
            received(plane_back(c))
            start(core_back(c))
        else:
            received(core_back(c))
            sums_copy(c).start()

    def sums_copy(c):
        return pltpu.make_async_copy(out_ref.at[c], sums_hbm.at[c], sums_sem.at[c])

    def small_run(stage):
        if stage == 0:
            small_got[0, 0] = small_in[...]
            start(small_copies(0))
        elif stage == 1:
            received(small_copies(0))
            small_got[1, 0] = small_got[0, 0] + small_got[0, 1]
            start(small_copies(1))
        elif stage == 2:
            received(small_copies(1))
            small_got[2, 0] = ordered(lambda j: small_got[1, j], plane_at, planes)
            start(small_copies(2))
        elif stage == 3:
            received(small_copies(2))
            small_out[...] = ordered(lambda j: small_got[2, j], high, lines)


    def prob_copy(p, slot):
        return pltpu.make_async_copy(
            probs_ref.at[pl.ds(2 * p, 2)], prob_buf.at[slot], prob_sem.at[slot]
        )

    full = 3 * width
    experts_cap = made_home.shape[1]
    slots = experts * experts_cap
    gain1, bias1 = vecs_ref[0:1, :], vecs_ref[1:2, :]
    gain2, bias2 = vecs_ref[2:3, :], vecs_ref[3:4, :]
    back_buf = prob_buf.at[1, :, :, 0:width]
    sources = [
        (back_hbm, back_buf),
        (hidden_hbm, grad_hidden),
        (cot_hbm, dq_all),
        (mixed_hbm, dv_all),
        (wo_hbm, weights.at[3]),
        (q_hbm, q_ref),
        (k_hbm, k_ref),
        (v_hbm, v_ref),
        (wq_hbm, weights.at[0]),
        (wk_hbm, weights.at[1]),
        (wv_hbm, weights.at[2]),
        (made_hbm.at[me], made_home.at[me]),
    ]
    loads = [
        pltpu.make_async_copy(src, dst, load_sem.at[i]) for i, (src, dst) in enumerate(sources)
    ]
    for load in loads:
        load.start()
    prob_copy(0, 0).start()
    pl.semaphore_wait(barrier, planes + lines - 1 + experts - 1)

    parts = PARTS * (experts - 1)
    early = min(PARTS_EARLY, parts)

    def made_copy(m):
        to = expert_peer(distance(experts, m // PARTS + 1))
        at = rows_at(m % PARTS * (experts_cap // PARTS), experts_cap // PARTS)
        return remote(
            made_hbm.at[to, at],
            made_home.at[me, at],
            made_send.at[m],
            made_recv.at[m],
            {"expert": to},
        )

    def made_start(m, carry):
        made_copy(m).start()
        return carry

    def made_received(m, carry):
        made_copy(m).wait_recv()
        return carry

    def made_sent(m, carry):
        made_copy(m).wait_send()
        return carry

    lax.fori_loop(0, early, made_start, 0)

    for c in range(n):
        grads[c, full:rows, :] = jnp.zeros((rows - full, 128), BF16)
    small_ref[...] = jnp.zeros_like(small_ref)
    dproj_sum[...] = jnp.zeros_like(dproj_sum)
    dembed_sum[...] = jnp.zeros_like(dembed_sum)
    upper, rest = split_two(tables_ref[0:width, :])
    proj_parts[:, 0:128] = upper
    proj_parts[:, 128:256] = rest
    split_line = iota((16, experts_cap), 0)
    for e in range(experts):
        line_grads = gate_grads_ref[e, 0:1, :]
        upper = line_grads.astype(BF16).astype(F32)
        mid = (line_grads - upper).astype(BF16).astype(F32)
        rest = line_grads - upper - mid
        split = jnp.where(split_line == 0, upper, jnp.where(split_line == 1, mid, rest))
        gate_parts[:, e * experts_cap : (e + 1) * experts_cap] = jnp.where(
            split_line < 3, split, 0.0
        ).astype(BF16)
    head_of = iota((8 * pairs, width), 1) // HEAD_DIM
    line = iota((8 * pairs, width), 0)
    head_lines = one_hot((head_of == line // 8 * 2 + line % 8) & (line % 8 < 2))
    embed = tables_ref[width:, :]
    for load in loads[0:5]:
        load.wait()

    def middle_block(i, carry):
        at = pl.ds(pl.multiple_of(i * block_rows, block_rows), block_rows)
        pick = one_hot(iota((block_rows, slots), 1) == col_of(lines_ref[0:1, at]))
        grad = mm(pick[:, 0:tokens], prob_buf[1, 0, :, 0:width])
        grad = grad + mm(pick[:, tokens:], prob_buf[1, 1, :, 0:width])
        gate_grad = jnp.sum(mm_cols(pick, gate_parts[...]), 1, keepdims=True)
        unit, unit_scale = norm_parts(grad_hidden[at, :])
        normed = unit * gain2 + bias2
        gate, probs, chosen, low, low_squares, low_scale, low_unit, _, _, table = router_parts(
            normed, proj_parts, embed, col_of(lines_ref[2:3, at]), experts
        )
        grad_logits = (gate_grad * gate * (chosen - probs) / SHARPNESS).astype(BF16)
        grad_unit = mm(grad_logits, table.astype(BF16))
        dembed_sum[...] += mm_rows(grad_logits, low_unit.astype(BF16))
        grad_low = clipped_back(grad_unit, low, low_scale, low_squares).astype(BF16)
        dproj_sum[...] += mm_rows(grad_low, normed.astype(BF16))
        grad = grad + mm_cols(grad_low, proj_parts[:, 0:128])
        small_ref[0:1, :] += jnp.sum(grad * unit, 0, keepdims=True)
        small_ref[1:2, :] += jnp.sum(grad, 0, keepdims=True)
        total_grad = dq_all[at, :].astype(F32) + norm_back(grad, gain2, unit, unit_scale)
        grad_hidden[at, :] = total_grad
        low_grad = total_grad.astype(BF16)
        dk_all[at, :] = low_grad
        grad_mixed = mm_cols(low_grad, weights[3]).astype(BF16)
        do_ref[at, :] = grad_mixed
        high, rest = split_two(grad_mixed.astype(F32) * dv_all[at, :].astype(F32))
        lines_sum = mm_cols(head_lines, high) + mm_cols(head_lines, rest)
        for p in range(pairs):
            delta_ref[p, :, at] = lines_sum[8 * p : 8 * p + 8, :]
        return carry

    lax.fori_loop(0, tokens // block_rows, middle_block, 0)
    squares = jnp.sum(embed * embed, -1, keepdims=True)
    table_scale = lax.rsqrt(jnp.maximum(squares, 1.0))
    dembed = clipped_back(dembed_sum[...], embed, table_scale, squares)
    lines2 = small_ref.shape[0]
    lines_proj = lines2 - 8 - max(8, experts)
    small_ref[8 : 8 + lines_proj, :] = dproj_sum[0:lines_proj, :]
    small_ref[8 + lines_proj :, 0:128] = dembed[0 : max(8, experts), :]
    for tile in range(width // 128):
        at = full + tile * lines2
        grads[0, at : at + lines2, :] = small_ref[:, tile * 128 : (tile + 1) * 128].astype(BF16)
    half_tiles = width // 256
    for wide in range(half_tiles):
        made = mm_rows(dv_all[...], dk_all[:, wide * 256 : (wide + 1) * 256]).astype(BF16)
        for i in range(2):
            tile = 2 * wide + i
            start_at = tile % half_tiles * width
            grads[tile // half_tiles, start_at : start_at + width, :] = made[
                :, i * 128 : (i + 1) * 128
            ]
        if wide == (half_tiles - 1) // 2:
            stage_run(0, 0)
    for at in range(0, tokens, block_rows):
        part = slice(at, at + block_rows)
        unit, _ = norm_parts(x_ref[part, :].astype(F32))
        normed = unit * gain1 + bias1
        normed_t[:, part] = normed.T.astype(BF16)
    stage_run(1, 0)
    stage_run(0, 1)
    for load in loads[5:8]:
        load.wait()
    scale = HEAD_DIM**-0.5
    lane = iota((tokens, PAIR), 1)
    own = (lane < HEAD_DIM, lane >= HEAD_DIM)
    zero = jnp.zeros((), BF16)

    def pair_step(p, carry):
        slot = lax.rem(p, 2)
        prob_copy(p, slot).wait()

        @pl.when(p < pairs - 1)
        def _():
            prob_copy(p + 1, 1 - slot).start()

        lanes = pl.ds(pl.multiple_of(p * PAIR, PAIR), PAIR)
        dk_sum[...] = jnp.zeros_like(dk_sum)
        dv_sum[...] = jnp.zeros_like(dv_sum)
        for block in range(tokens // block_rows):
            first, last = key_window(block, block_rows, tokens, longest)
            mine = slice(block * block_rows, (block + 1) * block_rows)
            values = v_ref[first:last, lanes]
            keys = k_ref[first:last, lanes]
            queries = q_ref[mine, lanes]
            grad_out = do_ref[mine, lanes]
            dq = jnp.zeros((block_rows, PAIR), F32)
            dk = jnp.zeros((last - first, PAIR), F32)
            dv = jnp.zeros((last - first, PAIR), F32)
            for h in range(2):
                do_h = jnp.where(own[h][mine], grad_out, zero)
                q_h = jnp.where(own[h][mine], queries, zero)
                k_h = jnp.where(own[h][first:last], keys, zero)
                probs = prob_buf[slot, h, first:last, mine]
                grad_probs = mm_cols(values, do_h)
                grad_scores = (
                    probs.astype(F32) * (grad_probs - delta_ref[p, h : h + 1, mine])
                ).astype(BF16)
                dq = dq + mm_rows(grad_scores, k_h)
                dk = dk + mm(grad_scores, q_h)
                dv = dv + mm(probs, do_h)
            dq_all[mine, lanes] = (dq * scale).astype(BF16)
            dk_sum[first:last, :] += dk
            dv_sum[first:last, :] += dv
        dk_all[:, lanes] = (dk_sum[...] * scale).astype(BF16)
        dv_all[:, lanes] = dv_sum[...].astype(BF16)
        first_part = jnp.minimum(early + p * PARTS_LOOP, parts)
        last_part = jnp.minimum(early + (p + 1) * PARTS_LOOP, parts)
        lax.fori_loop(first_part, last_part, made_start, 0)
        for w, ref in enumerate((dq_all, dk_all, dv_all)):
            made = mm(normed_t[...], ref[:, lanes]).astype(BF16)
            grads[p + 2, w * width : (w + 1) * width, :] = made
        for stage in reversed(range(7)):
            if stage <= 2:
                stage_run(stage, p + 2 - stage)
            else:

                @pl.when(p + 2 >= stage)
                def _(stage=stage):
                    stage_run(stage, p + 2 - stage)

        return carry

    lax.fori_loop(0, pairs, pair_step, 0)
    for load in loads[8:]:
        load.wait()
    small_in[...] = jnp.zeros_like(small_in)

    def row_block(i):
        at = slice(i * block_rows, (i + 1) * block_rows)
        unit, unit_scale = norm_parts(x_ref[at, :].astype(F32))
        grad = (
            mm_cols(dq_all[at, :], weights[0])
            + mm_cols(dk_all[at, :], weights[1])
            + mm_cols(dv_all[at, :], weights[2])
        )
        small_in[0:1, :] += jnp.sum(grad * unit, 0, keepdims=True)
        small_in[1:2, :] += jnp.sum(grad, 0, keepdims=True)
        grad_hidden[at, :] += norm_back(grad, gain1, unit, unit_scale)

    grad_copy = pltpu.make_async_copy(grad_hidden, grad_hbm, grad_sem.at[0])

    def hidden_copy(i):
        at = slice(i * block_rows, (i + 1) * block_rows)
        return pltpu.make_async_copy(hidden_hbm.at[at], hidden_part.at[i % 2], hidden_sem.at[i % 2])

    output_copy = pltpu.make_async_copy(do_ref, output_hbm, grad_sem.at[1])

    def output_block(i):
        at = slice(i * block_rows, (i + 1) * block_rows)
        if i == 0:
            lax.fori_loop(0, parts, made_received, 0)
        hidden_copy(i).wait()
        if i + 1 < tokens // block_rows:
            hidden_copy(i + 1).start()
        slot = col_of(lines_ref[1:2, at])
        pick = one_hot(iota((block_rows, slots), 1) == slot)
        produced = jnp.zeros((block_rows, width), F32)
        for e in range(experts):
            produced = produced + mm(
                pick[:, e * experts_cap : (e + 1) * experts_cap], made_home[e]
            )
        total = hidden_part[i % 2] + gate_ref[at, 0:1] * produced
        do_ref[at, :] = total.astype(BF16)

    hidden_copy(0).start()

    blocks = tokens // block_rows
    done = 0
    out_done = 0
    small_at = 0
    next_part = min(early + pairs * PARTS_LOOP, parts)
    for tick in range(pairs + 1, pairs + 8):
        if next_part < parts:
            some = min(parts, next_part + PARTS_DRAIN)
            lax.fori_loop(next_part, some, made_start, 0)
            next_part = some
        for _ in range(2):
            if done < blocks:
                row_block(done)
                done += 1
                if done == blocks:
                    grad_copy.start()
            elif out_done < blocks and tick > pairs + OUTPUT_TICK and next_part == parts:
                output_block(out_done)
                out_done += 1
                if out_done == blocks:
                    output_copy.start()
        for stage in reversed(range(7)):
            c = tick + 1 - stage
            if 0 <= c < n:
                stage_run(stage, c)
        if done == blocks and small_at < 4:
            small_run(small_at)
            small_at += 1
    while done < blocks:
        row_block(done)
        done += 1
        if done == blocks:
            grad_copy.start()
    lax.fori_loop(next_part, parts, made_start, 0)
    while out_done < blocks:
        output_block(out_done)
        out_done += 1
        if out_done == blocks:
            output_copy.start()
    while small_at < 4:
        small_run(small_at)
        small_at += 1
    for tile in range(width // 128):
        at = full + tile * lines2
        small_out2[:, tile * 128 : (tile + 1) * 128] = out_ref[0, at : at + lines2, :].astype(F32)
    grad_copy.wait()
    output_copy.wait()
    for c in range(n):
        sums_copy(c).wait()
    lax.fori_loop(0, parts, made_sent, 0)
    for stage in range(3):
        for copy in small_copies(stage):
            copy.wait_send()

    def sent(c, carry):
        for made in (core_copy, plane_copies, line_copies, line_back, plane_back, core_back):
            for copy in made(c):
                copy.wait_send()
        return carry

    lax.fori_loop(0, n, sent, 0)


def tail(
    x, vecs, tables, lines, gate_grads, gate, q, k, v, wq, wk, wv, wo, probs, back, hidden, cot,
    mixed, made, space, longest, dp_size, experts,
):
    tokens, width = x.shape
    pairs = width // PAIR
    n = 2 + pairs
    rows = chunk_rows(width, dp_size, experts)
    x_axis, members, planes = dp_size // 2, experts // 2, dp_size
    half = rows // 2
    quarter = half // planes
    piece = quarter // members
    most = max(planes, members)
    small_shape = (8, width)
    cap = made.shape[1]
    small2_shape = (8 + space + max(8, experts), width)
    block_rows = 256
    sems = pltpu.SemaphoreType.DMA
    local = pl.BlockSpec(memory_space=pltpu.VMEM)
    anywhere = pl.BlockSpec(memory_space=pl.ANY)
    low = pltpu.VMEM((tokens, width), BF16)
    return pl.pallas_call(
        functools.partial(tail_kernel, x_axis, experts, longest),
        in_specs=[local] * 6 + [anywhere] * 13,
        out_specs=[anywhere] * 3 + [local] * 2,
        out_shape=[
            jax.ShapeDtypeStruct((tokens, width), F32),
            jax.ShapeDtypeStruct((n, rows, 128), BF16),
            jax.ShapeDtypeStruct((tokens, width), BF16),
            jax.ShapeDtypeStruct(small_shape, F32),
            jax.ShapeDtypeStruct(small2_shape, F32),
        ],
        scratch_shapes=[
            low,
            low,
            low,
            low,
            pltpu.VMEM((4, width, width), BF16),
            pltpu.VMEM((n, rows, 128), BF16),
            pltpu.VMEM((experts, cap, width), BF16),
            pltpu.VMEM((2, block_rows, width), F32),
            pltpu.VMEM((pairs, 8, tokens), F32),
            pltpu.VMEM(small2_shape, F32),
            pltpu.VMEM((128, width), F32),
            pltpu.VMEM((128, 128), F32),
            pltpu.VMEM((16, experts * cap), BF16),
            pltpu.VMEM((width, 256), BF16),
            low,
            low,
            low,
            pltpu.VMEM((width, tokens), BF16),
            pltpu.VMEM((2, 2, tokens, tokens), BF16),
            pltpu.VMEM((tokens, PAIR), F32),
            pltpu.VMEM((tokens, PAIR), F32),
            pltpu.VMEM((n, rows, 128), BF16),
            pltpu.VMEM((tokens, width), F32),
            pltpu.VMEM(small_shape, F32),
            pltpu.VMEM((n, half, 128), BF16),
            pltpu.VMEM((n, half, 128), BF16),
            pltpu.VMEM((n, planes - 1, quarter, 128), BF16),
            pltpu.VMEM((n, quarter, 128), BF16),
            pltpu.VMEM((n, members - 1, piece, 128), BF16),
            pltpu.VMEM((3, most, *small_shape), F32),
            sems((12,)),
            sems((2,)),
            sems((n,)),
            sems((2,)),
            sems((2,)),
            sems((PARTS * (experts - 1),)),
            sems((PARTS * (experts - 1),)),
        ]
        + [sems((n,))] * 2
        + [sems((n, planes))] * 2
        + [sems((n, members))] * 4
        + [sems((n, planes))] * 2
        + [sems((n,))] * 2
        + [sems((3, most))] * 2,
        compiler_params=pltpu.CompilerParams(
            vmem_limit_bytes=63 * MIB, collective_id=1, has_side_effects=True
        ),
        cost_estimate=cost(16 * pairs * tokens * tokens * 256, 4 * pairs * tokens * tokens),
        name="tail",
    )(
        x, vecs, tables, lines, gate_grads, gate, q, k, v, wq, wk, wv, wo, probs,
        back.reshape(2, tokens, width), hidden, cot, mixed, made,
    )


def finish_kernel(x_axis, *refs):
    sums_refs = refs[:3]
    din_refs = refs[3 : 3 + x_axis]
    dout_refs = refs[3 + x_axis : 3 + 2 * x_axis]
    dwo_ref, dwq_ref, dwk_ref, dwv_ref, din_ref, dout_ref = refs[3 + 2 * x_axis :]
    width = dwo_ref.shape[1]
    half = width // 256
    for tile in range(width // 128):
        lanes = slice(tile * 128, (tile + 1) * 128)
        dwo_ref[:, lanes] = sums_refs[tile % half][tile // half].astype(F32)
        for w, ref in enumerate((dwq_ref, dwk_ref, dwv_ref)):
            ref[:, lanes] = sums_refs[w][2 + tile].astype(F32)
    for out, parts in ((din_ref, din_refs), (dout_ref, dout_refs)):
        total = parts[0][...].astype(F32)
        for part in parts[1:]:
            total = total + part[...].astype(F32)
        out[...] = total


def finish(width, sums, din, dout):
    n = sums.shape[0]
    steps = 4

    def row_spec(array):
        return pl.BlockSpec((array.shape[0] // steps, array.shape[1]), lambda i: (i, 0))

    square = jax.ShapeDtypeStruct((width, width), F32)
    out_shape = [square] * 4 + [
        jax.ShapeDtypeStruct(din[0].shape, F32),
        jax.ShapeDtypeStruct(dout[0].shape, F32),
    ]
    return pl.pallas_call(
        functools.partial(finish_kernel, len(din)),
        grid=(steps,),
        in_specs=[
            pl.BlockSpec((n, width // steps, 128), lambda i, w=w: (0, w * steps + i, 0))
            for w in range(3)
        ]
        + [row_spec(part) for part in (*din, *dout)],
        out_specs=[row_spec(out) for out in out_shape],
        out_shape=out_shape,
        compiler_params=params(),
        cost_estimate=cost(0, 24 * width * width),
        name="finish",
    )(sums, sums, sums, *din, *dout)


def output_kernel(experts, cap, made_ref, hidden_ref, gate_ref, lines_ref, out_ref):
    rows, width = hidden_ref.shape
    pick = one_hot(iota((rows, experts * cap), 1) == col_of(lines_ref[1:2, :]))
    produced = mm(pick, made_ref[...])
    out_ref[...] = (hidden_ref[...] + gate_ref[:, 0:1] * produced).astype(BF16)


def layer_output(made, hidden, gate, lines, experts, cap):
    tokens, width = hidden.shape
    rows = 256
    made = made.reshape(-1, width)
    block = pl.BlockSpec((rows, width), lambda i: (i, 0))
    return pl.pallas_call(
        functools.partial(output_kernel, experts, cap),
        grid=(tokens // rows,),
        in_specs=[
            spec_all(made.shape),
            block,
            pl.BlockSpec((rows, 128), lambda i: (i, 0)),
            pl.BlockSpec((8, rows), lambda i: (0, i)),
        ],
        out_specs=block,
        out_shape=jax.ShapeDtypeStruct((tokens, width), BF16),
        compiler_params=params(),
        cost_estimate=cost(2 * tokens * width * experts * cap, 10 * tokens * width),
        name="layer_output",
    )(made, hidden, gate, lines)


def exchange(blocks, axis):
    return lax.all_to_all(blocks, axis, split_axis=0, concat_axis=0, tiled=True)


def on_device(
    tokens,
    segment_ids,
    routes,
    norm1_gain,
    norm1_bias,
    query_weight,
    w_key,
    w_value,
    w_output,
    norm2_gain,
    norm2_bias,
    router_proj,
    expert_embed,
    expert_in,
    expert_out,
    cotangent,
):
    count, width = tokens.shape
    experts = lax.axis_size("expert")
    dp_size = lax.axis_size("dp")
    cap = 2 * count // experts
    longest = segment_ids.shape[1] // 2
    space = router_proj.shape[1]
    vecs = jnp.stack([norm1_gain, norm1_bias, norm2_gain, norm2_bias])
    tables = jnp.concatenate(
        [
            jnp.pad(router_proj, ((0, 0), (0, 128 - space))),
            jnp.pad(expert_embed, ((0, 128 - experts), (0, 128 - space))),
        ]
    )
    q, k, v, mixed, probs, hidden, gate, slots, gates, lines, up = forward(
        routes.reshape(1, count), segment_ids.reshape(1, count), cotangent, tokens, vecs, tables,
        query_weight, w_key, w_value, w_output, longest, experts, cap,
    )
    back, gate_grads, made, din, dout = expert(
        slots, gates, up, expert_in[0], expert_out[0], dp_size
    )
    if can_reduce(width, space, dp_size, experts):
        grad_input, sums, output, small1, small2 = tail(
            tokens, vecs, tables, lines, gate_grads, gate, q, k, v, query_weight, w_key, w_value,
            w_output, probs, back, hidden, cotangent, mixed, made, space, longest, dp_size,
            experts,
        )
    else:
        made = exchange(made, "expert")
        grad_hidden, grad_mixed, delta, dwo, small2 = middle_back(
            back, gate_grads, lines, hidden, cotangent, mixed, w_output, vecs[2:3], vecs[3:4],
            tables[:width], tables[width:], space, experts, cap,
        )
        dq, dk, dv = attention_back(q, k, v, grad_mixed, probs, delta, longest)
        grad_input, dwq, dwk, dwv, small1 = qkv_back(
            tokens, vecs[0:1], vecs[1:2], grad_hidden, dq, dk, dv, query_weight, w_key, w_value
        )
        half = width // 256
        chunks = [dwo[:half], dwo[half:]]
        for at in range(width // 128):
            chunks.append(jnp.stack([dwq[at], dwk[at], dwv[at]]))
        sums, small1, small2 = lax.psum(
            (jnp.stack(chunks).astype(F32), small1, small2), ("dp", "expert")
        )
        sums = sums.astype(BF16).reshape(len(chunks), -1, 128)
        output = layer_output(made, hidden, gate, lines, experts, cap)
    dwo, dwq, dwk, dwv, grad_in, grad_out = finish(width, sums, din, dout)
    return (
        output,
        grad_input,
        small1[0],
        small1[1],
        dwq,
        dwk,
        dwv,
        dwo,
        small2[0],
        small2[1],
        small2[8 : 8 + space].T,
        small2[8 + space : 8 + space + experts, :space],
        grad_in[None],
        grad_out[None],
    )


def solution(mesh):
    split = P(("dp", "expert"), None)
    in_specs = (
        (split,) * 3 + (P(),) * 10 + (P("expert", None, None), P("expert", None, None), split)
    )
    out_specs = (
        (split, split) + (P(),) * 10 + (P("expert", None, "dp"), P("expert", "dp", None))
    )
    return jax.shard_map(
        on_device, mesh=mesh, in_specs=in_specs, out_specs=out_specs, check_vma=False
    )
```

time: 442 us -> 402 us (0.910)
  the two profiles are of different devices: /device:TPU:15 before, /device:TPU:0 now
where the time goes in v4:
time: 402 us; the launch traced here: 396 us
  Pallas kernels  381 us (95%)
  local copies, waits for them, and re-layouts  12 us (3%)
    pallas_call x1, Pallas kernels, expert(): pl.pallas_call(functools.partial(expert_kernel, experts, x_axis), in_spec...  163 us
    pallas_call x1, Pallas kernels, tail(): pl.pallas_call(functools.partial(tail_kernel, x_axis, experts, longest),...  148 us
    pallas_call x1, Pallas kernels, forward(): pl.pallas_call(functools.partial(forward_kernel, experts, cap, longest),...  60.6 us
    pallas_call x1, Pallas kernels, finish(): pl.pallas_call(functools.partial(finish_kernel, len(din)), grid=(steps,),...  9.22 us

profile of v4, /device:TPU:0, one launch (start us, length us, event | category | flops | bytes accessed | tf_op | source)
XLA Modules:
  0.0 395.7 jit_solution(11050145531278896006)
XLA Ops:
  0.6 0.7 stack.15
  1.3 0.7 stack.16
  2.0 0.7 stack.17
  2.7 0.7 stack.18
  3.4 0.6 pad_maximum_fusion.vecs_ref
  4.0 1.0 copy.30
  5.0 1.5 select_maximum_fusion.tables_ref
  6.5 60.6 %forward.1 = (bf16[1024,768]{1,0:T(8,128)(2,1)}, bf16[1024,768]{1,0:T(8,128)(2,1)}, bf16[1024,768]{1,0:T(8,128)(2,1)}, bf16[1024,768]{1,0:T(8,128)(2,1)}, bf16[1...) custom-call(s32[1,1024]{1,0:T(1,128)} %bitcast.12, ...), custom_call_target="tpu_custom_call" | custom-call | flops 12884901888 | bytes 25165824 | tf_op jit(solution)/shard_map/forward/pallas_call | solution.py:397
  67.1 162.6 %expert.1 = (bf16[8,256,768]{2,1,0:T(8,128)(2,1)}, f32[8,8,256]{2,1,0:T(8,128)}, bf16[8,256,768]{2,1,0:T(8,128)(2,1)}, bf16[768,768]{1,0:T(8,128)(2,1)}, bf16[76...) custom-call(bf16[8,256,768]{2,1,0:T(8,128)(2,1)} %get-tuple-element.44.refs_0_, ...), custom_call_target="tpu_custom_call" | custom-call | flops 57982058496 | bytes 18874368 | tf_op jit(solution)/shard_map/expert/pallas_call | solution.py:712
  229.7 148.1 %tail.1 = (f32[1024,768]{1,0:T(8,128)}, bf16[8,2560,128]{2,1,0:T(8,128)(2,1)}, bf16[1024,768]{1,0:T(8,128)(2,1)}, f32[8,768]{1,0:T(8,128)}, f32[32,768]{1,0:T(8,128)}) custom-call(bf16[1024,768]{1,0:T(8,128)(2,1)} %x_ref.3, f32[4,768]{1,0:T(4,128)} %pad_maximum_fusion.vecs_ref, f32[896,128]{1,0:T(8,128)} %select_maximum_fusion.tables_ref, ...), custom_call_target="tpu_custom_call" | custom-call | flops 25769803776 | bytes 25165824 | tf_op jit(solution)/shard_map/tail/pallas_call | solution.py:1520
  377.8 1.3 slice.23
  379.1 1.5 slice_reduce_fusion
  380.5 1.4 slice_bitcast_fusion
  381.9 0.0 copy-start.1
  382.0 9.2 %finish.1 = (f32[768,768]{1,0:T(8,128)}, f32[768,768]{1,0:T(8,128)}, f32[768,768]{1,0:T(8,128)}, f32[768,768]{1,0:T(8,128)}, f32[768,768]{1,0:T(8,128)}, /*index=5*/f32[768,768]{1,0:T(8,128)}) custom-call(bf16[8,2560,128]{2,1,0:T(8,128)(2,1)} %get-tuple-element.60.refs_0_.refs_1_.refs_2_, bf16[8,2560,128]{2,1,0:T(8,128)(2,1)} %get-tuple-element.60.refs_0_.refs_1_.refs_2_, ...), custom_call_target="tpu_custom_call" | custom-call | bytes 14155776 | tf_op jit(solution)/shard_map/finish/pallas_call | solution.py:1618
  391.2 0.0 copy-start
  391.2 0.0 copy-done.1
  391.2 1.1 copy.33
  392.3 1.3 copy-done
  393.6 1.7 copy.34
Async XLA Ops:
  381.9 9.2 %copy-start.1 = (bf16[1024,768]{1,0:T(8,128)(2,1)S(1)}, bf16[1024,768]{1,0:T(8,128)(2,1)}, u32[]{:S(2)}) copy-start(bf16[1024,768]{1,0:T(8,128)(2,1)} %get-tuple-element.92) | copy-start | bytes 4718596
  391.2 2.5 copy-start

commit v5 on v4

--- a/solution.py
+++ b/solution.py
@@ -18,9 +18,9 @@
 WINDOW = 4
 PARTS = 4
 OUTPUT_TICK = 4
-PARTS_EARLY = 16
-PARTS_LOOP = 2
-PARTS_DRAIN = 2
+PARTS_EARLY = 18
+PARTS_LOOP = 1
+PARTS_DRAIN = 1
 
 
 def mm(left, right):
@@ -1217,8 +1217,13 @@
     parts = PARTS * (experts - 1)
     early = min(PARTS_EARLY, parts)
 
+    def half_peer(i):
+        half = experts // 2
+        far = (i + 1) // half
+        return lax.rem(me + i + 1, half) + half * lax.rem(me // half + far, 2)
+
     def made_copy(m):
-        to = expert_peer(distance(experts, m // PARTS + 1))
+        to = half_peer(m // PARTS)
         at = rows_at(m % PARTS * (experts_cap // PARTS), experts_cap // PARTS)
         return remote(
             made_hbm.at[to, at],
@@ -1688,7 +1693,7 @@
     cap = 2 * count // experts
     longest = segment_ids.shape[1] // 2
     space = router_proj.shape[1]
-    vecs = jnp.stack([norm1_gain, norm1_bias, norm2_gain, norm2_bias])
+    vecs = jnp.concatenate([norm1_gain, norm1_bias, norm2_gain, norm2_bias]).reshape(4, width)
     tables = jnp.concatenate(
         [
             jnp.pad(router_proj, ((0, 0), (0, 128 - space))),

time: 402 us -> 390 us (0.970)
  Pallas kernels: 381 us -> 371 us
    pallas_call x1, Pallas kernels: 148 us -> 139 us  [tail(): pl.pallas_call(functools.partial(tail_kernel, x_axis, experts, longest),...]
where the time goes in v5:
time: 390 us; the launch traced here: 384 us
  Pallas kernels  371 us (95%)
  local copies, waits for them, and re-layouts  9.82 us (3%)
    pallas_call x1, Pallas kernels, expert(): pl.pallas_call(functools.partial(expert_kernel, experts, x_axis), in_spec...  163 us
    pallas_call x1, Pallas kernels, tail(): pl.pallas_call(functools.partial(tail_kernel, x_axis, experts, longest),...  139 us
    pallas_call x1, Pallas kernels, forward(): pl.pallas_call(functools.partial(forward_kernel, experts, cap, longest),...  60.6 us
    pallas_call x1, Pallas kernels, finish(): pl.pallas_call(functools.partial(finish_kernel, len(din)), grid=(steps,),...  9.22 us

profile of v5, /device:TPU:0, one launch (start us, length us, event | category | flops | bytes accessed | tf_op | source)
XLA Modules:
  0.0 384.2 jit_solution(9852106723477851528)
XLA Ops:
  0.6 0.7 pad_maximum_fusion
  1.4 0.6 reshape.37.vecs_ref
  2.0 1.0 copy.30
  3.0 1.5 select_maximum_fusion.tables_ref
  4.5 60.6 %forward.1 = (bf16[1024,768]{1,0:T(8,128)(2,1)}, bf16[1024,768]{1,0:T(8,128)(2,1)}, bf16[1024,768]{1,0:T(8,128)(2,1)}, bf16[1024,768]{1,0:T(8,128)(2,1)}, bf16[1...) custom-call(s32[1,1024]{1,0:T(1,128)} %bitcast.12, ...), custom_call_target="tpu_custom_call" | custom-call | flops 12884901888 | bytes 25165824 | tf_op jit(solution)/shard_map/forward/pallas_call | solution.py:397
  65.1 162.6 %expert.1 = (bf16[8,256,768]{2,1,0:T(8,128)(2,1)}, f32[8,8,256]{2,1,0:T(8,128)}, bf16[8,256,768]{2,1,0:T(8,128)(2,1)}, bf16[768,768]{1,0:T(8,128)(2,1)}, bf16[76...) custom-call(bf16[8,256,768]{2,1,0:T(8,128)(2,1)} %get-tuple-element.44.refs_0_, ...), custom_call_target="tpu_custom_call" | custom-call | flops 57982058496 | bytes 18874368 | tf_op jit(solution)/shard_map/expert/pallas_call | solution.py:712
  227.7 138.6 %tail.1 = (f32[1024,768]{1,0:T(8,128)}, bf16[8,2560,128]{2,1,0:T(8,128)(2,1)}, bf16[1024,768]{1,0:T(8,128)(2,1)}, f32[8,768]{1,0:T(8,128)}, f32[32,768]{1,0:T(8,128)}) custom-call(bf16[1024,768]{1,0:T(8,128)(2,1)} %x_ref.3, f32[4,768]{1,0:T(4,128)} %reshape.37.vecs_ref, f32[896,128]{1,0:T(8,128)} %select_maximum_fusion.tables_ref, ...), custom_call_target="tpu_custom_call" | custom-call | flops 25769803776 | bytes 25165824 | tf_op jit(solution)/shard_map/tail/pallas_call | solution.py:1525
  366.2 1.3 slice.23
  367.5 1.5 slice_reduce_fusion
  368.9 1.4 slice_bitcast_fusion
  370.4 0.0 copy-start.1
  370.4 9.2 %finish.1 = (f32[768,768]{1,0:T(8,128)}, f32[768,768]{1,0:T(8,128)}, f32[768,768]{1,0:T(8,128)}, f32[768,768]{1,0:T(8,128)}, f32[768,768]{1,0:T(8,128)}, /*index=5*/f32[768,768]{1,0:T(8,128)}) custom-call(bf16[8,2560,128]{2,1,0:T(8,128)(2,1)} %get-tuple-element.60.refs_0_.refs_1_.refs_2_, bf16[8,2560,128]{2,1,0:T(8,128)(2,1)} %get-tuple-element.60.refs_0_.refs_1_.refs_2_, ...), custom_call_target="tpu_custom_call" | custom-call | bytes 14155776 | tf_op jit(solution)/shard_map/finish/pallas_call | solution.py:1623
  379.6 0.0 copy-start
  379.6 0.0 copy-done.1
  379.6 1.1 copy.33
  380.8 1.3 copy-done
  382.0 1.7 copy.34
Async XLA Ops:
  370.4 9.2 %copy-start.1 = (bf16[1024,768]{1,0:T(8,128)(2,1)S(1)}, bf16[1024,768]{1,0:T(8,128)(2,1)}, u32[]{:S(2)}) copy-start(bf16[1024,768]{1,0:T(8,128)(2,1)} %get-tuple-element.92) | copy-start | bytes 4718596
  379.6 2.5 copy-start
